TPU v7x, 32 devices: a whole 2x2x4 slice. The times are simulated.
32 devices in a mesh: wave: 4 (over x, core), deg: 8 (over z, y).
Axes of the slice: x: 2, y: 2, z: 4, core: 2. Of those that a mesh axis runs over, the one named last changes fastest.
Arguments:
- spectrum: bfloat16 [256, 2, 32, 2048], P('wave', None, None, 'deg'), may hold values from -2 to 2
- leaf_map: bfloat16 [256, 2048, 128], P('wave', 'deg'), may hold values from -0.375 to 0.375
- level_maps: bfloat16 [3, 256, 1024, 128], P(None, 'wave', 'deg'), may hold values from -0.5 to 0.5
- lat_map: bfloat16 [256, 128, 1024], P('wave', None, 'deg'), may hold values from -0.03125 to 0.03125
- skeleton: int32 [256, 1024], P('wave', 'deg'), may hold values from 0 to 255
- wavemap: int32 [256], replicated, may hold values from 0 to 4095, as said below
Outputs:
- grid: bfloat16 [32, 1024, 8192], P('wave', 'deg')
Inputs may be any that keep to these rules, and one draw needn't show every extreme that they name: `skeleton`: for slot m and block b, entries b * 128 to b * 128 + 127 are degrees counted from the first degree of block b. `wavemap`: no two slots hold the same wavenumber.
All inputs are finite; a program needn't handle non-finite values.
Results may differ from a plain program's by a relative error of at most 0.0086.
Values may be sent and summed in bfloat16 or wider, within the bound.
No kernel may reach another device: no remote copies, remote signals or barrier semaphores. Data moves between devices by JAX's collectives and lax.ppermute only.
A program may use at most 192 MiB of HBM per device.

v0:
```python
import jax
import jax.numpy as jnp
from jax import lax
from jax.sharding import PartitionSpec as P

NLON = 8192
LONG_SPLIT = 32


def partner(shard, axis, bit):
    return lax.ppermute(shard, axis, [(i, i ^ 1 << bit) for i in range(lax.axis_size(axis))])


def long_tables(lon_count, first):
    half = lon_count // 2
    second = half // first
    a_idx = lax.broadcasted_iota(jnp.int32, (first, 2 * first), 0)
    u_idx = lax.broadcasted_iota(jnp.int32, (first, 2 * first), 1)
    ang1 = (a_idx * u_idx % (2 * first)).astype(jnp.float32) * (2.0 * jnp.pi / (2 * first))
    cos1 = jnp.cos(ang1)
    sin1 = jnp.sin(ang1)
    table1 = jnp.stack([jnp.stack([cos1, sin1], 1), jnp.stack([-sin1, cos1], 1)], 0).astype(
        jnp.bfloat16
    )
    e_idx = lax.broadcasted_iota(jnp.int32, (second, 2 * first), 0)
    w_idx = lax.broadcasted_iota(jnp.int32, (second, 2 * first), 1)
    ang_tw = (e_idx * w_idx % lon_count).astype(jnp.float32) * (2.0 * jnp.pi / lon_count)
    tw_cos = jnp.cos(ang_tw)
    tw_sin = jnp.sin(ang_tw)
    e2_idx = lax.broadcasted_iota(jnp.int32, (second, second), 0)
    v_idx = lax.broadcasted_iota(jnp.int32, (second, second), 1)
    ang2 = (e2_idx * v_idx % second).astype(jnp.float32) * (2.0 * jnp.pi / second)
    table2 = jnp.stack([jnp.cos(ang2), -jnp.sin(ang2)]).astype(jnp.bfloat16)
    return (table1, tw_cos, tw_sin, table2)


def body(spectrum, leaf_map, level_maps, lat_map, skeleton, wavemap):
    slot_count = spectrum.shape[0]
    field_count = spectrum.shape[2]
    columns = 2 * field_count
    node_width = leaf_map.shape[2]
    half_width = node_width // 2
    flat_coef = spectrum.reshape(slot_count, columns, -1)
    degree_count = flat_coef.shape[2]
    degree_iota = lax.broadcasted_iota(jnp.int32, (slot_count, degree_count, node_width), 1)
    selector = (degree_iota == skeleton[:, None, :]).astype(jnp.bfloat16)
    picked = jnp.einsum("mcn,mnk->mck", flat_coef, selector, preferred_element_type=jnp.float32)
    node_state = (
        picked + jnp.einsum("mcn,mnk->mck", flat_coef, leaf_map, preferred_element_type=jnp.float32)
    ).astype(jnp.bfloat16)
    deg_index = lax.axis_index("deg")
    for level_num in range(level_maps.shape[0]):
        upper_bit = deg_index >> level_num & 1
        own_half = lax.dynamic_slice_in_dim(node_state, upper_bit * half_width, half_width, 2)
        payload = lax.dynamic_slice_in_dim(node_state, (1 - upper_bit) * half_width, half_width, 2)
        packed = payload.reshape(slot_count, columns // 2, 2 * half_width)
        factor = level_maps[level_num]
        own_rows = lax.dynamic_slice_in_dim(factor, upper_bit * half_width, half_width, 1)
        other_rows = lax.dynamic_slice_in_dim(factor, (1 - upper_bit) * half_width, half_width, 1)
        own_term = jnp.einsum(
            "mck,mks->mcs", own_half, own_rows, preferred_element_type=jnp.float32
        )
        arrived = partner(packed, "deg", level_num).reshape(payload.shape)
        other_term = jnp.einsum(
            "mck,mks->mcs", arrived, other_rows, preferred_element_type=jnp.float32
        )
        node_state = (own_term + other_term).astype(jnp.bfloat16)
    lat_values = jnp.einsum(
        "mck,mkl->mcl", node_state, lat_map, preferred_element_type=jnp.float32
    ).astype(jnp.bfloat16)
    lat_values = lat_values.reshape(slot_count, 2, field_count, -1)
    table1, tw_cos, tw_sin, table2 = long_tables(NLON, LONG_SPLIT)
    half = NLON // 2
    second = half // LONG_SPLIT
    weight = jnp.where(wavemap == 0, 1.0, 2.0).astype(jnp.float32)[:, None, None, None]
    slot_total = wavemap.shape[0]
    placement = (lax.broadcasted_iota(jnp.int32, (half, slot_total), 0) == wavemap[None, :]).astype(
        jnp.bfloat16
    )
    gathered = lax.all_to_all(lat_values, "wave", split_axis=2, concat_axis=0, tiled=True)
    local_fields = gathered.shape[2]
    row_count = gathered.shape[3]
    scaled = (weight * gathered.astype(jnp.float32)).astype(jnp.bfloat16)
    coeffs = jnp.einsum(
        "qm,mrfl->qrfl", placement, scaled, preferred_element_type=jnp.float32
    ).astype(jnp.bfloat16)
    coeffs = coeffs.reshape(LONG_SPLIT, second, 2, local_fields, row_count)
    section = jnp.einsum("aerfl,rapu->epufl", coeffs, table1, preferred_element_type=jnp.float32)
    real_part = section[:, 0]
    imag_part = section[:, 1]
    tc = tw_cos[:, :, None, None]
    ts = tw_sin[:, :, None, None]
    twisted = jnp.stack(
        [real_part * tc - imag_part * ts, real_part * ts + imag_part * tc], 1
    ).astype(jnp.bfloat16)
    result = jnp.einsum("epufl,pev->flvu", twisted, table2, preferred_element_type=jnp.float32)
    return result.reshape(local_fields, row_count, NLON).astype(jnp.bfloat16)


def solution(mesh):
    placed = (
        P("wave", None, None, "deg"),
        P("wave", "deg", None),
        P(None, "wave", "deg", None),
        P("wave", None, "deg"),
        P("wave", "deg"),
        P(),
    )
    return jax.shard_map(
        body, mesh=mesh, in_specs=placed, out_specs=P("wave", "deg", None), check_vma=False
    )
```

profile of v0, /device:TPU:0, one launch (start us, length us, event | category | flops | bytes accessed | tf_op | source)
XLA Modules:
  0.0 300.4 jit_solution(15246725738674639099)
XLA Ops:
  0.0 0.0 copy-start
  0.0 1.6 copy-done
  1.6 3.1 %fusion.70 = f32[64,64,128]{2,1,0:T(8,128)S(1)} fusion(bf16[64,64,256]{2,1,0:T(8,128)(2,1)S(1)} %bitcast.80, bf16[64,256,128]{2,1,0:T(8,128)(2,1)} %param.7), kind=kOutput, calls=%fused_computation.100 | convolution fusion | flops 268435456 | bytes 8388608 | tf_op jit(solution)/shard_map/mcn,mnk->mck/dot_general | solution.py:49
  4.7 0.0 copy-done.4
  4.7 1.9 fusion.12
  6.6 0.4 constant_dynamic-slice_fusion.1
  6.9 1.3 reshape.193
  8.2 3.0 collective-permute-start
  11.2 7.5 %fusion.69 = (bf16[1,64,128,128]{3,2,1,0:T(8,128)(2,1)S(1)}, bf16[1,64,128,128]{3,2,1,0:T(8,128)(2,1)}, bf16[1,64,128,128]{3,2,1,0:T(8,128)(2,1)}) fusion(bf16[3,64,128,128]{3,2,1,0:T(8,128)(2,1)} %param.8), kind=kLoop, calls=%fused_computation.99 | loop fusion | bytes 12582912 | tf_op jit(solution)/shard_map/slice | solution.py:57
  18.7 2.0 fusion.22
  20.7 0.0 copy-done.2
  20.7 2.7 collective-permute-done
  23.4 1.6 reshape.194
  25.1 2.4 add_convert_fusion.3
  27.4 0.4 constant_dynamic-slice_fusion
  27.8 0.5 reshape.195
  28.3 1.9 collective-permute-start.1
  30.2 3.0 %fusion.19 = f32[64,64,128]{2,1,0:T(8,128)} fusion(bf16[1,64,128,128]{3,2,1,0:T(8,128)(2,1)} %get-tuple-element.9, s32[]{:T(128)S(6)} %select_n.99, bf16[64,64,128]{2,1,0:T(8,128)(2,1)S(1)} %add_convert_fusion.3), kind=kOutput, calls=%fused_computation.30 | convolution fusion | flops 67108864 | bytes 4195328 | tf_op jit(solution)/shard_map/mck,mks->mcs/dot_general | solution.py:60
  33.2 8.3 %collective-permute-done.1 = bf16[64,32,128]{2,1,0:T(8,128)(2,1)S(1)} collective-permute-done((bf16[64,32,128]{2,1,0:T(8,128)(2,1)S(1)}, bf16[64,32,128]{2,1,0:T(8,128)(2,1)S(1)}, u32[]{:S(2)}, u32[]{:S(2)}) %collective-permute-start.1) | collective-permute-done | bytes 524320 | tf_op jit(solution)/shard_map/ppermute | solution.py:11
  41.5 0.4 reshape.196
  41.9 2.4 add_convert_fusion.2
  44.3 0.4 constant_dynamic-slice_fusion.2
  44.7 0.5 reshape.197
  45.1 2.6 collective-permute-start.2
  47.7 3.1 %fusion.16 = f32[64,64,128]{2,1,0:T(8,128)} fusion(bf16[1,64,128,128]{3,2,1,0:T(8,128)(2,1)} %get-tuple-element.8, s32[]{:T(128)S(6)} %select_n.101, bf16[64,64,128]{2,1,0:T(8,128)(2,1)S(1)} %add_convert_fusion.2), kind=kOutput, calls=%fused_computation.27 | convolution fusion | flops 67108864 | bytes 4195328 | tf_op jit(solution)/shard_map/mck,mks->mcs/dot_general | solution.py:60
  50.8 18.8 %collective-permute-done.2 = bf16[64,32,128]{2,1,0:T(8,128)(2,1)S(1)} collective-permute-done((bf16[64,32,128]{2,1,0:T(8,128)(2,1)S(1)}, bf16[64,32,128]{2,1,0:T(8,128)(2,1)S(1)}, u32[]{:S(2)}, u32[]{:S(2)}) %collective-permute-start.2) | collective-permute-done | bytes 524320 | tf_op jit(solution)/shard_map/ppermute | solution.py:11
  69.5 0.4 reshape.198
  70.0 3.5 %convolution_convert_fusion.1 = bf16[64,64,128]{2,1,0:T(8,128)(2,1)S(1)} fusion(bf16[64,128,128]{2,1,0:T(8,128)(2,1)} %param.9, f32[64,64,128]{2,1,0:T(8,128)} %fusion.16, bf16[64,64,64]{2,1,0:T(8,128)(2,1)S(1)} %reshape.198, bf16[1,64,128,128]{3,2,1,0:T(8,128)(2,1)} %get-tuple-element.8, s32[]{:T(128)S(6)} %select_n.102), kind=kOutput, calls=%fused_computation.25 | convolution fusion | flops 202899456 | bytes 6815748 | tf_op jit(solution)/shard_map/mck,mkl->mcl/dot_general | solution.py:68
  73.5 0.0 copy-start.3
  73.5 2.1 copy.18
  75.6 3.8 %all-to-all-start = ((bf16[64,2,32,128]{3,1,0,2:T(2,128)(2,1)}), bf16[64,2,32,128]{3,1,0,2:T(2,128)(2,1)S(1)}, u32[]{:S(2)}, u32[]{:S(2)}) async-start(bf16[64,2,32,128]{3,1,0,2:T(2,128)(2,1)} %copy.18), calls=%async_computation | async-start | bytes 2097152 | tf_op jit(solution)/shard_map/all_to_all | solution.py:80
  79.4 0.1 fusion.59
  79.4 0.1 negate_convert_fusion.1
  79.6 0.3 negate_convert_fusion
  79.8 0.3 fusion.50
  80.1 0.0 copy-done.3
  80.1 13.6 %all-to-all-done = bf16[64,2,32,128]{3,1,0,2:T(2,128)(2,1)S(1)} async-done(((bf16[64,2,32,128]{3,1,0,2:T(2,128)(2,1)}), bf16[64,2,32,128]{3,1,0,2:T(2,128)(2,1)S(1)}, u32[]{:S(2)}, u32[]{:S(2)}) %all-to-all-start) | async-done | bytes 1048608 | tf_op jit(solution)/shard_map/all_to_all | solution.py:80
  93.8 0.9 convert_bitcast_fusion
  94.7 0.3 copy.19
  94.9 0.3 fusion.11
  95.3 8.5 %convolution_convert_fusion = bf16[4096,2,8,128]{3,0,2,1:T(8,128)(2,1)} fusion(bf16[256,2,8,128]{3,0,2,1:T(8,128)(2,1)S(1)} %fusion.11, s32[256]{0:T(256)S(1)} %copy-done.3), kind=kOutput, calls=%fused_computation.10 | convolution fusion | flops 4304404480 | bytes 17826816 | tf_op jit(solution)/shard_map/qm,mrfl->qrfl/dot_general | solution.py:84
  103.8 32.7 %convolution_bitcast_fusion = f32[128,2,64,8,128]{4,2,3,0,1:T(8,128)} fusion(bf16[32,128,2,8,128]{4,1,0,3,2:T(8,128)(2,1)} %bitcast.81, bf16[1,32,2,64]{3,1,0,2:T(8,128)(2,1)S(1)} %get-tuple-element.11, bf16[1,32,2,64]{3,1,0,2:T(8,128)(2,1)S(1)} %get-tuple-element.10), kind=kOutput, calls=%fused_computation.6 | convolution fusion | flops 2147516416 | bytes 83902464 | tf_op jit(solution)/shard_map/aerfl,rapu->epufl/dot_general | solution.py:88
  136.5 33.9 %subtract_convert_fusion = (bf16[128,1,64,8,128]{4,2,3,0,1:T(8,128)(2,1)}, bf16[128,1,64,8,128]{4,2,3,0,1:T(8,128)(2,1)}) fusion(f32[128,2,64,8,128]{4,2,3,0,1:T(8,128)} %convolution_bitcast_fusion, f32[128,64]{1,0:T(8,128)S(1)} %get-tuple-element.14, f32[128,64]{1,0:T(8,128)S(1)} %get-tuple-element.15), kind=kLoop, calls=%fused_computation.5 | loop fusion | flops 67108864 | bytes 100728832 | tf_op jit(solution)/shard_map/convert.3
  170.4 22.9 %pad_maximum_fusion = bf16[128,2,64,8,128]{4,2,3,0,1:T(8,128)(2,1)} fusion(bf16[128,1,64,8,128]{4,2,3,0,1:T(8,128)(2,1)} %get-tuple-element.6, bf16[128,1,64,8,128]{4,2,3,0,1:T(8,128)(2,1)} %get-tuple-element.5), kind=kLoop, calls=%fused_computation | loop fusion | flops 16777216 | bytes 67108864 | tf_op jit(solution)/shard_map/stack | solution.py:93
  193.3 67.0 %fusion.2 = bf16[8,128,128,64]{1,2,0,3:T(8,128)(2,1)} fusion(bf16[128,2,64,8,128]{4,2,3,0,1:T(8,128)(2,1)} %pad_maximum_fusion, bf16[1,128,128]{1,2,0:T(8,128)(2,1)S(1)} %get-tuple-element.16, bf16[1,128,128]{1,2,0:T(8,128)(2,1)S(1)} %get-tuple-element.17), kind=kOutput, calls=%fused_computation.7 | convolution fusion | flops 4303486976 | bytes 50397184 | tf_op jit(solution)/shard_map/epufl,pev->flvu/dot_general | solution.py:96
  260.3 18.6 %copy.22 = bf16[8,128,128,64]{1,3,2,0:T(8,128)(2,1)} copy(bf16[8,128,128,64]{1,2,0,3:T(8,128)(2,1)} %fusion.2) | data formatting | bytes 33554432 | tf_op jit(solution)/shard_map/convert_element_type | solution.py:97
  278.9 21.3 %copy.23 = bf16[8,128,8192]{2,1,0:T(8,128)(2,1)} copy(bf16[8,128,8192]{1,2,0:T(8,128)(2,1)} %bitcast.82) | data formatting | bytes 33554432 | tf_op jit(solution)/shard_map/convert_element_type | solution.py:97
  300.2 0.0 copy-done.1
  (5 shorter events, 0.0 us)
Async XLA Ops:
  0.0 1.6 copy-start
  1.6 3.1 %copy-start.4 = (s32[64,128]{1,0:T(8,128)S(1)}, s32[64,128]{1,0:T(8,128)}, u32[]{:S(2)}) copy-start(s32[64,128]{1,0:T(8,128)} %param.10) | copy-start | bytes 98308
  8.2 15.2 %collective-permute-start = (bf16[64,32,128]{2,1,0:T(8,128)(2,1)}, bf16[64,32,128]{2,1,0:T(8,128)(2,1)}, u32[]{:S(2)}, u32[]{:S(2)}) collective-permute-start(bf16[64,32,128]{2,1,0:T(8,128)(2,1)} %reshape.193), channel_id=1, source_target_pairs={{0,1},{1,0},{2,3},{3,2},{4,5},{5,4},{6,7},{7,6},{8,9},{9,8},{10,11... | collective-permute-start | bytes 1572872 | tf_op jit(solution)/shard_map/ppermute | solution.py:11
  18.7 2.0 copy-start.2
  28.3 13.2 %collective-permute-start.1 = (bf16[64,32,128]{2,1,0:T(8,128)(2,1)S(1)}, bf16[64,32,128]{2,1,0:T(8,128)(2,1)S(1)}, u32[]{:S(2)}, u32[]{:S(2)}) collective-permute-start(bf16[64,32,128]{2,1,0:T(8,128)(2,1)S(1)} %reshape.195), channel_id=1, source_target_pairs={{0,2},{1,3},{2,0},{3,1},{4,6},{5,7},{6,4},{7,5},{8,10},{9,11},{10,... | collective-permute-start | bytes 1572872 | tf_op jit(solution)/shard_map/ppermute | solution.py:11
  45.1 24.4 %collective-permute-start.2 = (bf16[64,32,128]{2,1,0:T(8,128)(2,1)S(1)}, bf16[64,32,128]{2,1,0:T(8,128)(2,1)S(1)}, u32[]{:S(2)}, u32[]{:S(2)}) collective-permute-start(bf16[64,32,128]{2,1,0:T(8,128)(2,1)S(1)} %reshape.197), channel_id=1, source_target_pairs={{0,4},{1,5},{2,6},{3,7},{4,0},{5,1},{6,2},{7,3},{8,12},{9,13},{10,... | collective-permute-start | bytes 1572872 | tf_op jit(solution)/shard_map/ppermute | solution.py:11
  73.5 6.6 %copy-start.3 = (s32[256]{0:T(256)S(1)}, s32[256]{0:T(256)}, u32[]{:S(2)}) copy-start(s32[256]{0:T(256)} %param.11) | copy-start | bytes 3076
  75.6 18.2 %all-to-all-start = ((bf16[64,2,32,128]{3,1,0,2:T(2,128)(2,1)}), bf16[64,2,32,128]{3,1,0,2:T(2,128)(2,1)S(1)}, u32[]{:S(2)}, u32[]{:S(2)}) async-start(bf16[64,2,32,128]{3,1,0,2:T(2,128)(2,1)} %copy.18), calls=%async_computation | async-start | bytes 2097152 | tf_op jit(solution)/shard_map/all_to_all | solution.py:80
  278.9 21.3 %copy-start.1 = (bf16[64,2,32,256]{3,2,1,0:T(8,128)(2,1)S(1)}, bf16[64,2,32,256]{3,2,1,0:T(8,128)(2,1)}, u32[]{:S(2)}) copy-start(bf16[64,2,32,256]{3,2,1,0:T(8,128)(2,1)} %param.6) | copy-start | bytes 6291460
where the time goes:
time: 305 us; the launch traced here: 300 us
  matrix products  130 us (43%)
  other arithmetic  58.7 us (19%)
  local copies, waits for them, and re-layouts  57.2 us (19%)
  waiting for transfers between devices  43.4 us (14%)
  starting transfers between devices  11.2 us (4%)
    dot_general x1, matrix products, body(): jnp.einsum('epufl,pev->flvu', twisted, table2, preferred_element_type=jnp...  67 us
    convert_element_type x2, local copies, waits for them, and re-layouts, body(): return result.reshape(local_fields, row_count, NLON).astype(jnp.bfloat16)  39.9 us
    another operation x4, other arithmetic  34.3 us
    dot_general x1, matrix products, body(): jnp.einsum('aerfl,rapu->epufl', coeffs, table1, preferred_element_type=jn...  32.7 us
    ppermute x3, waiting for transfers between devices, partner(): lax.ppermute(shard, axis, [(i, i ^ 1 << bit) for i in range(lax.axis_size...  29.7 us
    another operation x1, other arithmetic, body(): jnp.stack([real_part * tc - imag_part * ts, real_part * ts + imag_part *...  22.9 us
    all_to_all x1, waiting for transfers between devices, body(): lax.all_to_all(lat_values, 'wave', split_axis=2, concat_axis=0, tiled=True)  13.6 us
    dot_general x1, matrix products, body(): jnp.einsum('qm,mrfl->qrfl', placement, scaled, preferred_element_type=jnp...  8.52 us
  transfers between devices with their start and end apart: 4, of which 4 were waited for; matrix products, arithmetic and copies ran while one was open for 5% of the time, Pallas kernels for 0%

commit v1 on v0

v1 whole, which is shorter than its diff:
```python
import jax
import jax.numpy as jnp
from jax import lax
from jax.sharding import PartitionSpec as P

NLON = 8192


def partner(shard, axis, bit):
    return lax.ppermute(shard, axis, [(i, i ^ 1 << bit) for i in range(lax.axis_size(axis))])


def wave_table(wavemap, lon_count):
    lanes = 128
    slots = wavemap.shape[0]
    scale = 2.0 * jnp.pi / lon_count
    q = wavemap[:, None]
    low = lax.broadcasted_iota(jnp.int32, (slots, lanes), 1)
    high = lanes * lax.broadcasted_iota(jnp.int32, (slots, lon_count // lanes), 1)
    low_angle = (q * low % lon_count).astype(jnp.float32) * scale
    high_angle = (q * high % lon_count).astype(jnp.float32) * scale
    weight = jnp.where(q == 0, 1.0, 2.0).astype(jnp.float32)
    cos_low, sin_low = (jnp.cos(low_angle) * weight)[:, None, :], (jnp.sin(low_angle) * weight)[:, None, :]
    cos_high, sin_high = jnp.cos(high_angle)[:, :, None], jnp.sin(high_angle)[:, :, None]
    cos_all = (cos_high * cos_low - sin_high * sin_low).reshape(slots, lon_count)
    sin_all = (sin_high * cos_low + cos_high * sin_low).reshape(slots, lon_count)
    return jnp.stack([cos_all, -sin_all]).astype(jnp.bfloat16)


def body(spectrum, leaf_map, level_maps, lat_map, skeleton, wavemap):
    slot_count = spectrum.shape[0]
    field_count = spectrum.shape[2]
    columns = 2 * field_count
    node_width = leaf_map.shape[2]
    half_width = node_width // 2
    flat_coef = spectrum.reshape(slot_count, columns, -1)
    degree_count = flat_coef.shape[2]
    degree_iota = lax.broadcasted_iota(jnp.int32, (slot_count, degree_count, node_width), 1)
    selector = (degree_iota == skeleton[:, None, :]).astype(jnp.bfloat16)
    picked = jnp.einsum("mcn,mnk->mck", flat_coef, selector, preferred_element_type=jnp.float32)
    node_state = (
        picked + jnp.einsum("mcn,mnk->mck", flat_coef, leaf_map, preferred_element_type=jnp.float32)
    ).astype(jnp.bfloat16)
    deg_index = lax.axis_index("deg")
    for level_num in range(level_maps.shape[0]):
        upper_bit = deg_index >> level_num & 1
        own_half = lax.dynamic_slice_in_dim(node_state, upper_bit * half_width, half_width, 2)
        payload = lax.dynamic_slice_in_dim(node_state, (1 - upper_bit) * half_width, half_width, 2)
        packed = payload.reshape(slot_count, columns // 2, 2 * half_width)
        factor = level_maps[level_num]
        own_rows = lax.dynamic_slice_in_dim(factor, upper_bit * half_width, half_width, 1)
        other_rows = lax.dynamic_slice_in_dim(factor, (1 - upper_bit) * half_width, half_width, 1)
        own_term = jnp.einsum(
            "mck,mks->mcs", own_half, own_rows, preferred_element_type=jnp.float32
        )
        arrived = partner(packed, "deg", level_num).reshape(payload.shape)
        other_term = jnp.einsum(
            "mck,mks->mcs", arrived, other_rows, preferred_element_type=jnp.float32
        )
        node_state = (own_term + other_term).astype(jnp.bfloat16)
    lat_values = jnp.einsum(
        "mck,mkl->mcl", node_state, lat_map, preferred_element_type=jnp.float32
    ).astype(jnp.bfloat16)
    lat_values = lat_values.reshape(slot_count, 2, field_count, -1)
    gathered = lax.all_to_all(lat_values, "wave", split_axis=2, concat_axis=0, tiled=True)
    local_fields = gathered.shape[2]
    row_count = gathered.shape[3]
    table = wave_table(wavemap, NLON)
    result = jnp.einsum("mrfl,rmn->fln", gathered, table, preferred_element_type=jnp.float32)
    return result.astype(jnp.bfloat16)


def solution(mesh):
    placed = (
        P("wave", None, None, "deg"),
        P("wave", "deg", None),
        P(None, "wave", "deg", None),
        P("wave", None, "deg"),
        P("wave", "deg"),
        P(),
    )
    return jax.shard_map(
        body, mesh=mesh, in_specs=placed, out_specs=P("wave", "deg", None), check_vma=False
    )
```

time: 305 us -> 120 us (0.39); the launches traced: 300 us -> 119 us
  matrix products: 130 us -> 36.4 us
  other arithmetic: 58.7 us -> 8.13 us
  local copies, waits for them, and re-layouts: 57.2 us -> 34 us
  waiting for transfers between devices: 43.4 us -> 29.1 us
    dot_general x3 -> x1, matrix products: 108 us -> 15.1 us  [body(): jnp.einsum('mrfl,rmn->fln', gathered, table, preferred_element_type=jnp.f...]
    another operation x6 -> x1, other arithmetic: 57.3 us -> 6.94 us
    convert_element_type x3 -> x0, local copies, waits for them, and re-layouts: 40.2 us -> none  [the longest x2 39.9 us: body(): return result.reshape(local_fields, row_count, NLON).astype(jnp.bfloat16)]
    all_to_all x1, waiting for transfers between devices: 13.6 us -> 0.01 us  [body(): lax.all_to_all(lat_values, 'wave', split_axis=2, concat_axis=0, tiled=True)]
    sub x0 -> x1, local copies, waits for them, and re-layouts: none -> 7.35 us  [wave_table(): cos_high * cos_low - sin_high * sin_low]
    neg x0 -> x1, local copies, waits for them, and re-layouts: none -> 7.31 us  [wave_table(): return jnp.stack([cos_all, -sin_all]).astype(jnp.bfloat16)]
  transfers between devices with their start and end apart: 4 -> 4, of which waited for: 4 -> 3; matrix products, arithmetic and copies ran while one was open for 5% -> 32% of each run, Pallas kernels for 0% -> 0%
where the time goes in v1:
time: 120 us; the launch traced here: 119 us
  matrix products  36.4 us (30%)
  local copies, waits for them, and re-layouts  34 us (28%)
  waiting for transfers between devices  29.1 us (24%)
  starting transfers between devices  11.1 us (9%)
  other arithmetic  8.13 us (7%)
    ppermute x3, waiting for transfers between devices, partner(): lax.ppermute(shard, axis, [(i, i ^ 1 << bit) for i in range(lax.axis_size...  29.1 us
    dot_general x1, matrix products, body(): jnp.einsum('mrfl,rmn->fln', gathered, table, preferred_element_type=jnp.f...  15.1 us
    dot_general x3, matrix products, body(): jnp.einsum('mck,mks->mcs', own_half, own_rows, preferred_element_type=jnp...  8.12 us
    slice x1, local copies, waits for them, and re-layouts, body(): factor = level_maps[level_num]  7.53 us
    ppermute x3, starting transfers between devices, partner(): lax.ppermute(shard, axis, [(i, i ^ 1 << bit) for i in range(lax.axis_size...  7.38 us
    sub x1, local copies, waits for them, and re-layouts, wave_table(): cos_high * cos_low - sin_high * sin_low  7.35 us
    neg x1, local copies, waits for them, and re-layouts, wave_table(): return jnp.stack([cos_all, -sin_all]).astype(jnp.bfloat16)  7.31 us
    another operation x1, other arithmetic  6.94 us
  transfers between devices with their start and end apart: 4, of which 3 were waited for; matrix products, arithmetic and copies ran while one was open for 32% of the time, Pallas kernels for 0%

profile of v1, /device:TPU:0, one launch (start us, length us, event | category | flops | bytes accessed | tf_op | source)
XLA Modules:
  0.0 118.9 jit_solution(7669824093544210791)
XLA Ops:
  0.0 0.0 copy-start
  0.0 1.6 %copy-done = bf16[64,2,32,256]{3,2,1,0:T(8,128)(2,1)S(1)} copy-done((bf16[64,2,32,256]{3,2,1,0:T(8,128)(2,1)S(1)}, bf16[64,2,32,256]{3,2,1,0:T(8,128)(2,1)}, u32[]{:S(2)}) %copy-start) | copy-done | bytes 2097176
  1.6 0.0 copy-start.5
  1.6 3.1 %fusion.46 = f32[64,64,128]{2,1,0:T(8,128)S(1)} fusion(bf16[64,64,256]{2,1,0:T(8,128)(2,1)S(1)} %bitcast.45, bf16[64,256,128]{2,1,0:T(8,128)(2,1)} %param.7), kind=kOutput, calls=%fused_computation.69 | convolution fusion | flops 268435456 | bytes 8388608 | tf_op jit(solution)/shard_map/mcn,mnk->mck/dot_general | solution.py:42
  4.7 0.0 copy-done.5
  4.7 1.9 %fusion.4 = bf16[64,64,128]{2,1,0:T(8,128)(2,1)S(1)} fusion(f32[64,64,128]{2,1,0:T(8,128)S(1)} %fusion.46, bf16[64,64,256]{2,1,0:T(8,128)(2,1)S(1)} %bitcast.44, s32[64,128]{1,0:T(8,128)S(1)} %copy-done.5), kind=kOutput, calls=%fused_computation.10 | convolution fusion | flops 271581184 | bytes 5275648 | tf_op jit(solution)/shard_map/mcn,mnk->mck/dot_general | solution.py:40
  6.6 0.4 constant_dynamic-slice_fusion.2
  6.9 1.3 %reshape.256 = bf16[64,32,128]{2,1,0:T(8,128)(2,1)} reshape(bf16[64,64,64]{2,1,0:T(8,128)(2,1)S(1)} %constant_dynamic-slice_fusion.2) | data formatting | bytes 1048576 | tf_op jit(solution)/shard_map/reshape | solution.py:49
  8.2 3.0 %collective-permute-start = (bf16[64,32,128]{2,1,0:T(8,128)(2,1)}, bf16[64,32,128]{2,1,0:T(8,128)(2,1)}, u32[]{:S(2)}, u32[]{:S(2)}) collective-permute-start(bf16[64,32,128]{2,1,0:T(8,128)(2,1)} %reshape.256), channel_id=1, source_target_pairs={{0,1},{1,0},{2,3},{3,2},{4,5},{5,4},{6,7},{7,6},{8,9},{9,8},{10,11... | collective-permute-start | bytes 1572872 | tf_op jit(solution)/shard_map/ppermute | solution.py:10
  11.2 7.5 %fusion.45 = (bf16[1,64,128,128]{3,2,1,0:T(8,128)(2,1)S(1)}, bf16[1,64,128,128]{3,2,1,0:T(8,128)(2,1)}, bf16[1,64,128,128]{3,2,1,0:T(8,128)(2,1)}) fusion(bf16[3,64,128,128]{3,2,1,0:T(8,128)(2,1)} %param.8), kind=kLoop, calls=%fused_computation.68 | loop fusion | bytes 12582912 | tf_op jit(solution)/shard_map/slice | solution.py:50
  18.7 0.0 copy-start.2
  18.7 2.0 %fusion.13 = f32[64,64,128]{2,1,0:T(8,128)} fusion(bf16[1,64,128,128]{3,2,1,0:T(8,128)(2,1)S(1)} %get-tuple-element.5, s32[]{:T(128)S(6)} %select_n.56, bf16[64,64,128]{2,1,0:T(8,128)(2,1)S(1)} %fusion.4), kind=kOutput, calls=%fused_computation.22 | convolution fusion | flops 67108864 | bytes 4195328 | tf_op jit(solution)/shard_map/mck,mks->mcs/dot_general | solution.py:53
  20.7 0.0 copy-done.2
  20.7 2.7 %collective-permute-done = bf16[64,32,128]{2,1,0:T(8,128)(2,1)} collective-permute-done((bf16[64,32,128]{2,1,0:T(8,128)(2,1)}, bf16[64,32,128]{2,1,0:T(8,128)(2,1)}, u32[]{:S(2)}, u32[]{:S(2)}) %collective-permute-start) | collective-permute-done | bytes 524320 | tf_op jit(solution)/shard_map/ppermute | solution.py:10
  23.4 1.6 %reshape.257 = bf16[64,64,64]{2,1,0:T(8,128)(2,1)S(1)} reshape(bf16[64,32,128]{2,1,0:T(8,128)(2,1)} %collective-permute-done) | data formatting | bytes 1048576 | tf_op jit(solution)/shard_map/reshape | solution.py:56
  25.1 2.4 %add_convert_fusion.2 = bf16[64,64,128]{2,1,0:T(8,128)(2,1)S(1)} fusion(f32[64,64,128]{2,1,0:T(8,128)} %fusion.13, bf16[64,64,64]{2,1,0:T(8,128)(2,1)S(1)} %reshape.257, bf16[1,64,128,128]{3,2,1,0:T(8,128)(2,1)} %copy-done.2, s32[]{:T(128)S(6)} %select_n.57), kind=kOutput, calls=%fused_computation.13 | convolution fusion | flops 68157440 | bytes 4718596 | tf_op jit(solution)/shard_map/mck,mks->mcs/dot_general | solution.py:57
  27.4 0.4 constant_dynamic-slice_fusion.1
  27.8 0.5 reshape.258
  28.3 1.9 %collective-permute-start.1 = (bf16[64,32,128]{2,1,0:T(8,128)(2,1)S(1)}, bf16[64,32,128]{2,1,0:T(8,128)(2,1)S(1)}, u32[]{:S(2)}, u32[]{:S(2)}) collective-permute-start(bf16[64,32,128]{2,1,0:T(8,128)(2,1)S(1)} %reshape.258), channel_id=1, source_target_pairs={{0,2},{1,3},{2,0},{3,1},{4,6},{5,7},{6,4},{7,5},{8,10},{9,11},{10,... | collective-permute-start | bytes 1572872 | tf_op jit(solution)/shard_map/ppermute | solution.py:10
  30.2 3.0 %fusion.10 = f32[64,64,128]{2,1,0:T(8,128)} fusion(bf16[1,64,128,128]{3,2,1,0:T(8,128)(2,1)} %get-tuple-element.7, s32[]{:T(128)S(6)} %select_n.58, bf16[64,64,128]{2,1,0:T(8,128)(2,1)S(1)} %add_convert_fusion.2), kind=kOutput, calls=%fused_computation.19 | convolution fusion | flops 67108864 | bytes 4195328 | tf_op jit(solution)/shard_map/mck,mks->mcs/dot_general | solution.py:53
  33.2 8.3 %collective-permute-done.1 = bf16[64,32,128]{2,1,0:T(8,128)(2,1)S(1)} collective-permute-done((bf16[64,32,128]{2,1,0:T(8,128)(2,1)S(1)}, bf16[64,32,128]{2,1,0:T(8,128)(2,1)S(1)}, u32[]{:S(2)}, u32[]{:S(2)}) %collective-permute-start.1) | collective-permute-done | bytes 524320 | tf_op jit(solution)/shard_map/ppermute | solution.py:10
  41.5 0.4 reshape.259
  41.9 2.4 %add_convert_fusion.1 = bf16[64,64,128]{2,1,0:T(8,128)(2,1)S(1)} fusion(f32[64,64,128]{2,1,0:T(8,128)} %fusion.10, bf16[64,64,64]{2,1,0:T(8,128)(2,1)S(1)} %reshape.259, bf16[1,64,128,128]{3,2,1,0:T(8,128)(2,1)} %get-tuple-element.7, s32[]{:T(128)S(6)} %select_n.59), kind=kOutput, calls=%fused_computation.12 | convolution fusion | flops 68157440 | bytes 4718596 | tf_op jit(solution)/shard_map/mck,mks->mcs/dot_general | solution.py:57
  44.3 0.0 copy-start.4
  44.3 0.4 constant_dynamic-slice_fusion
  44.7 0.5 reshape.260
  45.2 2.6 %collective-permute-start.2 = (bf16[64,32,128]{2,1,0:T(8,128)(2,1)S(1)}, bf16[64,32,128]{2,1,0:T(8,128)(2,1)S(1)}, u32[]{:S(2)}, u32[]{:S(2)}) collective-permute-start(bf16[64,32,128]{2,1,0:T(8,128)(2,1)S(1)} %reshape.260), channel_id=1, source_target_pairs={{0,4},{1,5},{2,6},{3,7},{4,0},{5,1},{6,2},{7,3},{8,12},{9,13},{10,... | collective-permute-start | bytes 1572872 | tf_op jit(solution)/shard_map/ppermute | solution.py:10
  47.7 0.0 copy-done.4
  47.7 0.6 fusion.36
  48.3 3.1 %fusion.7 = f32[64,64,128]{2,1,0:T(8,128)} fusion(bf16[1,64,128,128]{3,2,1,0:T(8,128)(2,1)} %get-tuple-element.6, s32[]{:T(128)S(6)} %select_n.60, bf16[64,64,128]{2,1,0:T(8,128)(2,1)S(1)} %add_convert_fusion.1), kind=kOutput, calls=%fused_computation.16 | convolution fusion | flops 67108864 | bytes 4195328 | tf_op jit(solution)/shard_map/mck,mks->mcs/dot_general | solution.py:53
  51.4 18.2 %collective-permute-done.2 = bf16[64,32,128]{2,1,0:T(8,128)(2,1)S(1)} collective-permute-done((bf16[64,32,128]{2,1,0:T(8,128)(2,1)S(1)}, bf16[64,32,128]{2,1,0:T(8,128)(2,1)S(1)}, u32[]{:S(2)}, u32[]{:S(2)}) %collective-permute-start.2) | collective-permute-done | bytes 524320 | tf_op jit(solution)/shard_map/ppermute | solution.py:10
  69.5 0.4 reshape.261
  70.0 3.5 %convolution_convert_fusion = bf16[64,64,128]{2,1,0:T(8,128)(2,1)S(1)} fusion(bf16[64,128,128]{2,1,0:T(8,128)(2,1)} %param.9, f32[64,64,128]{2,1,0:T(8,128)} %fusion.7, bf16[64,64,64]{2,1,0:T(8,128)(2,1)S(1)} %reshape.261, bf16[1,64,128,128]{3,2,1,0:T(8,128)(2,1)} %get-tuple-element.6, s32[]{:T(128)S(6)} %select_n.61), kind=kOutput, calls=%fused_computation.14 | convolution fusion | flops 202899456 | bytes 6815748 | tf_op jit(solution)/shard_map/mck,mkl->mcl/dot_general | solution.py:61
  73.5 2.1 %copy.11 = bf16[64,2,32,128]{3,1,0,2:T(2,128)(2,1)} copy(bf16[64,2,32,128]{3,2,1,0:T(8,128)(2,1)S(1)} %bitcast.47) | data formatting | bytes 2097152 | tf_op jit(solution)/shard_map/reshape | solution.py:64
  75.7 3.7 %all-to-all-start = ((bf16[64,2,32,128]{3,1,0,2:T(2,128)(2,1)}), bf16[64,2,32,128]{3,1,0,2:T(2,128)(2,1)S(1)}, u32[]{:S(2)}, u32[]{:S(2)}) async-start(bf16[64,2,32,128]{3,1,0,2:T(2,128)(2,1)} %copy.11), calls=%async_computation | async-start | bytes 2097152 | tf_op jit(solution)/shard_map/all_to_all | solution.py:65
  79.4 0.6 cosine_multiply_fusion
  80.0 6.9 %subtract_convert_fusion = (bf16[256,64,128]{2,1,0:T(8,128)(2,1)}, bf16[256,64,128]{2,1,0:T(8,128)(2,1)}) fusion(f32[256,128]{1,0:T(8,128)S(1)} %get-tuple-element.11, f32[256,64]{1,0:T(8,128)S(1)} %get-tuple-element.13, f32[256,128]{1,0:T(8,128)S(1)} %get-tuple-element.10, f32[256,64]{1,0:T(8,128)S(1)} %get-tuple-element.12), kind=kLoop, calls=%fused_computation.5 | loop fusion | flops 18874368 | bytes 8781824 | tf_op jit(solution)/shard_map/convert.3
  87.0 7.3 %sub.29 = bf16[1,256,8192]{2,1,0:T(8,128)(2,1)} reshape(bf16[256,64,128]{2,1,0:T(8,128)(2,1)} %get-tuple-element.8) | data formatting | bytes 8388608 | tf_op jit(solution)/shard_map/sub | solution.py:25
  94.3 7.3 %neg.14 = bf16[1,256,8192]{2,1,0:T(8,128)(2,1)} reshape(bf16[256,64,128]{2,1,0:T(8,128)(2,1)} %get-tuple-element.9) | data formatting | bytes 8388608 | tf_op jit(solution)/shard_map/neg | solution.py:27
  101.6 0.0 all-to-all-done
  101.6 0.0 copy-start.3
  101.6 1.2 %copy.19 = bf16[64,2,32,128]{3,2,1,0:T(8,128)(2,1)S(1)} copy(bf16[64,2,32,128]{3,1,0,2:T(2,128)(2,1)S(1)} %all-to-all-done) | data formatting | bytes 2097152 | tf_op jit(solution)/shard_map/all_to_all | solution.py:65
  102.8 0.2 copy.13
  103.0 0.8 copy-done.3
  103.8 0.0 copy-start.1
  103.8 15.1 %bitcast_convert_fusion = bf16[8,128,8192]{2,1,0:T(8,128)(2,1)} fusion(bf16[1,256,8192]{2,1,0:T(8,128)(2,1)} %neg.14, bf16[1,256,8192]{2,1,0:T(8,128)(2,1)S(1)} %copy-done.3, bf16[256,2,8,128]{3,2,1,0:T(8,128)(2,1)S(1)} %bitcast.48), kind=kOutput, calls=%fused_computation | convolution fusion | flops 8602517504 | bytes 26214400 | tf_op jit(solution)/shard_map/mrfl,rmn->fln/dot_general | solution.py:69
  118.9 0.0 copy-done.1
  (2 shorter events, 0.0 us)
Async XLA Ops:
  0.0 1.6 %copy-start = (bf16[64,2,32,256]{3,2,1,0:T(8,128)(2,1)S(1)}, bf16[64,2,32,256]{3,2,1,0:T(8,128)(2,1)}, u32[]{:S(2)}) copy-start(bf16[64,2,32,256]{3,2,1,0:T(8,128)(2,1)} %param.6) | copy-start | bytes 6291460
  1.6 3.1 %copy-start.5 = (s32[64,128]{1,0:T(8,128)S(1)}, s32[64,128]{1,0:T(8,128)}, u32[]{:S(2)}) copy-start(s32[64,128]{1,0:T(8,128)} %param.10) | copy-start | bytes 98308
  8.2 15.2 %collective-permute-start = (bf16[64,32,128]{2,1,0:T(8,128)(2,1)}, bf16[64,32,128]{2,1,0:T(8,128)(2,1)}, u32[]{:S(2)}, u32[]{:S(2)}) collective-permute-start(bf16[64,32,128]{2,1,0:T(8,128)(2,1)} %reshape.256), channel_id=1, source_target_pairs={{0,1},{1,0},{2,3},{3,2},{4,5},{5,4},{6,7},{7,6},{8,9},{9,8},{10,11... | collective-permute-start | bytes 1572872 | tf_op jit(solution)/shard_map/ppermute | solution.py:10
  18.7 2.0 %copy-start.2 = (bf16[1,64,128,128]{3,2,1,0:T(8,128)(2,1)}, bf16[1,64,128,128]{3,2,1,0:T(8,128)(2,1)S(1)}, u32[]{:S(2)}) copy-start(bf16[1,64,128,128]{3,2,1,0:T(8,128)(2,1)S(1)} %get-tuple-element.5) | copy-start | bytes 6291460
  28.3 13.2 %collective-permute-start.1 = (bf16[64,32,128]{2,1,0:T(8,128)(2,1)S(1)}, bf16[64,32,128]{2,1,0:T(8,128)(2,1)S(1)}, u32[]{:S(2)}, u32[]{:S(2)}) collective-permute-start(bf16[64,32,128]{2,1,0:T(8,128)(2,1)S(1)} %reshape.258), channel_id=1, source_target_pairs={{0,2},{1,3},{2,0},{3,1},{4,6},{5,7},{6,4},{7,5},{8,10},{9,11},{10,... | collective-permute-start | bytes 1572872 | tf_op jit(solution)/shard_map/ppermute | solution.py:10
  44.3 3.4 %copy-start.4 = (s32[256]{0:T(256)S(1)}, s32[256]{0:T(256)}, u32[]{:S(2)}) copy-start(s32[256]{0:T(256)} %param.11) | copy-start | bytes 3076
  45.2 24.4 %collective-permute-start.2 = (bf16[64,32,128]{2,1,0:T(8,128)(2,1)S(1)}, bf16[64,32,128]{2,1,0:T(8,128)(2,1)S(1)}, u32[]{:S(2)}, u32[]{:S(2)}) collective-permute-start(bf16[64,32,128]{2,1,0:T(8,128)(2,1)S(1)} %reshape.260), channel_id=1, source_target_pairs={{0,4},{1,5},{2,6},{3,7},{4,0},{5,1},{6,2},{7,3},{8,12},{9,13},{10,... | collective-permute-start | bytes 1572872 | tf_op jit(solution)/shard_map/ppermute | solution.py:10
  75.7 26.0 %all-to-all-start = ((bf16[64,2,32,128]{3,1,0,2:T(2,128)(2,1)}), bf16[64,2,32,128]{3,1,0,2:T(2,128)(2,1)S(1)}, u32[]{:S(2)}, u32[]{:S(2)}) async-start(bf16[64,2,32,128]{3,1,0,2:T(2,128)(2,1)} %copy.11), calls=%async_computation | async-start | bytes 2097152 | tf_op jit(solution)/shard_map/all_to_all | solution.py:65
  101.6 2.2 %copy-start.3 = (bf16[1,256,8192]{2,1,0:T(8,128)(2,1)S(1)}, bf16[1,256,8192]{2,1,0:T(8,128)(2,1)}, u32[]{:S(2)}) copy-start(bf16[1,256,8192]{2,1,0:T(8,128)(2,1)} %sub.29) | copy-start | bytes 12582916
  103.8 15.1 %copy-start.1 = (bf16[64,2,32,256]{3,2,1,0:T(8,128)(2,1)S(1)}, bf16[64,2,32,256]{3,2,1,0:T(8,128)(2,1)}, u32[]{:S(2)}) copy-start(bf16[64,2,32,256]{3,2,1,0:T(8,128)(2,1)} %param.6) | copy-start | bytes 6291460

commit v2 on v1

v2 whole, which is shorter than its diff:
```python
import functools

import jax
import jax.numpy as jnp
from jax import lax
from jax.experimental import pallas as pl
from jax.experimental.pallas import tpu as pltpu
from jax.sharding import PartitionSpec as P

NLON = 8192
CHUNKS = 2
GROUP = 16
LANES = 128
VMEM = 48 * 2**20


def exchange(shard, axis, step):
    return lax.ppermute(shard, axis, [(i, i ^ step) for i in range(lax.axis_size(axis))])


def low_lanes(rows, width):
    return lax.broadcasted_iota(jnp.int32, (rows, width), 1) < width // 2


def split_halves(state):
    fields, width = state.shape[0] // 2, state.shape[1]
    real, imag = state[:fields], state[fields:]
    low = low_lanes(fields, width)
    first = jnp.where(low, real, pltpu.roll(imag, width // 2, 1))
    second = jnp.where(low, pltpu.roll(real, width // 2, 1), imag)
    return first.astype(jnp.bfloat16), second.astype(jnp.bfloat16)


def join_halves(first, second):
    fields, width = first.shape
    low = low_lanes(fields, width)
    first, second = first.astype(jnp.float32), second.astype(jnp.float32)
    real = jnp.where(low, first, pltpu.roll(second, width // 2, 1))
    imag = jnp.where(low, pltpu.roll(first, width // 2, 1), second)
    return jnp.concatenate([real, imag], 0).astype(jnp.bfloat16)


def dot(a, b):
    return jnp.dot(a, b, preferred_element_type=jnp.float32)


def put_halves(upper, state, own_ref, send_ref, g):
    first, second = split_halves(state)
    own_ref[g] = jnp.where(upper == 1, second, first)
    send_ref[g] = jnp.where(upper == 1, first, second)


def joined_state(upper, own_ref, came_ref, g):
    own, came = own_ref[g], came_ref[g]
    return join_halves(jnp.where(upper == 1, came, own), jnp.where(upper == 1, own, came))


def leaf_kernel(upper_ref, coef_ref, map_ref, skel_ref, own_ref, send_ref):
    degrees, width = map_ref.shape[1:]
    rows = lax.broadcasted_iota(jnp.int32, (degrees, width), 0)
    for g in range(coef_ref.shape[0]):
        picks = (rows == skel_ref[g : g + 1, :]).astype(jnp.bfloat16)
        both = dot(coef_ref[g], jnp.concatenate([map_ref[g], picks], 1))
        put_halves(upper_ref[0], both[:, :width] + both[:, width:], own_ref, send_ref, g)


def level_kernel(upper_ref, own_in, came_in, map_ref, own_ref, send_ref):
    for g in range(own_in.shape[0]):
        joined = joined_state(upper_ref[0], own_in, came_in, g)
        put_halves(upper_ref[1], dot(joined, map_ref[0, g]), own_ref, send_ref, g)


def last_kernel(upper_ref, own_in, came_in, map_ref, lat_ref, *refs):
    out_refs, block_ref = refs[:-1], refs[-1]
    group, fields = own_in.shape[:2]
    peers = len(out_refs)
    share = fields // peers
    for g in range(group):
        joined = joined_state(upper_ref[0], own_in, came_in, g)
        node = dot(joined, map_ref[0, g]).astype(jnp.bfloat16)
        block_ref[g] = dot(node, lat_ref[g]).astype(jnp.bfloat16)
    tile = 16
    size = group * tile
    out_at = lax.broadcasted_iota(jnp.int32, (size, size), 0)
    in_at = lax.broadcasted_iota(jnp.int32, (size, size), 1)
    swap = ((out_at // group == in_at % tile) & (out_at % group == in_at // tile)).astype(jnp.bfloat16)
    rows = block_ref.shape[2]
    for c in range(0, 2 * fields, tile):
        moved = dot(swap, block_ref[:, c : c + tile, :].reshape(size, rows)).astype(jnp.bfloat16)
        moved = moved.reshape(tile, group, rows)
        part, first = c // fields, c % fields
        for at in range(0, tile, share):
            peer = (first + at) // share
            for step in range(peers):

                @pl.when((upper_ref[1] ^ peer) == step)
                def _():
                    out_refs[step][:, part, :, :] = moved[at : at + share]


def table_kernel(cos_low, sin_low, cos_high, sin_high, table_ref):
    cl, sl = cos_low[...], sin_low[...]
    for h in range(cos_high.shape[1]):
        ch, sh = cos_high[:, h : h + 1], sin_high[:, h : h + 1]
        table_ref[0, 0, :, h * LANES : (h + 1) * LANES] = (ch * cl - sh * sl).astype(jnp.bfloat16)
        table_ref[0, 1, :, h * LANES : (h + 1) * LANES] = (-(sh * cl) - ch * sl).astype(jnp.bfloat16)


def wave_table(slots, lon_count):
    blocks, count = slots.shape
    high = lon_count // LANES
    scale = 2.0 * jnp.pi / lon_count
    q = slots.reshape(-1, 1)
    total = q.shape[0]
    low_at = lax.broadcasted_iota(jnp.int32, (total, LANES), 1)
    high_at = LANES * lax.broadcasted_iota(jnp.int32, (total, high), 1)
    low_angle = (q * low_at % lon_count).astype(jnp.float32) * scale
    high_angle = (q * high_at % lon_count).astype(jnp.float32) * scale
    weight = jnp.where(q == 0, 1.0, 2.0).astype(jnp.float32)
    low_spec = pl.BlockSpec((count, LANES), lambda i: (i, 0))
    high_spec = pl.BlockSpec((count, high), lambda i: (i, 0))
    return pl.pallas_call(
        table_kernel,
        grid=(blocks,),
        in_specs=[low_spec, low_spec, high_spec, high_spec],
        out_specs=pl.BlockSpec((1, 2, count, lon_count), lambda i: (i, 0, 0, 0)),
        out_shape=jax.ShapeDtypeStruct((blocks, 2, count, lon_count), jnp.bfloat16),
        cost_estimate=pl.CostEstimate(
            flops=8 * total * lon_count, bytes_accessed=4 * total * lon_count, transcendentals=0
        ),
        compiler_params=pltpu.CompilerParams(vmem_limit_bytes=VMEM),
        name="table",
    )(
        jnp.cos(low_angle) * weight,
        jnp.sin(low_angle) * weight,
        jnp.cos(high_angle),
        jnp.sin(high_angle),
    )


def synthesis_kernel(*refs):
    block_refs, table_ref, out_ref, left_ref = refs[:-3], refs[-3], refs[-2], refs[-1]
    fields, rows = out_ref.shape[:2]

    @pl.when(pl.program_id(0) == 0)
    def _():
        for f in range(fields):
            parts = [ref[f].reshape(-1, rows) for ref in block_refs]
            left_ref[f * rows : (f + 1) * rows, :] = jnp.concatenate(parts, 0).T

    out = dot(left_ref[...], table_ref[...]).astype(jnp.bfloat16)
    out_ref[...] = out.reshape(out_ref.shape)


def synthesis(blocks, table):
    fields, _, _, rows = blocks[0].shape
    depth, lon_count = table.shape
    width = 8 * LANES
    return pl.pallas_call(
        synthesis_kernel,
        grid=(lon_count // width,),
        in_specs=[pl.BlockSpec(b.shape, lambda i: (0, 0, 0, 0)) for b in blocks]
        + [pl.BlockSpec((depth, width), lambda i: (0, i))],
        out_specs=pl.BlockSpec((fields, rows, width), lambda i: (0, 0, i)),
        out_shape=jax.ShapeDtypeStruct((fields, rows, lon_count), jnp.bfloat16),
        scratch_shapes=[pltpu.VMEM((fields * rows, depth), jnp.bfloat16)],
        cost_estimate=pl.CostEstimate(
            flops=2 * fields * rows * depth * lon_count,
            bytes_accessed=2 * lon_count * (fields * rows + depth),
            transcendentals=0,
        ),
        compiler_params=pltpu.CompilerParams(vmem_limit_bytes=VMEM),
        name="synthesis",
    )(*blocks, table)


def slot_spec(shape, first=0, lead=None):
    if lead is None:
        return pl.BlockSpec((GROUP,) + shape[1:], lambda i: (first + i,) + (0,) * (len(shape) - 1))
    return pl.BlockSpec((1, GROUP) + shape[2:], lambda i: (lead, first + i) + (0,) * (len(shape) - 2))


def body(spectrum, leaf_map, level_maps, lat_map, skeleton, wavemap):
    slots, _, fields, degrees = spectrum.shape
    columns = 2 * fields
    width = leaf_map.shape[2]
    levels = level_maps.shape[0]
    rows = lat_map.shape[2]
    coef = spectrum.reshape(slots, columns, degrees)
    peers = lax.axis_size("wave")
    me = lax.axis_index("wave")
    place = lax.axis_index("deg")
    bits = [place >> level & 1 for level in range(levels)]
    count = slots // CHUNKS
    steps = count // GROUP
    scalar = pl.BlockSpec(memory_space=pltpu.SMEM)
    params = pltpu.CompilerParams(vmem_limit_bytes=VMEM)
    half = jax.ShapeDtypeStruct((count, fields, width), jnp.bfloat16)
    half_spec = slot_spec(half.shape)

    def leaf(chunk):
        first = chunk * steps
        return pl.pallas_call(
            leaf_kernel,
            grid=(steps,),
            in_specs=[
                scalar,
                slot_spec(coef.shape, first),
                slot_spec(leaf_map.shape, first),
                slot_spec(skeleton.shape, first),
            ],
            out_specs=[half_spec, half_spec],
            out_shape=[half, half],
            cost_estimate=pl.CostEstimate(
                flops=4 * count * columns * degrees * width,
                bytes_accessed=2 * count * degrees * (columns + width),
                transcendentals=0,
            ),
            compiler_params=params,
            name="leaf",
        )(jnp.stack(bits[:1]), coef, leaf_map, skeleton)

    def level(chunk, num, own, came):
        first = chunk * steps
        return pl.pallas_call(
            level_kernel,
            grid=(steps,),
            in_specs=[scalar, half_spec, half_spec, slot_spec(level_maps.shape, first, num)],
            out_specs=[half_spec, half_spec],
            out_shape=[half, half],
            cost_estimate=pl.CostEstimate(
                flops=2 * count * columns * width * width,
                bytes_accessed=2 * count * width * (width + 2 * columns),
                transcendentals=0,
            ),
            compiler_params=params,
            name="level",
        )(jnp.stack(bits[num : num + 2]), own, came, level_maps)

    def last(chunk, own, came):
        first = chunk * steps
        share = fields // peers
        piece = jax.ShapeDtypeStruct((share, 2, count, rows), jnp.bfloat16)
        return pl.pallas_call(
            last_kernel,
            grid=(steps,),
            in_specs=[
                scalar,
                half_spec,
                half_spec,
                slot_spec(level_maps.shape, first, levels - 1),
                slot_spec(lat_map.shape, first),
            ],
            out_specs=[pl.BlockSpec((share, 2, GROUP, rows), lambda i: (0, 0, i, 0))] * peers,
            out_shape=[piece] * peers,
            scratch_shapes=[pltpu.VMEM((GROUP, columns, rows), jnp.bfloat16)],
            cost_estimate=pl.CostEstimate(
                flops=2 * count * columns * width * (width + rows),
                bytes_accessed=2 * count * width * (width + rows + 2 * columns),
                transcendentals=0,
            ),
            compiler_params=params,
            name="last",
        )(jnp.stack([bits[-1], me]), own, came, level_maps, lat_map)

    state = [leaf(chunk) for chunk in range(CHUNKS)]
    for num in range(levels):
        for chunk in range(CHUNKS):
            own, send = state[chunk]
            came = exchange(send, "deg", 1 << num)
            if num + 1 < levels:
                state[chunk] = level(chunk, num, own, came)
            else:
                state[chunk] = last(chunk, own, came)
    blocks = []
    for chunk in range(CHUNKS):
        for step in range(peers):
            piece = state[chunk][step]
            blocks.append(piece if step == 0 else exchange(piece, "wave", step))

    by_peer = wavemap.reshape(peers, CHUNKS, count)
    order = by_peer[me ^ jnp.arange(peers)].transpose(1, 0, 2).reshape(CHUNKS * peers, count)
    table = wave_table(order, NLON).reshape(-1, NLON)
    return synthesis(blocks, table)


def solution(mesh):
    placed = (
        P("wave", None, None, "deg"),
        P("wave", "deg", None),
        P(None, "wave", "deg", None),
        P("wave", None, "deg"),
        P("wave", "deg"),
        P(),
    )
    return jax.shard_map(
        body, mesh=mesh, in_specs=placed, out_specs=P("wave", "deg", None), check_vma=False
    )
```

time: 120 us -> 85.1 us (0.71)
  Pallas kernels: 0 us -> 45.5 us
  matrix products: 36.4 us -> 0 us
  local copies, waits for them, and re-layouts: 34 us -> 3.1 us
  waiting for transfers between devices: 29.1 us -> 17.4 us
  other arithmetic: 8.13 us -> 1.43 us
  starting transfers between devices: 11.1 us -> 16.8 us
    pallas_call x0 -> x10, Pallas kernels: none -> 45.5 us  [the longest x1 15.4 us: synthesis(): pl.pallas_call(synthesis_kernel, grid=(lon_count // width,), in_specs=[pl...]
    dot_general x9 -> x0, matrix products: 36.4 us -> none  [the longest x1 15.1 us: body(): jnp.einsum('mrfl,rmn->fln', gathered, table, preferred_element_type=jnp.f...]
    ppermute x3 -> x12, waiting for transfers between devices: 29.1 us -> 17.4 us  [exchange(): lax.ppermute(shard, axis, [(i, i ^ step) for i in range(lax.axis_size(axi...]
    ppermute x3 -> x12, starting transfers between devices: 7.38 us -> 16.8 us  [exchange(): lax.ppermute(shard, axis, [(i, i ^ step) for i in range(lax.axis_size(axi...]
    slice x1 -> x0, local copies, waits for them, and re-layouts: 7.53 us -> none  [body(): factor = level_maps[level_num]]
    sub x1 -> x0, local copies, waits for them, and re-layouts: 7.35 us -> none  [wave_table(): cos_high * cos_low - sin_high * sin_low]
    neg x1 -> x0, local copies, waits for them, and re-layouts: 7.31 us -> none  [wave_table(): return jnp.stack([cos_all, -sin_all]).astype(jnp.bfloat16)]
    reshape x7 -> x1, local copies, waits for them, and re-layouts: 6.86 us -> 0.08 us  [body(): by_peer = wavemap.reshape(peers, CHUNKS, count)]
  transfers between devices with their start and end apart: 4 -> 12, of which waited for: 3 -> 4; matrix products, arithmetic and copies ran while one was open for 32% -> 3% of each run, Pallas kernels for 0% -> 33%
where the time goes in v2:
time: 85.1 us; the launch traced here: 84.3 us
  Pallas kernels  45.5 us (53%)
  waiting for transfers between devices  17.4 us (20%)
  starting transfers between devices  16.8 us (20%)
  local copies, waits for them, and re-layouts  3.1 us (4%)
  other arithmetic  1.43 us (2%)
    ppermute x12, waiting for transfers between devices, exchange(): lax.ppermute(shard, axis, [(i, i ^ step) for i in range(lax.axis_size(axi...  17.4 us
    ppermute x12, starting transfers between devices, exchange(): lax.ppermute(shard, axis, [(i, i ^ step) for i in range(lax.axis_size(axi...  16.8 us
    pallas_call x1, Pallas kernels, synthesis(): pl.pallas_call(synthesis_kernel, grid=(lon_count // width,), in_specs=[pl...  15.4 us
    pallas_call x4, Pallas kernels, level(): pl.pallas_call(level_kernel, grid=(steps,), in_specs=[scalar, half_spec,...  9.09 us
    pallas_call x2, Pallas kernels, last(): pl.pallas_call(last_kernel, grid=(steps,), in_specs=[scalar, half_spec, h...  8.49 us
    pallas_call x1, Pallas kernels, wave_table(): pl.pallas_call(table_kernel, grid=(blocks,), in_specs=[low_spec, low_spec...  7.66 us
    pallas_call x2, Pallas kernels, leaf(): pl.pallas_call(leaf_kernel, grid=(steps,), in_specs=[scalar, slot_spec(co...  4.81 us
    unnamed x8, local copies, waits for them, and re-layouts  2.36 us
  transfers between devices with their start and end apart: 12, of which 4 were waited for; matrix products, arithmetic and copies ran while one was open for 3% of the time, Pallas kernels for 33%

profile of v2, /device:TPU:0, one launch (start us, length us, event | category | flops | bytes accessed | tf_op | source)
XLA Modules:
  0.0 84.3 jit_solution(7776490618275229833)
XLA Ops:
  0.0 0.0 copy-start
  0.0 1.6 %copy-done = bf16[64,2,32,256]{3,2,1,0:T(8,128)(2,1)S(1)} copy-done((bf16[64,2,32,256]{3,2,1,0:T(8,128)(2,1)S(1)}, bf16[64,2,32,256]{3,2,1,0:T(8,128)(2,1)}, u32[]{:S(2)}) %copy-start) | copy-done | bytes 2097176
  1.6 0.8 copy-done.2
  2.4 2.4 %leaf.3 = (bf16[32,32,128]{2,1,0:T(8,128)(2,1)S(1)}, bf16[32,32,128]{2,1,0:T(8,128)(2,1)S(1)}) custom-call(s32[1]{0:T(128)} %bitcast.3.upper_ref, bf16[64,64,256]{2,1,0:T(8,128)(2,1)S(1)} %bitcast.9, bf16[64,256,128]{2,1,0:T(8,128)(2,1)} %map_ref.12, s32[64,128]{1,0:T(8,128)S(1)} %copy-done.2), custom_call_target="tpu_custom_call" | custom-call | flops 268435456 | bytes 3145728 | tf_op jit(solution)/shard_map/leaf/pallas_call | solution.py:203
  4.8 3.0 %collective-permute-start.6 = (bf16[32,32,128]{2,1,0:T(8,128)(2,1)S(1)}, bf16[32,32,128]{2,1,0:T(8,128)(2,1)S(1)}, u32[]{:S(2)}, u32[]{:S(2)}) collective-permute-start(bf16[32,32,128]{2,1,0:T(8,128)(2,1)S(1)} %get-tuple-element.36), channel_id=1, source_target_pairs={{0,1},{1,0},{2,3},{3,2},{4,5},{5,4},{6,7},{7,6},{8,9},{9,8},{10,11... | collective-permute-start | bytes 786440 | tf_op jit(solution)/shard_map/ppermute | solution.py:18
  7.8 2.4 %leaf.2 = (bf16[32,32,128]{2,1,0:T(8,128)(2,1)S(1)}, bf16[32,32,128]{2,1,0:T(8,128)(2,1)S(1)}) custom-call(s32[1]{0:T(128)} %bitcast.3.upper_ref, bf16[64,64,256]{2,1,0:T(8,128)(2,1)S(1)} %bitcast.10, bf16[64,256,128]{2,1,0:T(8,128)(2,1)} %map_ref.12, s32[64,128]{1,0:T(8,128)S(1)} %copy-done.2), custom_call_target="tpu_custom_call" | custom-call | flops 268435456 | bytes 3145728 | tf_op jit(solution)/shard_map/leaf/pallas_call | solution.py:203
  10.2 0.1 collective-permute-start
  10.3 0.1 pad_add_fusion.2.upper_ref
  10.4 4.6 %collective-permute-done.6.came_in = bf16[32,32,128]{2,1,0:T(8,128)(2,1)S(1)} collective-permute-done((bf16[32,32,128]{2,1,0:T(8,128)(2,1)S(1)}, bf16[32,32,128]{2,1,0:T(8,128)(2,1)S(1)}, u32[]{:S(2)}, u32[]{:S(2)}) %collective-permute-start.6) | collective-permute-done | bytes 262176 | tf_op jit(solution)/shard_map/ppermute | solution.py:18
  14.9 1.9 %level.6 = (bf16[32,32,128]{2,1,0:T(8,128)(2,1)S(1)}, bf16[32,32,128]{2,1,0:T(8,128)(2,1)S(1)}) custom-call(s32[2]{0:T(128)S(1)} %pad_add_fusion.2.upper_ref, bf16[32,32,128]{2,1,0:T(8,128)(2,1)S(1)} %get-tuple-element.35.own_in, bf16[32,32,128]{2,1,0:T(8,128)(2,1)S(1)} %collective-permute-done.6.came_in, bf16[3,64,128,128]{3,2,1,0:T(8,128)(2,1)} %map_ref.15), custom_call_target="tpu_custom_call" | custom-call | flops 67108864 | bytes 2097152 | tf_op jit(solution)/shard_map/level/pallas_call | solution.py:225
  16.9 2.2 %collective-permute-start.7 = (bf16[32,32,128]{2,1,0:T(8,128)(2,1)S(1)}, bf16[32,32,128]{2,1,0:T(8,128)(2,1)S(1)}, u32[]{:S(2)}, u32[]{:S(2)}) collective-permute-start(bf16[32,32,128]{2,1,0:T(8,128)(2,1)S(1)} %get-tuple-element.38), channel_id=1, source_target_pairs={{0,2},{1,3},{2,0},{3,1},{4,6},{5,7},{6,4},{7,5},{8,10},{9,11},{10,... | collective-permute-start | bytes 786440 | tf_op jit(solution)/shard_map/ppermute | solution.py:18
  19.0 0.1 pad_add_fusion.1.upper_ref
  19.1 0.6 collective-permute-done.came_in
  19.7 0.0 copy-start.3
  19.7 2.6 %level.4 = (bf16[32,32,128]{2,1,0:T(8,128)(2,1)S(1)}, bf16[32,32,128]{2,1,0:T(8,128)(2,1)}) custom-call(s32[2]{0:T(128)S(1)} %pad_add_fusion.2.upper_ref, bf16[32,32,128]{2,1,0:T(8,128)(2,1)S(1)} %get-tuple-element.25.own_in, bf16[32,32,128]{2,1,0:T(8,128)(2,1)S(1)} %collective-permute-done.came_in, bf16[3,64,128,128]{3,2,1,0:T(8,128)(2,1)} %map_ref.15), custom_call_target="tpu_custom_call" | custom-call | flops 67108864 | bytes 2097152 | tf_op jit(solution)/shard_map/level/pallas_call | solution.py:225
  22.3 1.8 %collective-permute-start.1 = (bf16[32,32,128]{2,1,0:T(8,128)(2,1)}, bf16[32,32,128]{2,1,0:T(8,128)(2,1)S(1)}, u32[]{:S(2)}, u32[]{:S(2)}) collective-permute-start(bf16[32,32,128]{2,1,0:T(8,128)(2,1)} %get-tuple-element.28), channel_id=1, source_target_pairs={{0,2},{1,3},{2,0},{3,1},{4,6},{5,7},{6,4},{7,5},{8,10},{9,11},{10,... | collective-permute-start | bytes 786440 | tf_op jit(solution)/shard_map/ppermute | solution.py:18
  24.1 0.0 collective-permute-done.7.came_in
  24.1 2.7 %level.7 = (bf16[32,32,128]{2,1,0:T(8,128)(2,1)S(1)}, bf16[32,32,128]{2,1,0:T(8,128)(2,1)}) custom-call(s32[2]{0:T(128)S(1)} %pad_add_fusion.1.upper_ref, bf16[32,32,128]{2,1,0:T(8,128)(2,1)S(1)} %get-tuple-element.37.own_in, bf16[32,32,128]{2,1,0:T(8,128)(2,1)S(1)} %collective-permute-done.7.came_in, bf16[3,64,128,128]{3,2,1,0:T(8,128)(2,1)} %map_ref.15), custom_call_target="tpu_custom_call" | custom-call | flops 67108864 | bytes 2097152 | tf_op jit(solution)/shard_map/level/pallas_call | solution.py:225
  26.8 2.6 %collective-permute-start.8 = (bf16[32,32,128]{2,1,0:T(8,128)(2,1)}, bf16[32,32,128]{2,1,0:T(8,128)(2,1)S(1)}, u32[]{:S(2)}, u32[]{:S(2)}) collective-permute-start(bf16[32,32,128]{2,1,0:T(8,128)(2,1)} %get-tuple-element.40), channel_id=1, source_target_pairs={{0,4},{1,5},{2,6},{3,7},{4,0},{5,1},{6,2},{7,3},{8,12},{9,13},{10,... | collective-permute-start | bytes 786440 | tf_op jit(solution)/shard_map/ppermute | solution.py:18
  29.4 0.1 pad_add_fusion.upper_ref
  29.5 0.0 copy-done.3
  29.5 0.1 reshape.36
  29.5 0.6 gather_fusion
  30.1 0.1 mul.51
  30.2 1.2 %collective-permute-done.1.came_in = bf16[32,32,128]{2,1,0:T(8,128)(2,1)S(1)} collective-permute-done((bf16[32,32,128]{2,1,0:T(8,128)(2,1)}, bf16[32,32,128]{2,1,0:T(8,128)(2,1)S(1)}, u32[]{:S(2)}, u32[]{:S(2)}) %collective-permute-start.1) | collective-permute-done | bytes 262176 | tf_op jit(solution)/shard_map/ppermute | solution.py:18
  31.4 1.9 %level.5 = (bf16[32,32,128]{2,1,0:T(8,128)(2,1)S(1)}, bf16[32,32,128]{2,1,0:T(8,128)(2,1)S(1)}) custom-call(s32[2]{0:T(128)S(1)} %pad_add_fusion.1.upper_ref, bf16[32,32,128]{2,1,0:T(8,128)(2,1)S(1)} %get-tuple-element.27.own_in, bf16[32,32,128]{2,1,0:T(8,128)(2,1)S(1)} %collective-permute-done.1.came_in, bf16[3,64,128,128]{3,2,1,0:T(8,128)(2,1)} %map_ref.15), custom_call_target="tpu_custom_call" | custom-call | flops 67108864 | bytes 2097152 | tf_op jit(solution)/shard_map/level/pallas_call | solution.py:225
  33.4 3.2 %collective-permute-start.2 = (bf16[32,32,128]{2,1,0:T(8,128)(2,1)S(1)}, bf16[32,32,128]{2,1,0:T(8,128)(2,1)S(1)}, u32[]{:S(2)}, u32[]{:S(2)}) collective-permute-start(bf16[32,32,128]{2,1,0:T(8,128)(2,1)S(1)} %get-tuple-element.30), channel_id=1, source_target_pairs={{0,4},{1,5},{2,6},{3,7},{4,0},{5,1},{6,2},{7,3},{8,12},{9,13},{10,... | collective-permute-start | bytes 786440 | tf_op jit(solution)/shard_map/ppermute | solution.py:18
  36.5 11.0 %collective-permute-done.8.came_in = bf16[32,32,128]{2,1,0:T(8,128)(2,1)S(1)} collective-permute-done((bf16[32,32,128]{2,1,0:T(8,128)(2,1)}, bf16[32,32,128]{2,1,0:T(8,128)(2,1)S(1)}, u32[]{:S(2)}, u32[]{:S(2)}) %collective-permute-start.8) | collective-permute-done | bytes 262176 | tf_op jit(solution)/shard_map/ppermute | solution.py:18
  47.6 0.0 copy-done.1
  47.6 4.2 %last.3 = (bf16[8,2,32,128]{3,2,1,0:T(8,128)(2,1)S(1)}, bf16[8,2,32,128]{3,2,1,0:T(8,128)(2,1)S(1)}, bf16[8,2,32,128]{3,2,1,0:T(8,128)(2,1)S(1)}, bf16[8,2,32,128]{3,2,1,0:T(8,128)(2,1)S(1)}) custom-call(s32[2]{0:T(128)S(1)} %pad_add_fusion.upper_ref, bf16[32,32,128]{2,1,0:T(8,128)(2,1)S(1)} %get-tuple-element.39.own_in, ...), custom_call_target="tpu_custom_call" | custom-call | flops 134217728 | bytes 3145728 | tf_op jit(solution)/shard_map/last/pallas_call | solution.py:244
  51.8 0.1 collective-permute-start.9
  51.9 0.6 sine_multiply_fusion
  52.5 1.6 %collective-permute-start.10 = (bf16[8,2,32,128]{3,2,1,0:T(8,128)(2,1)S(1)}, bf16[8,2,32,128]{3,2,1,0:T(8,128)(2,1)S(1)}, u32[]{:S(2)}, u32[]{:S(2)}) collective-permute-start(bf16[8,2,32,128]{3,2,1,0:T(8,128)(2,1)S(1)} %get-tuple-element.43), channel_id=1, source_target_pairs={{0,16},{8,24},{16,0},{24,8},{1,17},{9,25},{17,1},{25,9},{2,18},{10... | collective-permute-start | bytes 393224 | tf_op jit(solution)/shard_map/ppermute | solution.py:18
  54.1 0.4 collective-permute-start.11
  54.4 0.0 collective-permute-done.2.came_in
  54.4 4.2 %last.2 = (bf16[8,2,32,128]{3,2,1,0:T(8,128)(2,1)S(1)}, bf16[8,2,32,128]{3,2,1,0:T(8,128)(2,1)S(1)}, bf16[8,2,32,128]{3,2,1,0:T(8,128)(2,1)S(1)}, bf16[8,2,32,128]{3,2,1,0:T(8,128)(2,1)S(1)}) custom-call(s32[2]{0:T(128)S(1)} %pad_add_fusion.upper_ref, bf16[32,32,128]{2,1,0:T(8,128)(2,1)S(1)} %get-tuple-element.29.own_in, ...), custom_call_target="tpu_custom_call" | custom-call | flops 134217728 | bytes 3145728 | tf_op jit(solution)/shard_map/last/pallas_call | solution.py:244
  58.7 0.3 collective-permute-start.3
  59.0 1.5 %collective-permute-start.4 = (bf16[8,2,32,128]{3,2,1,0:T(8,128)(2,1)S(1)}, bf16[8,2,32,128]{3,2,1,0:T(8,128)(2,1)S(1)}, u32[]{:S(2)}, u32[]{:S(2)}) collective-permute-start(bf16[8,2,32,128]{3,2,1,0:T(8,128)(2,1)S(1)} %get-tuple-element.33), channel_id=1, source_target_pairs={{0,16},{8,24},{16,0},{24,8},{1,17},{9,25},{17,1},{25,9},{2,18},{10... | collective-permute-start | bytes 393224 | tf_op jit(solution)/shard_map/ppermute | solution.py:18
  60.5 0.0 collective-permute-done.9.refs_5_
  60.5 0.1 collective-permute-start.5
  60.6 0.6 fusion.9
  61.2 7.7 %table.1 = bf16[8,2,32,8192]{3,2,1,0:T(8,128)(2,1)} custom-call(f32[256,128]{1,0:T(8,128)S(1)} %get-tuple-element.46.cos_low, f32[256,128]{1,0:T(8,128)S(1)} %get-tuple-element.45.sin_low, f32[256,64]{1,0:T(8,128)S(1)} %get-tuple-element.48.cos_high, f32[256,64]{1,0:T(8,128)S(1)} %get-tuple-element.47.sin_high), custom_call_target="tpu_custom_call" | custom-call | flops 16777216 | bytes 8388608 | tf_op jit(solution)/shard_map/table/pallas_call | solution.py:122
  68.9 0.0 collective-permute-done.10.refs_6_
  68.9 0.0 collective-permute-done.11.refs_7_
  68.9 0.0 collective-permute-done.3.refs_1_
  68.9 0.0 collective-permute-done.4.refs_2_
  68.9 0.0 collective-permute-done.5.refs_3_
  68.9 15.4 %synthesis.1 = bf16[8,128,8192]{2,1,0:T(8,128)(2,1)} custom-call(bf16[8,2,32,128]{3,2,1,0:T(8,128)(2,1)S(1)} %get-tuple-element.31.refs_0_, bf16[8,2,32,128]{3,2,1,0:T(8,128)(2,1)S(1)} %collective-permute-done.3.refs_1_, bf16[8,2,32,128]{3,2,1,0:T(8,128)(2,1)S(1)} %collective-permute-done.4.refs_2_, ...), custom_call_target="tpu_custom_call" | custom-call | flops 8589934592 | bytes 25165824 | tf_op jit(solution)/shard_map/synthesis/pallas_call | solution.py:159
  (7 shorter events, 0.0 us)
Async XLA Ops:
  0.0 1.6 %copy-start = (bf16[64,2,32,256]{3,2,1,0:T(8,128)(2,1)S(1)}, bf16[64,2,32,256]{3,2,1,0:T(8,128)(2,1)}, u32[]{:S(2)}) copy-start(bf16[64,2,32,256]{3,2,1,0:T(8,128)(2,1)} %param.6) | copy-start | bytes 6291460
  1.6 0.8 copy-start.2
  4.8 10.2 %collective-permute-start.6 = (bf16[32,32,128]{2,1,0:T(8,128)(2,1)S(1)}, bf16[32,32,128]{2,1,0:T(8,128)(2,1)S(1)}, u32[]{:S(2)}, u32[]{:S(2)}) collective-permute-start(bf16[32,32,128]{2,1,0:T(8,128)(2,1)S(1)} %get-tuple-element.36), channel_id=1, source_target_pairs={{0,1},{1,0},{2,3},{3,2},{4,5},{5,4},{6,7},{7,6},{8,9},{9,8},{10,11... | collective-permute-start | bytes 786440 | tf_op jit(solution)/shard_map/ppermute | solution.py:18
  10.2 9.5 %collective-permute-start = (bf16[32,32,128]{2,1,0:T(8,128)(2,1)S(1)}, bf16[32,32,128]{2,1,0:T(8,128)(2,1)S(1)}, u32[]{:S(2)}, u32[]{:S(2)}) collective-permute-start(bf16[32,32,128]{2,1,0:T(8,128)(2,1)S(1)} %get-tuple-element.26), channel_id=1, source_target_pairs={{0,1},{1,0},{2,3},{3,2},{4,5},{5,4},{6,7},{7,6},{8,9},{9,8},{10,11... | collective-permute-start | bytes 786440 | tf_op jit(solution)/shard_map/ppermute | solution.py:18
  16.9 7.2 %collective-permute-start.7 = (bf16[32,32,128]{2,1,0:T(8,128)(2,1)S(1)}, bf16[32,32,128]{2,1,0:T(8,128)(2,1)S(1)}, u32[]{:S(2)}, u32[]{:S(2)}) collective-permute-start(bf16[32,32,128]{2,1,0:T(8,128)(2,1)S(1)} %get-tuple-element.38), channel_id=1, source_target_pairs={{0,2},{1,3},{2,0},{3,1},{4,6},{5,7},{6,4},{7,5},{8,10},{9,11},{10,... | collective-permute-start | bytes 786440 | tf_op jit(solution)/shard_map/ppermute | solution.py:18
  19.7 9.7 %copy-start.3 = (s32[256]{0:T(256)S(1)}, s32[256]{0:T(256)}, u32[]{:S(2)}) copy-start(s32[256]{0:T(256)} %param.11) | copy-start | bytes 3076
  22.3 9.2 %collective-permute-start.1 = (bf16[32,32,128]{2,1,0:T(8,128)(2,1)}, bf16[32,32,128]{2,1,0:T(8,128)(2,1)S(1)}, u32[]{:S(2)}, u32[]{:S(2)}) collective-permute-start(bf16[32,32,128]{2,1,0:T(8,128)(2,1)} %get-tuple-element.28), channel_id=1, source_target_pairs={{0,2},{1,3},{2,0},{3,1},{4,6},{5,7},{6,4},{7,5},{8,10},{9,11},{10,... | collective-permute-start | bytes 786440 | tf_op jit(solution)/shard_map/ppermute | solution.py:18
  24.1 23.5 %copy-start.1 = (bf16[64,128,128]{2,1,0:T(8,128)(2,1)S(1)}, bf16[64,128,128]{2,1,0:T(8,128)(2,1)}, u32[]{:S(2)}) copy-start(bf16[64,128,128]{2,1,0:T(8,128)(2,1)} %lat_ref.3) | copy-start | bytes 6291460
  26.8 20.8 %collective-permute-start.8 = (bf16[32,32,128]{2,1,0:T(8,128)(2,1)}, bf16[32,32,128]{2,1,0:T(8,128)(2,1)S(1)}, u32[]{:S(2)}, u32[]{:S(2)}) collective-permute-start(bf16[32,32,128]{2,1,0:T(8,128)(2,1)} %get-tuple-element.40), channel_id=1, source_target_pairs={{0,4},{1,5},{2,6},{3,7},{4,0},{5,1},{6,2},{7,3},{8,12},{9,13},{10,... | collective-permute-start | bytes 786440 | tf_op jit(solution)/shard_map/ppermute | solution.py:18
  33.4 21.1 %collective-permute-start.2 = (bf16[32,32,128]{2,1,0:T(8,128)(2,1)S(1)}, bf16[32,32,128]{2,1,0:T(8,128)(2,1)S(1)}, u32[]{:S(2)}, u32[]{:S(2)}) collective-permute-start(bf16[32,32,128]{2,1,0:T(8,128)(2,1)S(1)} %get-tuple-element.30), channel_id=1, source_target_pairs={{0,4},{1,5},{2,6},{3,7},{4,0},{5,1},{6,2},{7,3},{8,12},{9,13},{10,... | collective-permute-start | bytes 786440 | tf_op jit(solution)/shard_map/ppermute | solution.py:18
  51.8 8.7 %collective-permute-start.9 = (bf16[8,2,32,128]{3,2,1,0:T(8,128)(2,1)S(1)}, bf16[8,2,32,128]{3,2,1,0:T(8,128)(2,1)S(1)}, u32[]{:S(2)}, u32[]{:S(2)}) collective-permute-start(bf16[8,2,32,128]{3,2,1,0:T(8,128)(2,1)S(1)} %get-tuple-element.42), channel_id=1, source_target_pairs={{0,8},{8,0},{16,24},{24,16},{1,9},{9,1},{17,25},{25,17},{2,10},{10... | collective-permute-start | bytes 393224 | tf_op jit(solution)/shard_map/ppermute | solution.py:18
  52.5 16.4 %collective-permute-start.10 = (bf16[8,2,32,128]{3,2,1,0:T(8,128)(2,1)S(1)}, bf16[8,2,32,128]{3,2,1,0:T(8,128)(2,1)S(1)}, u32[]{:S(2)}, u32[]{:S(2)}) collective-permute-start(bf16[8,2,32,128]{3,2,1,0:T(8,128)(2,1)S(1)} %get-tuple-element.43), channel_id=1, source_target_pairs={{0,16},{8,24},{16,0},{24,8},{1,17},{9,25},{17,1},{25,9},{2,18},{10... | collective-permute-start | bytes 393224 | tf_op jit(solution)/shard_map/ppermute | solution.py:18
  54.1 14.8 %collective-permute-start.11 = (bf16[8,2,32,128]{3,2,1,0:T(8,128)(2,1)S(1)}, bf16[8,2,32,128]{3,2,1,0:T(8,128)(2,1)S(1)}, u32[]{:S(2)}, u32[]{:S(2)}) collective-permute-start(bf16[8,2,32,128]{3,2,1,0:T(8,128)(2,1)S(1)} %get-tuple-element.44), channel_id=1, source_target_pairs={{0,24},{8,16},{16,8},{24,0},{1,25},{9,17},{17,9},{25,1},{2,26},{10... | collective-permute-start | bytes 393224 | tf_op jit(solution)/shard_map/ppermute | solution.py:18
  58.7 10.2 %collective-permute-start.3 = (bf16[8,2,32,128]{3,2,1,0:T(8,128)(2,1)S(1)}, bf16[8,2,32,128]{3,2,1,0:T(8,128)(2,1)S(1)}, u32[]{:S(2)}, u32[]{:S(2)}) collective-permute-start(bf16[8,2,32,128]{3,2,1,0:T(8,128)(2,1)S(1)} %get-tuple-element.32), channel_id=1, source_target_pairs={{0,8},{8,0},{16,24},{24,16},{1,9},{9,1},{17,25},{25,17},{2,10},{10... | collective-permute-start | bytes 393224 | tf_op jit(solution)/shard_map/ppermute | solution.py:18
  59.0 9.9 %collective-permute-start.4 = (bf16[8,2,32,128]{3,2,1,0:T(8,128)(2,1)S(1)}, bf16[8,2,32,128]{3,2,1,0:T(8,128)(2,1)S(1)}, u32[]{:S(2)}, u32[]{:S(2)}) collective-permute-start(bf16[8,2,32,128]{3,2,1,0:T(8,128)(2,1)S(1)} %get-tuple-element.33), channel_id=1, source_target_pairs={{0,16},{8,24},{16,0},{24,8},{1,17},{9,25},{17,1},{25,9},{2,18},{10... | collective-permute-start | bytes 393224 | tf_op jit(solution)/shard_map/ppermute | solution.py:18
  60.5 8.4 %collective-permute-start.5 = (bf16[8,2,32,128]{3,2,1,0:T(8,128)(2,1)S(1)}, bf16[8,2,32,128]{3,2,1,0:T(8,128)(2,1)S(1)}, u32[]{:S(2)}, u32[]{:S(2)}) collective-permute-start(bf16[8,2,32,128]{3,2,1,0:T(8,128)(2,1)S(1)} %get-tuple-element.34), channel_id=1, source_target_pairs={{0,24},{8,16},{16,8},{24,0},{1,25},{9,17},{17,9},{25,1},{2,26},{10... | collective-permute-start | bytes 393224 | tf_op jit(solution)/shard_map/ppermute | solution.py:18

commit v3 on v1

v3 whole, which is shorter than its diff:
```python
import functools

import jax
import jax.numpy as jnp
from jax import lax
from jax.experimental import pallas as pl
from jax.experimental.pallas import tpu as pltpu
from jax.sharding import PartitionSpec as P

NLON = 8192
SHARES = (1, 1)
LANES = 128
PARTS = 4
TILE = 512
ROWS = 256
SLOTS = 3
IN_ANY = pl.BlockSpec(memory_space=pl.ANY)
IN_VMEM = pl.BlockSpec(memory_space=pltpu.VMEM)


def stay(array):
    return pltpu.with_memory_space_constraint(array, pltpu.HBM)


def exchange(shard, axis, step):
    return lax.ppermute(shard, axis, [(i, i ^ step) for i in range(lax.axis_size(axis))])


def low_lanes(rows, width):
    return lax.broadcasted_iota(jnp.int32, (rows, width), 1) < width // 2


def split_halves(state):
    fields, width = state.shape[0] // 2, state.shape[1]
    real, imag = state[:fields], state[fields:]
    low = low_lanes(fields, width)
    first = jnp.where(low, real, pltpu.roll(imag, width // 2, 1))
    second = jnp.where(low, pltpu.roll(real, width // 2, 1), imag)
    return first.astype(jnp.bfloat16), second.astype(jnp.bfloat16)


def join_halves(first, second):
    fields, width = first.shape
    low = low_lanes(fields, width)
    first, second = first.astype(jnp.float32), second.astype(jnp.float32)
    real = jnp.where(low, first, pltpu.roll(second, width // 2, 1))
    imag = jnp.where(low, pltpu.roll(first, width // 2, 1), second)
    return jnp.concatenate([real, imag], 0).astype(jnp.bfloat16)


def dot(a, b):
    return jnp.dot(a, b, preferred_element_type=jnp.float32)


def upper_bit(level):
    return lax.axis_index("deg") >> level & 1


def put_halves(upper, state, own_ref, send_ref, g):
    first, second = split_halves(state)
    own_ref[g] = jnp.where(upper == 1, second, first)
    send_ref[g] = jnp.where(upper == 1, first, second)


def joined_state(upper, own_ref, came_ref, g):
    own, came = own_ref[g], came_ref[g]
    return join_halves(jnp.where(upper == 1, came, own), jnp.where(upper == 1, own, came))


def load_parts(source, target, sems):
    part = target.shape[0] // PARTS
    copies = []
    for n in range(PARTS):
        here = pl.ds(n * part, part)
        copies.append(pltpu.make_async_copy(source.at[here], target.at[here], sems.at[n]))
        copies[-1].start()
    return copies


def start_fetches(places, sources, targets, sems):
    copies = []
    for n, (place, source, target) in enumerate(zip(places, sources, targets)):
        copies.append(pltpu.make_async_copy(source.at[place], target, sems.at[n]))
        copies[-1].start()
    return copies


def leaf_kernel(places, *refs):
    fetches = len(places)
    coef, maps, skel, _, *sources = refs[: 4 + fetches]
    own_ref, send_ref, *targets = refs[4 + fetches : 6 + 2 * fetches]
    count, _, width = own_ref.shape
    degrees = maps.shape[1]
    scratch = refs[6 + 2 * fetches :]
    parts = []
    if len(scratch) > 1:
        coef_hbm, map_hbm, skel_hbm = coef, maps, skel
        coef, maps, skel, sems = scratch[:4]
        skel_copy = pltpu.make_async_copy(skel_hbm.at[pl.ds(0, count)], skel, sems.at[2, 0])
        skel_copy.start()
        parts = [load_parts(map_hbm, maps, sems.at[0]), load_parts(coef_hbm, coef, sems.at[1])]
    later = start_fetches(places, sources, targets, scratch[-1])
    if parts:
        skel_copy.wait()
    rows = lax.broadcasted_iota(jnp.int32, (degrees, width), 0)
    for g in range(count):
        for copies in parts:
            if g % (count // PARTS) == 0:
                copies[g // (count // PARTS)].wait()
        picks = (rows == skel[g : g + 1, :]).astype(jnp.bfloat16)
        both = dot(coef[g], jnp.concatenate([maps[g], picks], 1))
        put_halves(upper_bit(0), both[:, :width] + both[:, width:], own_ref, send_ref, g)
    for copy in later:
        copy.wait()


def level_kernel(first, num, places, *refs):
    fetches = len(places)
    own_in, came_in, maps, _, *sources = refs[: 4 + fetches]
    own_ref, send_ref, *targets = refs[4 + fetches : 6 + 2 * fetches]
    later = start_fetches(places, sources, targets, refs[-1]) if fetches else []
    for g in range(own_in.shape[0]):
        joined = joined_state(upper_bit(num), own_in, came_in, g)
        put_halves(upper_bit(num + 1), dot(joined, maps[first + g]), own_ref, send_ref, g)
    for copy in later:
        copy.wait()


def last_kernel(first, num, own_in, came_in, maps, lats, _, *refs):
    out_refs, block_ref = refs[:-1], refs[-1]
    count, fields = own_in.shape[:2]
    peers = len(out_refs)
    share = fields // peers
    for g in range(count):
        joined = joined_state(upper_bit(num), own_in, came_in, g)
        node = dot(joined, maps[first + g]).astype(jnp.bfloat16)
        block_ref[g] = dot(node, lats[first + g]).astype(jnp.bfloat16)
    tile = 16
    size = tile * tile
    out_at = lax.broadcasted_iota(jnp.int32, (size, size), 0)
    in_at = lax.broadcasted_iota(jnp.int32, (size, size), 1)
    swap = ((out_at // tile == in_at % tile) & (out_at % tile == in_at // tile)).astype(jnp.bfloat16)
    rows = block_ref.shape[2]
    me = lax.axis_index("wave")
    for g in range(0, count, tile):
        for c in range(0, 2 * fields, tile):
            moved = dot(swap, block_ref[g : g + tile, c : c + tile, :].reshape(size, rows)).astype(jnp.bfloat16)
            moved = moved.reshape(tile, tile, rows)
            part, field = c // fields, c % fields
            for at in range(0, tile, share):
                peer = (field + at) // share
                for step in range(peers):

                    @pl.when((me ^ peer) == step)
                    def _():
                        out_refs[step][:, part, g : g + tile, :] = moved[at : at + share]


def table_kernel(lon_count, slots, sizes, map_ref, after_ref, table_ref, q_ref):
    me = lax.axis_index("wave")
    row = 0
    for n, size in enumerate(sizes):
        for step in range(map_ref.shape[0] // slots):
            start = (me ^ step) * slots + sum(sizes[:n])

            def put(m, carry, row=row, start=start):
                q_ref[pl.ds(row + m, 1), :] = jnp.full((1, LANES), map_ref[start + m], jnp.int32)
                return carry

            lax.fori_loop(0, size, put, 0, unroll=8)
            row += size
    scale = 2.0 * jnp.pi / lon_count
    lane = lax.broadcasted_iota(jnp.int32, (16, LANES), 1)

    def rows(i, carry):
        here = pl.ds(pl.multiple_of(i * 16, 16), 16)
        q = q_ref[here, :]
        low = (q * lane % lon_count).astype(jnp.float32) * scale
        high = (q * (lane * LANES) % lon_count).astype(jnp.float32) * scale
        weight = jnp.where(q == 0, 1.0, 2.0).astype(jnp.float32)
        cl, sl = jnp.cos(low) * weight, jnp.sin(low) * -weight
        ch, sh = jnp.cos(high), jnp.sin(high)
        for h in range(table_ref.shape[2] // LANES):
            c, s = ch[:, h : h + 1], sh[:, h : h + 1]
            table_ref[0, here, h * LANES : (h + 1) * LANES] = (c * cl + s * sl).astype(jnp.bfloat16)
            table_ref[1, here, h * LANES : (h + 1) * LANES] = (c * sl - s * cl).astype(jnp.bfloat16)
        return carry

    lax.fori_loop(0, q_ref.shape[0] // 16, rows, 0)


def wave_table(wavemap, slots, sizes, lon_count, after):
    total = wavemap.shape[0]
    return pl.pallas_call(
        functools.partial(table_kernel, lon_count, slots, sizes),
        in_specs=[pl.BlockSpec(memory_space=pltpu.SMEM), IN_ANY],
        out_specs=IN_VMEM,
        out_shape=jax.ShapeDtypeStruct((2, total, lon_count // 2 + LANES), jnp.bfloat16),
        scratch_shapes=[pltpu.VMEM((total, LANES), jnp.int32)],
        cost_estimate=pl.CostEstimate(
            flops=8 * total * lon_count, bytes_accessed=8 * total * lon_count, transcendentals=0
        ),
        compiler_params=pltpu.CompilerParams(vmem_limit_bytes=16 * 2**20),
        name="table",
    )(wavemap, after)


def synthesis_kernel(*refs):
    block_refs = refs[:-6]
    table_ref, out_ref, left_ref, carry_ref, buffer_ref, sems = refs[-6:]
    fields, rows, lon_count = out_ref.shape
    slots, width = buffer_ref.shape[0], buffer_ref.shape[-1]
    for f in range(fields):
        for p in range(2):
            left_ref[p, f * rows : (f + 1) * rows, :] = jnp.concatenate([ref[f, p] for ref in block_refs], 0).T
    middle = pl.ds(lon_count // 2, LANES)
    carry_ref[...] = dot(left_ref[0], table_ref[0, :, middle]) - dot(left_ref[1], table_ref[1, :, middle])
    tiles = lon_count // width
    steps = tiles // 2
    size = ROWS
    lane = lax.broadcasted_iota(jnp.int32, (size, LANES), 1)
    mirror = (LANES - lane) % LANES

    def copies(i):
        slot, at = i % slots, steps - 1 - i
        straight = pl.ds(pl.multiple_of(at * width, width), width)
        turned = pl.ds(pl.multiple_of((tiles - 1 - at) * width, width), width)
        return (
            pltpu.make_async_copy(buffer_ref.at[slot, 0], out_ref.at[:, :, straight], sems.at[slot, 0]),
            pltpu.make_async_copy(buffer_ref.at[slot, 1], out_ref.at[:, :, turned], sems.at[slot, 1]),
        )

    def step(i, carry):
        slot, at = i % slots, steps - 1 - i
        straight = pl.ds(pl.multiple_of(at * width, width), width)

        @pl.when(i >= slots)
        def _():
            for copy in copies(i - slots):
                copy.wait()

        for r in range(0, fields * rows, size):
            f = r // rows
            n = size // rows
            cos_sum = dot(left_ref[0, r : r + size, :], table_ref[0, :, straight])
            sin_sum = dot(left_ref[1, r : r + size, :], table_ref[1, :, straight])
            buffer_ref[slot, 0, f : f + n] = (cos_sum + sin_sum).astype(jnp.bfloat16).reshape(n, rows, width)
            back = cos_sum - sin_sum
            following = carry_ref[r : r + size, :]
            for t in reversed(range(width // LANES)):
                piece = back[:, t * LANES : (t + 1) * LANES]
                turned = jnp.take_along_axis(piece, mirror, axis=1, mode="promise_in_bounds")
                turned = jnp.where(lane == 0, following, turned).astype(jnp.bfloat16)
                to = width - (t + 1) * LANES
                buffer_ref[slot, 1, f : f + n, :, to : to + LANES] = turned.reshape(n, rows, LANES)
                following = piece
            carry_ref[r : r + size, :] = following
        for copy in copies(i):
            copy.start()
        return carry

    lax.fori_loop(0, steps, step, 0)
    for i in range(max(0, steps - slots), steps):
        for copy in copies(i):
            copy.wait()


def synthesis(blocks, table, lon_count):
    fields, _, _, rows = blocks[0].shape
    depth = table.shape[1]
    return pl.pallas_call(
        synthesis_kernel,
        in_specs=[IN_VMEM] * (len(blocks) + 1),
        out_specs=pl.BlockSpec(memory_space=pl.ANY),
        out_shape=jax.ShapeDtypeStruct((fields, rows, lon_count), jnp.bfloat16),
        scratch_shapes=[
            pltpu.VMEM((2, fields * rows, depth), jnp.bfloat16),
            pltpu.VMEM((fields * rows, LANES), jnp.float32),
            pltpu.VMEM((SLOTS, 2, fields, rows, TILE), jnp.bfloat16),
            pltpu.SemaphoreType.DMA((SLOTS, 2)),
        ],
        cost_estimate=pl.CostEstimate(
            flops=2 * fields * rows * depth * lon_count,
            bytes_accessed=2 * lon_count * (fields * rows + depth),
            transcendentals=0,
        ),
        compiler_params=pltpu.CompilerParams(vmem_limit_bytes=32 * 2**20),
        name="synthesis",
    )(*blocks, table)


def body(spectrum, leaf_map, level_maps, lat_map, skeleton, wavemap):
    slots, _, fields, degrees = spectrum.shape
    columns = 2 * fields
    width = leaf_map.shape[2]
    levels = level_maps.shape[0]
    rows = lat_map.shape[2]
    coef = spectrum.reshape(slots, columns, degrees)
    peers = lax.axis_size("wave")
    sizes = [slots * share // sum(SHARES) for share in SHARES]
    firsts = [sum(sizes[:n]) for n in range(len(sizes))]
    chunks = range(len(sizes))
    params = pltpu.CompilerParams(vmem_limit_bytes=16 * 2**20)

    def half(chunk):
        return jax.ShapeDtypeStruct((sizes[chunk], fields, width), jnp.bfloat16)

    def fetched(fetches):
        shapes = []
        for array, place in fetches:
            view = jax.eval_shape(lambda a, place=place: a[place], array)
            shapes.append(jax.ShapeDtypeStruct(view.shape, view.dtype))
        sems = [pltpu.SemaphoreType.DMA((len(fetches),))] if fetches else []
        return [stay(array) for array, _ in fetches], [at(place) for _, place in fetches], shapes, sems

    def at(place):
        return pl.ds(place.start, place.stop - place.start) if isinstance(place, slice) else place

    def leaf(chunk, inputs, after, fetches):
        count = sizes[chunk]
        sources, places, shapes, sems = fetched(fetches)
        scratch = [] if chunk else [
            pltpu.VMEM((count, columns, degrees), jnp.bfloat16),
            pltpu.VMEM((count, degrees, width), jnp.bfloat16),
            pltpu.VMEM((count, width), jnp.int32),
            pltpu.SemaphoreType.DMA((3, PARTS)),
        ]
        return pl.pallas_call(
            functools.partial(leaf_kernel, places),
            in_specs=[IN_VMEM if chunk else IN_ANY] * 3 + [IN_ANY] * (1 + len(fetches)),
            out_specs=[IN_VMEM] * (2 + len(fetches)),
            out_shape=[half(chunk)] * 2 + shapes,
            scratch_shapes=scratch + sems,
            cost_estimate=pl.CostEstimate(
                flops=4 * count * columns * degrees * width,
                bytes_accessed=2 * count * degrees * (columns + width),
                transcendentals=0,
            ),
            compiler_params=params,
            name="leaf",
        )(*inputs, after, *sources)

    def level(chunk, num, own, came, maps, after, fetches):
        count = sizes[chunk]
        sources, places, shapes, sems = fetched(fetches)
        return pl.pallas_call(
            functools.partial(level_kernel, firsts[chunk], num, places),
            in_specs=[IN_VMEM] * 3 + [IN_ANY] * (1 + len(fetches)),
            out_specs=[IN_VMEM] * (2 + len(fetches)),
            out_shape=[half(chunk)] * 2 + shapes,
            scratch_shapes=sems,
            cost_estimate=pl.CostEstimate(
                flops=2 * count * columns * width * width,
                bytes_accessed=2 * count * width * (width + 2 * columns),
                transcendentals=0,
            ),
            compiler_params=params,
            name="level",
        )(own, came, maps, after, *sources)

    def last(chunk, own, came, maps, lats, after):
        count = sizes[chunk]
        piece = jax.ShapeDtypeStruct((fields // peers, 2, count, rows), jnp.bfloat16)
        return pl.pallas_call(
            functools.partial(last_kernel, firsts[chunk], levels - 1),
            in_specs=[IN_VMEM] * 4 + [IN_ANY],
            out_specs=[IN_VMEM] * peers,
            out_shape=[piece] * peers,
            scratch_shapes=[pltpu.VMEM((count, columns, rows), jnp.bfloat16)],
            cost_estimate=pl.CostEstimate(
                flops=2 * count * columns * width * (width + rows),
                bytes_accessed=2 * count * width * (width + rows + 2 * columns),
                transcendentals=0,
            ),
            compiler_params=params,
            name="last",
        )(own, came, maps, lats, after)

    whole = [coef, leaf_map, skeleton]
    state, before, inputs = [], stay(skeleton), [stay(array) for array in whole]
    for chunk in chunks:
        if chunk + 1 < len(sizes):
            ahead = slice(firsts[chunk + 1], firsts[chunk + 1] + sizes[chunk + 1])
            fetches = [(array, ahead) for array in whole]
        else:
            fetches = [(level_maps, 0)]
        before, send, *inputs = leaf(chunk, inputs, before, fetches)
        state.append((before, exchange(send, "deg", 1)))
    maps = {0: inputs[0]}
    wanted = [(level_maps, num) for num in range(1, levels)] + [(lat_map, slice(0, slots))]
    for num in range(levels - 1):
        for chunk in chunks:
            fetches = [wanted[len(maps) - 1]] if len(maps) <= len(wanted) else []
            before, send, *more = level(chunk, num, *state[chunk], maps[num], before, fetches)
            maps.update({len(maps): array for array in more})
            state[chunk] = before, exchange(send, "deg", 2 << num)
    before = table = wave_table(wavemap, slots, sizes, NLON, before)
    blocks = []
    for chunk in chunks:
        pieces = last(chunk, *state[chunk], maps[levels - 1], maps[levels], before)
        before = pieces[0]
        blocks += [p if step == 0 else exchange(p, "wave", step) for step, p in enumerate(pieces)]
    return synthesis(blocks, table, NLON)


def solution(mesh):
    placed = (
        P("wave", None, None, "deg"),
        P("wave", "deg", None),
        P(None, "wave", "deg", None),
        P("wave", None, "deg"),
        P("wave", "deg"),
        P(),
    )
    return jax.shard_map(
        body, mesh=mesh, in_specs=placed, out_specs=P("wave", "deg", None), check_vma=False
    )
```

time: 120 us -> 69.1 us (0.58)
  matrix products: 36.4 us -> 0 us
  local copies, waits for them, and re-layouts: 34 us -> 0.01 us
  Pallas kernels: 0 us -> 30 us
  other arithmetic: 8.13 us -> 0 us
  waiting for transfers between devices: 29.1 us -> 23.7 us
  starting transfers between devices: 11.1 us -> 15.1 us
    dot_general x9 -> x0, matrix products: 36.4 us -> none  [the longest x1 15.1 us: body(): jnp.einsum('mrfl,rmn->fln', gathered, table, preferred_element_type=jnp.f...]
    pallas_call x0 -> x10, Pallas kernels: none -> 30 us  [the longest x1 8.69 us: synthesis(): pl.pallas_call(synthesis_kernel, in_specs=[IN_VMEM] * (len(blocks) + 1),...]
    ppermute x3 -> x12, starting transfers between devices: 7.38 us -> 15.1 us  [exchange(): lax.ppermute(shard, axis, [(i, i ^ step) for i in range(lax.axis_size(axi...]
    slice x1 -> x0, local copies, waits for them, and re-layouts: 7.53 us -> none  [body(): factor = level_maps[level_num]]
    sub x1 -> x0, local copies, waits for them, and re-layouts: 7.35 us -> none  [wave_table(): cos_high * cos_low - sin_high * sin_low]
    neg x1 -> x0, local copies, waits for them, and re-layouts: 7.31 us -> none  [wave_table(): return jnp.stack([cos_all, -sin_all]).astype(jnp.bfloat16)]
    another operation x1 -> x0, other arithmetic: 6.94 us -> none
    reshape x7 -> x0, local copies, waits for them, and re-layouts: 6.86 us -> none  [the longest x3 2.46 us: body(): arrived = partner(packed, 'deg', level_num).reshape(payload.shape)]
  transfers between devices with their start and end apart: 4 -> 12, of which waited for: 3 -> 9; matrix products, arithmetic and copies ran while one was open for 32% -> 0% of each run, Pallas kernels for 0% -> 26%
where the time goes in v3:
time: 69.1 us; the launch traced here: 68.9 us
  Pallas kernels  30 us (43%)
  waiting for transfers between devices  23.7 us (34%)
  starting transfers between devices  15.1 us (22%)
    ppermute x12, waiting for transfers between devices, exchange(): lax.ppermute(shard, axis, [(i, i ^ step) for i in range(lax.axis_size(axi...  23.7 us
    ppermute x12, starting transfers between devices, exchange(): lax.ppermute(shard, axis, [(i, i ^ step) for i in range(lax.axis_size(axi...  15.1 us
    pallas_call x1, Pallas kernels, synthesis(): pl.pallas_call(synthesis_kernel, in_specs=[IN_VMEM] * (len(blocks) + 1),...  8.69 us
    pallas_call x1, Pallas kernels, wave_table(): pl.pallas_call(functools.partial(table_kernel, lon_count, slots, sizes),...  5.96 us
    pallas_call x4, Pallas kernels, level(): pl.pallas_call(functools.partial(level_kernel, firsts[chunk], num, places...  5.73 us
    pallas_call x2, Pallas kernels, leaf(): pl.pallas_call(functools.partial(leaf_kernel, places), in_specs=[IN_VMEM...  4.88 us
    pallas_call x2, Pallas kernels, last(): pl.pallas_call(functools.partial(last_kernel, firsts[chunk], levels - 1),...  4.78 us
  transfers between devices with their start and end apart: 12, of which 9 were waited for; matrix products, arithmetic and copies ran while one was open for 0% of the time, Pallas kernels for 26%

profile of v3, /device:TPU:0, one launch (start us, length us, event | category | flops | bytes accessed | tf_op | source)
XLA Modules:
  0.0 68.9 jit_solution(8383126439941819545)
XLA Ops:
  0.0 3.3 %leaf.2 = (bf16[32,32,128]{2,1,0:T(8,128)(2,1)S(1)}, bf16[32,32,128]{2,1,0:T(8,128)(2,1)S(1)}, bf16[32,64,256]{2,1,0:T(8,128)(2,1)S(1)}, bf16[32,256,128]{2,1,0:T(8,128)(2,1)S(1)}, s32[32,128]{1,0:T(8,128)S(1)}) custom-call(bf16[64,64,256]{2,1,0:T(8,128)(2,1)} %bitcast.1, bf16[64,256,128]{2,1,0:T(8,128)(2,1)} %refs_5_.1, s32[64,128]{1,0:T(8,128)} %refs_6_.1, ...), custom_call_target="tpu_custom_call" | custom-call | flops 268435456 | bytes 3145728 | tf_op jit(solution)/shard_map/leaf/pallas_call | solution.py:328
  3.3 3.0 %collective-permute-start = (bf16[32,32,128]{2,1,0:T(8,128)(2,1)S(1)}, bf16[32,32,128]{2,1,0:T(8,128)(2,1)S(1)}, u32[]{:S(2)}, u32[]{:S(2)}) collective-permute-start(bf16[32,32,128]{2,1,0:T(8,128)(2,1)S(1)} %get-tuple-element.33), channel_id=1, source_target_pairs={{0,1},{1,0},{2,3},{3,2},{4,5},{5,4},{6,7},{7,6},{8,9},{9,8},{10,11... | collective-permute-start | bytes 786440 | tf_op jit(solution)/shard_map/ppermute | solution.py:26
  6.3 1.6 %leaf.3 = (bf16[32,32,128]{2,1,0:T(8,128)(2,1)S(1)}, bf16[32,32,128]{2,1,0:T(8,128)(2,1)S(1)}, bf16[64,128,128]{2,1,0:T(8,128)(2,1)S(1)}) custom-call(bf16[32,64,256]{2,1,0:T(8,128)(2,1)S(1)} %get-tuple-element.34.refs_0_, bf16[32,256,128]{2,1,0:T(8,128)(2,1)S(1)} %get-tuple-element.35.refs_1_, s32[32,128]{1,0:T(8,128)S(1)} %get-tuple-element.36.refs_2_, ...), custom_call_target="tpu_custom_call" | custom-call | flops 268435456 | bytes 3145728 | tf_op jit(solution)/shard_map/leaf/pallas_call | solution.py:328
  7.9 0.1 collective-permute-start.2
  8.0 5.4 %collective-permute-done.refs_1_ = bf16[32,32,128]{2,1,0:T(8,128)(2,1)S(1)} collective-permute-done((bf16[32,32,128]{2,1,0:T(8,128)(2,1)S(1)}, bf16[32,32,128]{2,1,0:T(8,128)(2,1)S(1)}, u32[]{:S(2)}, u32[]{:S(2)}) %collective-permute-start) | collective-permute-done | bytes 262176 | tf_op jit(solution)/shard_map/ppermute | solution.py:26
  13.4 1.6 %level.4 = (bf16[32,32,128]{2,1,0:T(8,128)(2,1)S(1)}, bf16[32,32,128]{2,1,0:T(8,128)(2,1)S(1)}, bf16[64,128,128]{2,1,0:T(8,128)(2,1)S(1)}) custom-call(bf16[32,32,128]{2,1,0:T(8,128)(2,1)S(1)} %get-tuple-element.32.refs_3_.refs_0_, bf16[32,32,128]{2,1,0:T(8,128)(2,1)S(1)} %collective-permute-done.refs_1_, ...), custom_call_target="tpu_custom_call" | custom-call | flops 67108864 | bytes 2097152 | tf_op jit(solution)/shard_map/level/pallas_call | solution.py:346
  15.1 2.2 %collective-permute-start.1 = (bf16[32,32,128]{2,1,0:T(8,128)(2,1)S(1)}, bf16[32,32,128]{2,1,0:T(8,128)(2,1)S(1)}, u32[]{:S(2)}, u32[]{:S(2)}) collective-permute-start(bf16[32,32,128]{2,1,0:T(8,128)(2,1)S(1)} %get-tuple-element.40), channel_id=1, source_target_pairs={{0,2},{1,3},{2,0},{3,1},{4,6},{5,7},{6,4},{7,5},{8,10},{9,11},{10,... | collective-permute-start | bytes 786440 | tf_op jit(solution)/shard_map/ppermute | solution.py:26
  17.2 1.0 %collective-permute-done.2.refs_1_ = bf16[32,32,128]{2,1,0:T(8,128)(2,1)S(1)} collective-permute-done((bf16[32,32,128]{2,1,0:T(8,128)(2,1)S(1)}, bf16[32,32,128]{2,1,0:T(8,128)(2,1)S(1)}, u32[]{:S(2)}, u32[]{:S(2)}) %collective-permute-start.2) | collective-permute-done | bytes 262176 | tf_op jit(solution)/shard_map/ppermute | solution.py:26
  18.2 1.6 %level.5 = (bf16[32,32,128]{2,1,0:T(8,128)(2,1)S(1)}, bf16[32,32,128]{2,1,0:T(8,128)(2,1)S(1)}, bf16[64,128,128]{2,1,0:T(8,128)(2,1)S(1)}) custom-call(bf16[32,32,128]{2,1,0:T(8,128)(2,1)S(1)} %get-tuple-element.38.refs_3_.refs_0_, bf16[32,32,128]{2,1,0:T(8,128)(2,1)S(1)} %collective-permute-done.2.refs_1_, ...), custom_call_target="tpu_custom_call" | custom-call | flops 67108864 | bytes 2097152 | tf_op jit(solution)/shard_map/level/pallas_call | solution.py:346
  19.9 1.9 %collective-permute-start.4 = (bf16[32,32,128]{2,1,0:T(8,128)(2,1)S(1)}, bf16[32,32,128]{2,1,0:T(8,128)(2,1)S(1)}, u32[]{:S(2)}, u32[]{:S(2)}) collective-permute-start(bf16[32,32,128]{2,1,0:T(8,128)(2,1)S(1)} %get-tuple-element.48), channel_id=1, source_target_pairs={{0,2},{1,3},{2,0},{3,1},{4,6},{5,7},{6,4},{7,5},{8,10},{9,11},{10,... | collective-permute-start | bytes 786440 | tf_op jit(solution)/shard_map/ppermute | solution.py:26
  21.7 0.1 collective-permute-done.1.refs_1_
  21.8 1.6 %level.6 = (bf16[32,32,128]{2,1,0:T(8,128)(2,1)S(1)}, bf16[32,32,128]{2,1,0:T(8,128)(2,1)S(1)}, bf16[64,128,128]{2,1,0:T(8,128)(2,1)S(1)}) custom-call(bf16[32,32,128]{2,1,0:T(8,128)(2,1)S(1)} %get-tuple-element.39.refs_3_.refs_0_, bf16[32,32,128]{2,1,0:T(8,128)(2,1)S(1)} %collective-permute-done.1.refs_1_, ...), custom_call_target="tpu_custom_call" | custom-call | flops 67108864 | bytes 2097152 | tf_op jit(solution)/shard_map/level/pallas_call | solution.py:346
  23.4 0.0 copy-start
  23.4 3.2 %collective-permute-start.3 = (bf16[32,32,128]{2,1,0:T(8,128)(2,1)S(1)}, bf16[32,32,128]{2,1,0:T(8,128)(2,1)S(1)}, u32[]{:S(2)}, u32[]{:S(2)}) collective-permute-start(bf16[32,32,128]{2,1,0:T(8,128)(2,1)S(1)} %get-tuple-element.45), channel_id=1, source_target_pairs={{0,4},{1,5},{2,6},{3,7},{4,0},{5,1},{6,2},{7,3},{8,12},{9,13},{10,... | collective-permute-start | bytes 786440 | tf_op jit(solution)/shard_map/ppermute | solution.py:26
  26.6 5.0 %collective-permute-done.4.refs_1_ = bf16[32,32,128]{2,1,0:T(8,128)(2,1)S(1)} collective-permute-done((bf16[32,32,128]{2,1,0:T(8,128)(2,1)S(1)}, bf16[32,32,128]{2,1,0:T(8,128)(2,1)S(1)}, u32[]{:S(2)}, u32[]{:S(2)}) %collective-permute-start.4) | collective-permute-done | bytes 262176 | tf_op jit(solution)/shard_map/ppermute | solution.py:26
  31.6 0.9 %level.7 = (bf16[32,32,128]{2,1,0:T(8,128)(2,1)S(1)}, bf16[32,32,128]{2,1,0:T(8,128)(2,1)S(1)}) custom-call(bf16[32,32,128]{2,1,0:T(8,128)(2,1)S(1)} %get-tuple-element.43.refs_3_.refs_0_, bf16[32,32,128]{2,1,0:T(8,128)(2,1)S(1)} %collective-permute-done.4.refs_1_, bf16[64,128,128]{2,1,0:T(8,128)(2,1)S(1)} %get-tuple-element.41.refs_2_, ...), custom_call_target="tpu_custom_call" | custom-call | flops 67108864 | bytes 2097152 | tf_op jit(solution)/shard_map/level/pallas_call | solution.py:346
  32.5 0.9 %collective-permute-start.8 = (bf16[32,32,128]{2,1,0:T(8,128)(2,1)S(1)}, bf16[32,32,128]{2,1,0:T(8,128)(2,1)S(1)}, u32[]{:S(2)}, u32[]{:S(2)}) collective-permute-start(bf16[32,32,128]{2,1,0:T(8,128)(2,1)S(1)} %get-tuple-element.54), channel_id=1, source_target_pairs={{0,4},{1,5},{2,6},{3,7},{4,0},{5,1},{6,2},{7,3},{8,12},{9,13},{10,... | collective-permute-start | bytes 786440 | tf_op jit(solution)/shard_map/ppermute | solution.py:26
  33.4 0.0 copy-done
  33.4 6.0 %table.1._.refs_8_ = bf16[2,256,4224]{2,1,0:T(8,128)(2,1)S(1)} custom-call(s32[256]{0:T(256)S(1)} %copy-done, bf16[32,32,128]{2,1,0:T(8,128)(2,1)S(1)} %get-tuple-element.49.after_ref.own_in), custom_call_target="tpu_custom_call" | custom-call | flops 16777216 | bytes 16777216 | tf_op jit(solution)/shard_map/table/pallas_call | solution.py:194
  39.3 4.5 %collective-permute-done.3.came_in = bf16[32,32,128]{2,1,0:T(8,128)(2,1)S(1)} collective-permute-done((bf16[32,32,128]{2,1,0:T(8,128)(2,1)S(1)}, bf16[32,32,128]{2,1,0:T(8,128)(2,1)S(1)}, u32[]{:S(2)}, u32[]{:S(2)}) %collective-permute-start.3) | collective-permute-done | bytes 262176 | tf_op jit(solution)/shard_map/ppermute | solution.py:26
  43.9 2.4 %last.2 = (bf16[8,2,32,128]{3,2,1,0:T(8,128)(2,1)S(1)}, bf16[8,2,32,128]{3,2,1,0:T(8,128)(2,1)S(1)}, bf16[8,2,32,128]{3,2,1,0:T(8,128)(2,1)S(1)}, bf16[8,2,32,128]{3,2,1,0:T(8,128)(2,1)S(1)}) custom-call(bf16[32,32,128]{2,1,0:T(8,128)(2,1)S(1)} %get-tuple-element.44.refs_3_.own_in, bf16[32,32,128]{2,1,0:T(8,128)(2,1)S(1)} %collective-permute-done.3.came_in, ...), custom_call_target="tpu_custom_call" | custom-call | flops 134217728 | bytes 3145728 | tf_op jit(solution)/shard_map/last/pallas_call | solution.py:364
  46.2 0.1 collective-permute-start.5
  46.3 1.6 %collective-permute-start.6 = (bf16[8,2,32,128]{3,2,1,0:T(8,128)(2,1)S(1)}, bf16[8,2,32,128]{3,2,1,0:T(8,128)(2,1)S(1)}, u32[]{:S(2)}, u32[]{:S(2)}) collective-permute-start(bf16[8,2,32,128]{3,2,1,0:T(8,128)(2,1)S(1)} %get-tuple-element.52), channel_id=1, source_target_pairs={{0,16},{8,24},{16,0},{24,8},{1,17},{9,25},{17,1},{25,9},{2,18},{10... | collective-permute-start | bytes 393224 | tf_op jit(solution)/shard_map/ppermute | solution.py:26
  47.9 0.3 collective-permute-start.7
  48.2 0.0 collective-permute-done.8.came_in
  48.2 2.4 %last.3 = (bf16[8,2,32,128]{3,2,1,0:T(8,128)(2,1)S(1)}, bf16[8,2,32,128]{3,2,1,0:T(8,128)(2,1)S(1)}, bf16[8,2,32,128]{3,2,1,0:T(8,128)(2,1)S(1)}, bf16[8,2,32,128]{3,2,1,0:T(8,128)(2,1)S(1)}) custom-call(bf16[32,32,128]{2,1,0:T(8,128)(2,1)S(1)} %get-tuple-element.49.after_ref.own_in, bf16[32,32,128]{2,1,0:T(8,128)(2,1)S(1)} %collective-permute-done.8.came_in, ...), custom_call_target="tpu_custom_call" | custom-call | flops 134217728 | bytes 3145728 | tf_op jit(solution)/shard_map/last/pallas_call | solution.py:364
  50.6 0.4 collective-permute-start.9
  51.0 1.5 %collective-permute-start.10 = (bf16[8,2,32,128]{3,2,1,0:T(8,128)(2,1)S(1)}, bf16[8,2,32,128]{3,2,1,0:T(8,128)(2,1)S(1)}, u32[]{:S(2)}, u32[]{:S(2)}) collective-permute-start(bf16[8,2,32,128]{3,2,1,0:T(8,128)(2,1)S(1)} %get-tuple-element.57), channel_id=1, source_target_pairs={{0,16},{8,24},{16,0},{24,8},{1,17},{9,25},{17,1},{25,9},{2,18},{10... | collective-permute-start | bytes 393224 | tf_op jit(solution)/shard_map/ppermute | solution.py:26
  52.5 0.0 collective-permute-done.5.refs_1_
  52.5 0.0 collective-permute-start.11
  52.5 0.1 collective-permute-done.6.refs_2_
  52.7 1.9 %collective-permute-done.7.refs_3_ = bf16[8,2,32,128]{3,2,1,0:T(8,128)(2,1)S(1)} collective-permute-done((bf16[8,2,32,128]{3,2,1,0:T(8,128)(2,1)S(1)}, bf16[8,2,32,128]{3,2,1,0:T(8,128)(2,1)S(1)}, u32[]{:S(2)}, u32[]{:S(2)}) %collective-permute-start.7) | collective-permute-done | bytes 131104 | tf_op jit(solution)/shard_map/ppermute | solution.py:26
  54.6 0.0 collective-permute-done.9.refs_5_
  54.6 3.7 %collective-permute-done.10.refs_6_ = bf16[8,2,32,128]{3,2,1,0:T(8,128)(2,1)S(1)} collective-permute-done((bf16[8,2,32,128]{3,2,1,0:T(8,128)(2,1)S(1)}, bf16[8,2,32,128]{3,2,1,0:T(8,128)(2,1)S(1)}, u32[]{:S(2)}, u32[]{:S(2)}) %collective-permute-start.10) | collective-permute-done | bytes 131104 | tf_op jit(solution)/shard_map/ppermute | solution.py:26
  58.3 1.9 %collective-permute-done.11.refs_7_ = bf16[8,2,32,128]{3,2,1,0:T(8,128)(2,1)S(1)} collective-permute-done((bf16[8,2,32,128]{3,2,1,0:T(8,128)(2,1)S(1)}, bf16[8,2,32,128]{3,2,1,0:T(8,128)(2,1)S(1)}, u32[]{:S(2)}, u32[]{:S(2)}) %collective-permute-start.11) | collective-permute-done | bytes 131104 | tf_op jit(solution)/shard_map/ppermute | solution.py:26
  60.2 8.7 %synthesis.1 = bf16[8,128,8192]{2,1,0:T(8,128)(2,1)} custom-call(bf16[8,2,32,128]{3,2,1,0:T(8,128)(2,1)S(1)} %get-tuple-element.50._.refs_0_, bf16[8,2,32,128]{3,2,1,0:T(8,128)(2,1)S(1)} %collective-permute-done.5.refs_1_, bf16[8,2,32,128]{3,2,1,0:T(8,128)(2,1)S(1)} %collective-permute-done.6.refs_2_, ...), custom_call_target="tpu_custom_call" | custom-call | flops 4294967296 | bytes 20971520 | tf_op jit(solution)/shard_map/synthesis/pallas_call | solution.py:271
Async XLA Ops:
  3.3 10.2 %collective-permute-start = (bf16[32,32,128]{2,1,0:T(8,128)(2,1)S(1)}, bf16[32,32,128]{2,1,0:T(8,128)(2,1)S(1)}, u32[]{:S(2)}, u32[]{:S(2)}) collective-permute-start(bf16[32,32,128]{2,1,0:T(8,128)(2,1)S(1)} %get-tuple-element.33), channel_id=1, source_target_pairs={{0,1},{1,0},{2,3},{3,2},{4,5},{5,4},{6,7},{7,6},{8,9},{9,8},{10,11... | collective-permute-start | bytes 786440 | tf_op jit(solution)/shard_map/ppermute | solution.py:26
  7.9 10.3 %collective-permute-start.2 = (bf16[32,32,128]{2,1,0:T(8,128)(2,1)S(1)}, bf16[32,32,128]{2,1,0:T(8,128)(2,1)S(1)}, u32[]{:S(2)}, u32[]{:S(2)}) collective-permute-start(bf16[32,32,128]{2,1,0:T(8,128)(2,1)S(1)} %get-tuple-element.42), channel_id=1, source_target_pairs={{0,1},{1,0},{2,3},{3,2},{4,5},{5,4},{6,7},{7,6},{8,9},{9,8},{10,11... | collective-permute-start | bytes 786440 | tf_op jit(solution)/shard_map/ppermute | solution.py:26
  15.1 6.7 %collective-permute-start.1 = (bf16[32,32,128]{2,1,0:T(8,128)(2,1)S(1)}, bf16[32,32,128]{2,1,0:T(8,128)(2,1)S(1)}, u32[]{:S(2)}, u32[]{:S(2)}) collective-permute-start(bf16[32,32,128]{2,1,0:T(8,128)(2,1)S(1)} %get-tuple-element.40), channel_id=1, source_target_pairs={{0,2},{1,3},{2,0},{3,1},{4,6},{5,7},{6,4},{7,5},{8,10},{9,11},{10,... | collective-permute-start | bytes 786440 | tf_op jit(solution)/shard_map/ppermute | solution.py:26
  19.9 11.7 %collective-permute-start.4 = (bf16[32,32,128]{2,1,0:T(8,128)(2,1)S(1)}, bf16[32,32,128]{2,1,0:T(8,128)(2,1)S(1)}, u32[]{:S(2)}, u32[]{:S(2)}) collective-permute-start(bf16[32,32,128]{2,1,0:T(8,128)(2,1)S(1)} %get-tuple-element.48), channel_id=1, source_target_pairs={{0,2},{1,3},{2,0},{3,1},{4,6},{5,7},{6,4},{7,5},{8,10},{9,11},{10,... | collective-permute-start | bytes 786440 | tf_op jit(solution)/shard_map/ppermute | solution.py:26
  23.4 10.0 %copy-start = (s32[256]{0:T(256)S(1)}, s32[256]{0:T(256)}, u32[]{:S(2)}) copy-start(s32[256]{0:T(256)} %map_ref.1) | copy-start | bytes 3076
  23.4 20.4 %collective-permute-start.3 = (bf16[32,32,128]{2,1,0:T(8,128)(2,1)S(1)}, bf16[32,32,128]{2,1,0:T(8,128)(2,1)S(1)}, u32[]{:S(2)}, u32[]{:S(2)}) collective-permute-start(bf16[32,32,128]{2,1,0:T(8,128)(2,1)S(1)} %get-tuple-element.45), channel_id=1, source_target_pairs={{0,4},{1,5},{2,6},{3,7},{4,0},{5,1},{6,2},{7,3},{8,12},{9,13},{10,... | collective-permute-start | bytes 786440 | tf_op jit(solution)/shard_map/ppermute | solution.py:26
  32.5 15.7 %collective-permute-start.8 = (bf16[32,32,128]{2,1,0:T(8,128)(2,1)S(1)}, bf16[32,32,128]{2,1,0:T(8,128)(2,1)S(1)}, u32[]{:S(2)}, u32[]{:S(2)}) collective-permute-start(bf16[32,32,128]{2,1,0:T(8,128)(2,1)S(1)} %get-tuple-element.54), channel_id=1, source_target_pairs={{0,4},{1,5},{2,6},{3,7},{4,0},{5,1},{6,2},{7,3},{8,12},{9,13},{10,... | collective-permute-start | bytes 786440 | tf_op jit(solution)/shard_map/ppermute | solution.py:26
  46.2 6.3 %collective-permute-start.5 = (bf16[8,2,32,128]{3,2,1,0:T(8,128)(2,1)S(1)}, bf16[8,2,32,128]{3,2,1,0:T(8,128)(2,1)S(1)}, u32[]{:S(2)}, u32[]{:S(2)}) collective-permute-start(bf16[8,2,32,128]{3,2,1,0:T(8,128)(2,1)S(1)} %get-tuple-element.51), channel_id=1, source_target_pairs={{0,8},{8,0},{16,24},{24,16},{1,9},{9,1},{17,25},{25,17},{2,10},{10... | collective-permute-start | bytes 393224 | tf_op jit(solution)/shard_map/ppermute | solution.py:26
  46.3 6.4 %collective-permute-start.6 = (bf16[8,2,32,128]{3,2,1,0:T(8,128)(2,1)S(1)}, bf16[8,2,32,128]{3,2,1,0:T(8,128)(2,1)S(1)}, u32[]{:S(2)}, u32[]{:S(2)}) collective-permute-start(bf16[8,2,32,128]{3,2,1,0:T(8,128)(2,1)S(1)} %get-tuple-element.52), channel_id=1, source_target_pairs={{0,16},{8,24},{16,0},{24,8},{1,17},{9,25},{17,1},{25,9},{2,18},{10... | collective-permute-start | bytes 393224 | tf_op jit(solution)/shard_map/ppermute | solution.py:26
  47.9 6.7 %collective-permute-start.7 = (bf16[8,2,32,128]{3,2,1,0:T(8,128)(2,1)S(1)}, bf16[8,2,32,128]{3,2,1,0:T(8,128)(2,1)S(1)}, u32[]{:S(2)}, u32[]{:S(2)}) collective-permute-start(bf16[8,2,32,128]{3,2,1,0:T(8,128)(2,1)S(1)} %get-tuple-element.53), channel_id=1, source_target_pairs={{0,24},{8,16},{16,8},{24,0},{1,25},{9,17},{17,9},{25,1},{2,26},{10... | collective-permute-start | bytes 393224 | tf_op jit(solution)/shard_map/ppermute | solution.py:26
  50.6 4.0 %collective-permute-start.9 = (bf16[8,2,32,128]{3,2,1,0:T(8,128)(2,1)S(1)}, bf16[8,2,32,128]{3,2,1,0:T(8,128)(2,1)S(1)}, u32[]{:S(2)}, u32[]{:S(2)}) collective-permute-start(bf16[8,2,32,128]{3,2,1,0:T(8,128)(2,1)S(1)} %get-tuple-element.56), channel_id=1, source_target_pairs={{0,8},{8,0},{16,24},{24,16},{1,9},{9,1},{17,25},{25,17},{2,10},{10... | collective-permute-start | bytes 393224 | tf_op jit(solution)/shard_map/ppermute | solution.py:26
  51.0 7.3 %collective-permute-start.10 = (bf16[8,2,32,128]{3,2,1,0:T(8,128)(2,1)S(1)}, bf16[8,2,32,128]{3,2,1,0:T(8,128)(2,1)S(1)}, u32[]{:S(2)}, u32[]{:S(2)}) collective-permute-start(bf16[8,2,32,128]{3,2,1,0:T(8,128)(2,1)S(1)} %get-tuple-element.57), channel_id=1, source_target_pairs={{0,16},{8,24},{16,0},{24,8},{1,17},{9,25},{17,1},{25,9},{2,18},{10... | collective-permute-start | bytes 393224 | tf_op jit(solution)/shard_map/ppermute | solution.py:26
  52.5 7.7 %collective-permute-start.11 = (bf16[8,2,32,128]{3,2,1,0:T(8,128)(2,1)S(1)}, bf16[8,2,32,128]{3,2,1,0:T(8,128)(2,1)S(1)}, u32[]{:S(2)}, u32[]{:S(2)}) collective-permute-start(bf16[8,2,32,128]{3,2,1,0:T(8,128)(2,1)S(1)} %get-tuple-element.58), channel_id=1, source_target_pairs={{0,24},{8,16},{16,8},{24,0},{1,25},{9,17},{17,9},{25,1},{2,26},{10... | collective-permute-start | bytes 393224 | tf_op jit(solution)/shard_map/ppermute | solution.py:26

commit v4 on v3

--- a/solution.py
+++ b/solution.py
@@ -8,12 +8,18 @@
 from jax.sharding import PartitionSpec as P
 
 NLON = 8192
-SHARES = (1, 1)
+SHARES = (1, 1, 1, 1)
+GROUPS = ((0, 1), (2, 3))
+TURN = -1
+BLOCK = 64
+TABLE_STAGE = 2
+TABLE_CHUNK = 2
 LANES = 128
 PARTS = 4
 TILE = 512
 ROWS = 256
 SLOTS = 3
+CHEAP = pl.CostEstimate(flops=0, bytes_accessed=0, transcendentals=0)
 IN_ANY = pl.BlockSpec(memory_space=pl.ANY)
 IN_VMEM = pl.BlockSpec(memory_space=pltpu.VMEM)
 
@@ -93,13 +99,13 @@
     degrees = maps.shape[1]
     scratch = refs[6 + 2 * fetches :]
     parts = []
-    if len(scratch) > 1:
+    if len(scratch) > 3:
         coef_hbm, map_hbm, skel_hbm = coef, maps, skel
         coef, maps, skel, sems = scratch[:4]
         skel_copy = pltpu.make_async_copy(skel_hbm.at[pl.ds(0, count)], skel, sems.at[2, 0])
         skel_copy.start()
         parts = [load_parts(map_hbm, maps, sems.at[0]), load_parts(coef_hbm, coef, sems.at[1])]
-    later = start_fetches(places, sources, targets, scratch[-1])
+    later = start_fetches(places, sources, targets, scratch[-1]) if fetches else []
     if parts:
         skel_copy.wait()
     rows = lax.broadcasted_iota(jnp.int32, (degrees, width), 0)
@@ -121,19 +127,19 @@
     later = start_fetches(places, sources, targets, refs[-1]) if fetches else []
     for g in range(own_in.shape[0]):
         joined = joined_state(upper_bit(num), own_in, came_in, g)
-        put_halves(upper_bit(num + 1), dot(joined, maps[first + g]), own_ref, send_ref, g)
+        put_halves(upper_bit(num + 1), dot(joined, maps[num, first + g]), own_ref, send_ref, g)
     for copy in later:
         copy.wait()
 
 
-def last_kernel(first, num, own_in, came_in, maps, lats, _, *refs):
-    out_refs, block_ref = refs[:-1], refs[-1]
+def last_kernel(first, num, offset, own_in, came_in, maps, lats, _, *refs):
+    peers = lax.axis_size("wave")
+    out_refs, block_ref = refs[-1 - peers : -1], refs[-1]
     count, fields = own_in.shape[:2]
-    peers = len(out_refs)
     share = fields // peers
     for g in range(count):
         joined = joined_state(upper_bit(num), own_in, came_in, g)
-        node = dot(joined, maps[first + g]).astype(jnp.bfloat16)
+        node = dot(joined, maps[num, first + g]).astype(jnp.bfloat16)
         block_ref[g] = dot(node, lats[first + g]).astype(jnp.bfloat16)
     tile = 16
     size = tile * tile
@@ -153,7 +159,7 @@
 
                     @pl.when((me ^ peer) == step)
                     def _():
-                        out_refs[step][:, part, g : g + tile, :] = moved[at : at + share]
+                        out_refs[step][:, part, offset + g : offset + g + tile, :] = moved[at : at + share]
 
 
 def table_kernel(lon_count, slots, sizes, map_ref, after_ref, table_ref, q_ref):
@@ -170,13 +176,13 @@
             lax.fori_loop(0, size, put, 0, unroll=8)
             row += size
     scale = 2.0 * jnp.pi / lon_count
-    lane = lax.broadcasted_iota(jnp.int32, (16, LANES), 1)
+    lane = lax.broadcasted_iota(jnp.int32, (BLOCK, LANES), 1)
 
     def rows(i, carry):
-        here = pl.ds(pl.multiple_of(i * 16, 16), 16)
+        here = pl.ds(pl.multiple_of(i * BLOCK, BLOCK), BLOCK)
         q = q_ref[here, :]
-        low = (q * lane % lon_count).astype(jnp.float32) * scale
-        high = (q * (lane * LANES) % lon_count).astype(jnp.float32) * scale
+        low = (q * lane & lon_count - 1).astype(jnp.float32) * scale
+        high = (q * (lane * LANES) & lon_count - 1).astype(jnp.float32) * scale
         weight = jnp.where(q == 0, 1.0, 2.0).astype(jnp.float32)
         cl, sl = jnp.cos(low) * weight, jnp.sin(low) * -weight
         ch, sh = jnp.cos(high), jnp.sin(high)
@@ -186,7 +192,7 @@
             table_ref[1, here, h * LANES : (h + 1) * LANES] = (c * sl - s * cl).astype(jnp.bfloat16)
         return carry
 
-    lax.fori_loop(0, q_ref.shape[0] // 16, rows, 0)
+    lax.fori_loop(0, q_ref.shape[0] // BLOCK, rows, 0)
 
 
 def wave_table(wavemap, slots, sizes, lon_count, after):
@@ -197,9 +203,7 @@
         out_specs=IN_VMEM,
         out_shape=jax.ShapeDtypeStruct((2, total, lon_count // 2 + LANES), jnp.bfloat16),
         scratch_shapes=[pltpu.VMEM((total, LANES), jnp.int32)],
-        cost_estimate=pl.CostEstimate(
-            flops=8 * total * lon_count, bytes_accessed=8 * total * lon_count, transcendentals=0
-        ),
+        cost_estimate=CHEAP,
         compiler_params=pltpu.CompilerParams(vmem_limit_bytes=16 * 2**20),
         name="table",
     )(wavemap, after)
@@ -279,11 +283,7 @@
             pltpu.VMEM((SLOTS, 2, fields, rows, TILE), jnp.bfloat16),
             pltpu.SemaphoreType.DMA((SLOTS, 2)),
         ],
-        cost_estimate=pl.CostEstimate(
-            flops=2 * fields * rows * depth * lon_count,
-            bytes_accessed=2 * lon_count * (fields * rows + depth),
-            transcendentals=0,
-        ),
+        cost_estimate=CHEAP,
         compiler_params=pltpu.CompilerParams(vmem_limit_bytes=32 * 2**20),
         name="synthesis",
     )(*blocks, table)
@@ -331,11 +331,7 @@
             out_specs=[IN_VMEM] * (2 + len(fetches)),
             out_shape=[half(chunk)] * 2 + shapes,
             scratch_shapes=scratch + sems,
-            cost_estimate=pl.CostEstimate(
-                flops=4 * count * columns * degrees * width,
-                bytes_accessed=2 * count * degrees * (columns + width),
-                transcendentals=0,
-            ),
+            cost_estimate=CHEAP,
             compiler_params=params,
             name="leaf",
         )(*inputs, after, *sources)
@@ -349,57 +345,56 @@
             out_specs=[IN_VMEM] * (2 + len(fetches)),
             out_shape=[half(chunk)] * 2 + shapes,
             scratch_shapes=sems,
-            cost_estimate=pl.CostEstimate(
-                flops=2 * count * columns * width * width,
-                bytes_accessed=2 * count * width * (width + 2 * columns),
-                transcendentals=0,
-            ),
+            cost_estimate=CHEAP,
             compiler_params=params,
             name="level",
         )(own, came, maps, after, *sources)
 
-    def last(chunk, own, came, maps, lats, after):
+    def last(chunk, own, came, maps, lats, after, group, begun):
         count = sizes[chunk]
-        piece = jax.ShapeDtypeStruct((fields // peers, 2, count, rows), jnp.bfloat16)
+        piece = jax.ShapeDtypeStruct((fields // peers, 2, sum(sizes[n] for n in group), rows), jnp.bfloat16)
         return pl.pallas_call(
-            functools.partial(last_kernel, firsts[chunk], levels - 1),
-            in_specs=[IN_VMEM] * 4 + [IN_ANY],
+            functools.partial(last_kernel, firsts[chunk], levels - 1, firsts[chunk] - firsts[group[0]]),
+            in_specs=[IN_VMEM] * 4 + [IN_ANY] + [IN_VMEM] * len(begun),
             out_specs=[IN_VMEM] * peers,
             out_shape=[piece] * peers,
+            input_output_aliases={5 + n: n for n in range(len(begun))},
             scratch_shapes=[pltpu.VMEM((count, columns, rows), jnp.bfloat16)],
-            cost_estimate=pl.CostEstimate(
-                flops=2 * count * columns * width * (width + rows),
-                bytes_accessed=2 * count * width * (width + rows + 2 * columns),
-                transcendentals=0,
-            ),
+            cost_estimate=CHEAP,
             compiler_params=params,
             name="last",
-        )(own, came, maps, lats, after)
+        )(own, came, maps, lats, after, *begun)
 
     whole = [coef, leaf_map, skeleton]
-    state, before, inputs = [], stay(skeleton), [stay(array) for array in whole]
-    for chunk in chunks:
-        if chunk + 1 < len(sizes):
-            ahead = slice(firsts[chunk + 1], firsts[chunk + 1] + sizes[chunk + 1])
-            fetches = [(array, ahead) for array in whole]
+    order = [(chunk, stage) for chunk in chunks for stage in range(levels + 1)]
+    order.sort(key=lambda turn: (sum(turn), TURN * turn[0]))
+    wanted = []
+    for chunk, stage in order:
+        if stage == 0 and chunk:
+            ahead = slice(firsts[chunk], firsts[chunk] + sizes[chunk])
+            wanted.append((("leaf", chunk), [(array, ahead) for array in whole]))
+    wanted.reverse()
+    held = {("leaf", 0): [stay(array) for array in whole]}
+    before, table = stay(skeleton), None
+    state, begun, blocks = {}, [], []
+    for chunk, stage in order:
+        name, fetches = wanted.pop() if wanted else (None, [])
+        if stage == TABLE_STAGE and chunk == TABLE_CHUNK:
+            before = table = wave_table(wavemap, slots, [sum(sizes[n] for n in group) for group in GROUPS], NLON, before)
+        if stage == levels:
+            group = next(group for group in GROUPS if chunk in group)
+            begun = last(chunk, *state[chunk], level_maps, lat_map, before, group, begun)
+            before = begun[0]
+            if chunk == group[-1]:
+                blocks += [p if step == 0 else exchange(p, "wave", step) for step, p in enumerate(begun)]
+                begun = []
+            continue
+        if stage == 0:
+            before, send, *more = leaf(chunk, held["leaf", chunk], before, fetches)
         else:
-            fetches = [(level_maps, 0)]
-        before, send, *inputs = leaf(chunk, inputs, before, fetches)
-        state.append((before, exchange(send, "deg", 1)))
-    maps = {0: inputs[0]}
-    wanted = [(level_maps, num) for num in range(1, levels)] + [(lat_map, slice(0, slots))]
-    for num in range(levels - 1):
-        for chunk in chunks:
-            fetches = [wanted[len(maps) - 1]] if len(maps) <= len(wanted) else []
-            before, send, *more = level(chunk, num, *state[chunk], maps[num], before, fetches)
-            maps.update({len(maps): array for array in more})
-            state[chunk] = before, exchange(send, "deg", 2 << num)
-    before = table = wave_table(wavemap, slots, sizes, NLON, before)
-    blocks = []
-    for chunk in chunks:
-        pieces = last(chunk, *state[chunk], maps[levels - 1], maps[levels], before)
-        before = pieces[0]
-        blocks += [p if step == 0 else exchange(p, "wave", step) for step, p in enumerate(pieces)]
+            before, send, *more = level(chunk, stage - 1, *state[chunk], level_maps, before, fetches)
+        held[name] = more
+        state[chunk] = before, exchange(send, "deg", 1 << stage)
     return synthesis(blocks, table, NLON)
 
 

time: 69.1 us -> 65.3 us (0.945)
  waiting for transfers between devices: 23.7 us -> 11.7 us
  starting transfers between devices: 15.1 us -> 24.6 us
  Pallas kernels: 30 us -> 28.6 us
    ppermute x12 -> x18, waiting for transfers between devices: 23.7 us -> 11.7 us  [exchange(): lax.ppermute(shard, axis, [(i, i ^ step) for i in range(lax.axis_size(axi...]
    ppermute x12 -> x18, starting transfers between devices: 15.1 us -> 24.6 us  [exchange(): lax.ppermute(shard, axis, [(i, i ^ step) for i in range(lax.axis_size(axi...]
    pallas_call x1, Pallas kernels: 5.96 us -> 4.27 us  [wave_table(): pl.pallas_call(functools.partial(table_kernel, lon_count, slots, sizes),...]
    pallas_call x4 -> x8, Pallas kernels: 5.73 us -> 4.29 us  [level(): pl.pallas_call(functools.partial(level_kernel, firsts[chunk], num, places...]
    pallas_call x2 -> x4, Pallas kernels: 4.78 us -> 5.78 us  [last(): pl.pallas_call(functools.partial(last_kernel, firsts[chunk], levels - 1,...]
    pallas_call x2 -> x4, Pallas kernels: 4.88 us -> 5.6 us  [leaf(): pl.pallas_call(functools.partial(leaf_kernel, places), in_specs=[IN_VMEM...]
  transfers between devices with their start and end apart: 12 -> 18, of which waited for: 9 -> 5; matrix products, arithmetic and copies ran while one was open for 0% -> 0% of each run, Pallas kernels for 26% -> 26%
where the time goes in v4:
time: 65.3 us; the launch traced here: 65.2 us
  Pallas kernels  28.6 us (44%)
  starting transfers between devices  24.6 us (38%)
  waiting for transfers between devices  11.7 us (18%)
    ppermute x18, starting transfers between devices, exchange(): lax.ppermute(shard, axis, [(i, i ^ step) for i in range(lax.axis_size(axi...  24.6 us
    ppermute x18, waiting for transfers between devices, exchange(): lax.ppermute(shard, axis, [(i, i ^ step) for i in range(lax.axis_size(axi...  11.7 us
    pallas_call x1, Pallas kernels, synthesis(): pl.pallas_call(synthesis_kernel, in_specs=[IN_VMEM] * (len(blocks) + 1),...  8.69 us
    pallas_call x4, Pallas kernels, last(): pl.pallas_call(functools.partial(last_kernel, firsts[chunk], levels - 1,...  5.78 us
    pallas_call x4, Pallas kernels, leaf(): pl.pallas_call(functools.partial(leaf_kernel, places), in_specs=[IN_VMEM...  5.6 us
    pallas_call x8, Pallas kernels, level(): pl.pallas_call(functools.partial(level_kernel, firsts[chunk], num, places...  4.29 us
    pallas_call x1, Pallas kernels, wave_table(): pl.pallas_call(functools.partial(table_kernel, lon_count, slots, sizes),...  4.27 us
  transfers between devices with their start and end apart: 18, of which 5 were waited for; matrix products, arithmetic and copies ran while one was open for 0% of the time, Pallas kernels for 26%

profile of v4, /device:TPU:0, one launch (start us, length us, event | category | flops | bytes accessed | tf_op | source)
XLA Modules:
  0.0 65.2 jit_solution(17847185325613131942)
XLA Ops:
  0.0 2.7 %leaf.4 = (bf16[16,32,128]{2,1,0:T(8,128)(2,1)S(1)}, bf16[16,32,128]{2,1,0:T(8,128)(2,1)S(1)}, bf16[16,64,256]{2,1,0:T(8,128)(2,1)S(1)}, bf16[16,256,128]{2,1,0:T(8,128)(2,1)S(1)}, s32[16,128]{1,0:T(8,128)S(1)}) custom-call(bf16[64,64,256]{2,1,0:T(8,128)(2,1)} %bitcast.3, bf16[64,256,128]{2,1,0:T(8,128)(2,1)} %refs_5_.5, s32[64,128]{1,0:T(8,128)} %refs_6_.5, ...), custom_call_target="tpu_custom_call" | custom-call | tf_op jit(solution)/shard_map/leaf/pallas_call | solution.py:328
  2.7 3.0 %collective-permute-start.1 = (bf16[16,32,128]{2,1,0:T(8,128)(2,1)S(1)}, bf16[16,32,128]{2,1,0:T(8,128)(2,1)S(1)}, u32[]{:S(2)}, u32[]{:S(2)}) collective-permute-start(bf16[16,32,128]{2,1,0:T(8,128)(2,1)S(1)} %get-tuple-element.63), channel_id=1, source_target_pairs={{0,1},{1,0},{2,3},{3,2},{4,5},{5,4},{6,7},{7,6},{8,9},{9,8},{10,11... | collective-permute-start | bytes 393224 | tf_op jit(solution)/shard_map/ppermute | solution.py:32
  5.7 1.8 %leaf.5 = (bf16[16,32,128]{2,1,0:T(8,128)(2,1)S(1)}, bf16[16,32,128]{2,1,0:T(8,128)(2,1)S(1)}, bf16[16,64,256]{2,1,0:T(8,128)(2,1)S(1)}, bf16[16,256,128]{2,1,0:T(8,128)(2,1)S(1)}, s32[16,128]{1,0:T(8,128)S(1)}) custom-call(bf16[16,64,256]{2,1,0:T(8,128)(2,1)S(1)} %get-tuple-element.54.refs_0_, bf16[16,256,128]{2,1,0:T(8,128)(2,1)S(1)} %get-tuple-element.55.refs_1_, ...), custom_call_target="tpu_custom_call" | custom-call | tf_op jit(solution)/shard_map/leaf/pallas_call | solution.py:328
  7.5 0.1 collective-permute-start
  7.6 1.9 %collective-permute-done.1.refs_1_ = bf16[16,32,128]{2,1,0:T(8,128)(2,1)S(1)} collective-permute-done((bf16[16,32,128]{2,1,0:T(8,128)(2,1)S(1)}, bf16[16,32,128]{2,1,0:T(8,128)(2,1)S(1)}, u32[]{:S(2)}, u32[]{:S(2)}) %collective-permute-start.1) | collective-permute-done | bytes 131104 | tf_op jit(solution)/shard_map/ppermute | solution.py:32
  9.5 1.4 %level.8 = (bf16[16,32,128]{2,1,0:T(8,128)(2,1)S(1)}, bf16[16,32,128]{2,1,0:T(8,128)(2,1)S(1)}, bf16[16,64,256]{2,1,0:T(8,128)(2,1)S(1)}, bf16[16,256,128]{2,1,0:T(8,128)(2,1)S(1)}, s32[16,128]{1,0:T(8,128)S(1)}) custom-call(bf16[16,32,128]{2,1,0:T(8,128)(2,1)S(1)} %get-tuple-element.57.refs_3_.refs_0_, ...), custom_call_target="tpu_custom_call" | custom-call | tf_op jit(solution)/shard_map/level/pallas_call | solution.py:342
  10.9 1.6 %collective-permute-start.4 = (bf16[16,32,128]{2,1,0:T(8,128)(2,1)S(1)}, bf16[16,32,128]{2,1,0:T(8,128)(2,1)S(1)}, u32[]{:S(2)}, u32[]{:S(2)}) collective-permute-start(bf16[16,32,128]{2,1,0:T(8,128)(2,1)S(1)} %get-tuple-element.72), channel_id=1, source_target_pairs={{0,2},{1,3},{2,0},{3,1},{4,6},{5,7},{6,4},{7,5},{8,10},{9,11},{10,... | collective-permute-start | bytes 393224 | tf_op jit(solution)/shard_map/ppermute | solution.py:32
  12.5 0.6 leaf.6
  13.1 2.3 %collective-permute-start.3 = (bf16[16,32,128]{2,1,0:T(8,128)(2,1)S(1)}, bf16[16,32,128]{2,1,0:T(8,128)(2,1)S(1)}, u32[]{:S(2)}, u32[]{:S(2)}) collective-permute-start(bf16[16,32,128]{2,1,0:T(8,128)(2,1)S(1)} %get-tuple-element.68), channel_id=1, source_target_pairs={{0,1},{1,0},{2,3},{3,2},{4,5},{5,4},{6,7},{7,6},{8,9},{9,8},{10,11... | collective-permute-start | bytes 393224 | tf_op jit(solution)/shard_map/ppermute | solution.py:32
  15.4 0.4 level.9
  15.8 0.8 %collective-permute-start.2 = (bf16[16,32,128]{2,1,0:T(8,128)(2,1)S(1)}, bf16[16,32,128]{2,1,0:T(8,128)(2,1)S(1)}, u32[]{:S(2)}, u32[]{:S(2)}) collective-permute-start(bf16[16,32,128]{2,1,0:T(8,128)(2,1)S(1)} %get-tuple-element.67), channel_id=1, source_target_pairs={{0,2},{1,3},{2,0},{3,1},{4,6},{5,7},{6,4},{7,5},{8,10},{9,11},{10,... | collective-permute-start | bytes 393224 | tf_op jit(solution)/shard_map/ppermute | solution.py:32
  16.6 0.0 collective-permute-done.4.refs_1_
  16.6 0.4 level.10
  17.0 2.4 %collective-permute-start.8 = (bf16[16,32,128]{2,1,0:T(8,128)(2,1)S(1)}, bf16[16,32,128]{2,1,0:T(8,128)(2,1)S(1)}, u32[]{:S(2)}, u32[]{:S(2)}) collective-permute-start(bf16[16,32,128]{2,1,0:T(8,128)(2,1)S(1)} %get-tuple-element.80), channel_id=1, source_target_pairs={{0,4},{1,5},{2,6},{3,7},{4,0},{5,1},{6,2},{7,3},{8,12},{9,13},{10,... | collective-permute-start | bytes 393224 | tf_op jit(solution)/shard_map/ppermute | solution.py:32
  19.4 0.6 leaf.7
  20.0 3.3 %collective-permute-start.7 = (bf16[16,32,128]{2,1,0:T(8,128)(2,1)S(1)}, bf16[16,32,128]{2,1,0:T(8,128)(2,1)S(1)}, u32[]{:S(2)}, u32[]{:S(2)}) collective-permute-start(bf16[16,32,128]{2,1,0:T(8,128)(2,1)S(1)} %get-tuple-element.79), channel_id=1, source_target_pairs={{0,1},{1,0},{2,3},{3,2},{4,5},{5,4},{6,7},{7,6},{8,9},{9,8},{10,11... | collective-permute-start | bytes 393224 | tf_op jit(solution)/shard_map/ppermute | solution.py:32
  23.3 0.4 level.11
  23.7 0.0 copy-start
  23.7 1.1 %collective-permute-start.6 = (bf16[16,32,128]{2,1,0:T(8,128)(2,1)S(1)}, bf16[16,32,128]{2,1,0:T(8,128)(2,1)S(1)}, u32[]{:S(2)}, u32[]{:S(2)}) collective-permute-start(bf16[16,32,128]{2,1,0:T(8,128)(2,1)S(1)} %get-tuple-element.78), channel_id=1, source_target_pairs={{0,2},{1,3},{2,0},{3,1},{4,6},{5,7},{6,4},{7,5},{8,10},{9,11},{10,... | collective-permute-start | bytes 393224 | tf_op jit(solution)/shard_map/ppermute | solution.py:32
  24.8 0.0 collective-permute-done.2.refs_1_
  24.8 0.4 level.12
  25.2 0.7 %collective-permute-start.5 = (bf16[16,32,128]{2,1,0:T(8,128)(2,1)S(1)}, bf16[16,32,128]{2,1,0:T(8,128)(2,1)S(1)}, u32[]{:S(2)}, u32[]{:S(2)}) collective-permute-start(bf16[16,32,128]{2,1,0:T(8,128)(2,1)S(1)} %get-tuple-element.77), channel_id=1, source_target_pairs={{0,4},{1,5},{2,6},{3,7},{4,0},{5,1},{6,2},{7,3},{8,12},{9,13},{10,... | collective-permute-start | bytes 393224 | tf_op jit(solution)/shard_map/ppermute | solution.py:32
  25.9 0.0 collective-permute-done.8.came_in
  25.9 1.4 %last.4 = (bf16[8,2,32,128]{3,2,1,0:T(8,128)(2,1)S(1)}, bf16[8,2,32,128]{3,2,1,0:T(8,128)(2,1)S(1)}, bf16[8,2,32,128]{3,2,1,0:T(8,128)(2,1)S(1)}, bf16[8,2,32,128]{3,2,1,0:T(8,128)(2,1)S(1)}) custom-call(bf16[16,32,128]{2,1,0:T(8,128)(2,1)S(1)} %get-tuple-element.73.refs_3_.own_in, bf16[16,32,128]{2,1,0:T(8,128)(2,1)S(1)} %collective-permute-done.8.came_in, ...), custom_call_target="tpu_custom_call" | custom-call | tf_op jit(solution)/shard_map/last/pallas_call | solution.py:356
  27.4 0.0 copy-start.1
  27.4 0.4 level.13
  27.8 2.1 %collective-permute-start.12 = (bf16[16,32,128]{2,1,0:T(8,128)(2,1)S(1)}, bf16[16,32,128]{2,1,0:T(8,128)(2,1)S(1)}, u32[]{:S(2)}, u32[]{:S(2)}) collective-permute-start(bf16[16,32,128]{2,1,0:T(8,128)(2,1)S(1)} %get-tuple-element.91), channel_id=1, source_target_pairs={{0,2},{1,3},{2,0},{3,1},{4,6},{5,7},{6,4},{7,5},{8,10},{9,11},{10,... | collective-permute-start | bytes 393224 | tf_op jit(solution)/shard_map/ppermute | solution.py:32
  29.9 4.3 %table.1.refs_3_.refs_8_ = bf16[2,256,4224]{2,1,0:T(8,128)(2,1)S(1)} custom-call(s32[256]{0:T(256)S(1)} %copy-done.1, bf16[16,32,128]{2,1,0:T(8,128)(2,1)S(1)} %get-tuple-element.82.after_ref.refs_0_), custom_call_target="tpu_custom_call" | custom-call | tf_op jit(solution)/shard_map/table/pallas_call | solution.py:200
  34.2 0.4 level.14
  34.6 3.2 %collective-permute-start.14 = (bf16[16,32,128]{2,1,0:T(8,128)(2,1)S(1)}, bf16[16,32,128]{2,1,0:T(8,128)(2,1)S(1)}, u32[]{:S(2)}, u32[]{:S(2)}) collective-permute-start(bf16[16,32,128]{2,1,0:T(8,128)(2,1)S(1)} %get-tuple-element.94), channel_id=1, source_target_pairs={{0,4},{1,5},{2,6},{3,7},{4,0},{5,1},{6,2},{7,3},{8,12},{9,13},{10,... | collective-permute-start | bytes 393224 | tf_op jit(solution)/shard_map/ppermute | solution.py:32
  37.9 0.0 collective-permute-done.5.came_in
  37.9 1.4 %last.5 = (bf16[8,2,32,128]{3,2,1,0:T(8,128)(2,1)S(1)}, bf16[8,2,32,128]{3,2,1,0:T(8,128)(2,1)S(1)}, bf16[8,2,32,128]{3,2,1,0:T(8,128)(2,1)S(1)}, bf16[8,2,32,128]{3,2,1,0:T(8,128)(2,1)S(1)}) custom-call(bf16[16,32,128]{2,1,0:T(8,128)(2,1)S(1)} %get-tuple-element.76._.own_in, ...), custom_call_target="tpu_custom_call", output_to_operand_aliasing={{0}: (5, {}), {1}: (6, {}), {2}: (7, {}), {3}: (8, {})} | custom-call | tf_op jit(solution)/shard_map/last/pallas_call | solution.py:356
  39.3 0.4 level.15
  39.7 0.1 collective-permute-start.13
  39.8 0.1 collective-permute-start.9
  39.9 1.6 %collective-permute-start.10 = (bf16[8,2,32,128]{3,2,1,0:T(8,128)(2,1)S(1)}, bf16[8,2,32,128]{3,2,1,0:T(8,128)(2,1)S(1)}, u32[]{:S(2)}, u32[]{:S(2)}) collective-permute-start(bf16[8,2,32,128]{3,2,1,0:T(8,128)(2,1)S(1)} %get-tuple-element.89), channel_id=1, source_target_pairs={{0,16},{8,24},{16,0},{24,8},{1,17},{9,25},{17,1},{25,9},{2,18},{10... | collective-permute-start | bytes 393224 | tf_op jit(solution)/shard_map/ppermute | solution.py:32
  41.5 0.3 collective-permute-start.11
  41.8 0.1 collective-permute-done.14.came_in
  41.8 1.4 %last.6 = (bf16[8,2,32,128]{3,2,1,0:T(8,128)(2,1)S(1)}, bf16[8,2,32,128]{3,2,1,0:T(8,128)(2,1)S(1)}, bf16[8,2,32,128]{3,2,1,0:T(8,128)(2,1)S(1)}, bf16[8,2,32,128]{3,2,1,0:T(8,128)(2,1)S(1)}) custom-call(bf16[16,32,128]{2,1,0:T(8,128)(2,1)S(1)} %get-tuple-element.83._.own_in, bf16[16,32,128]{2,1,0:T(8,128)(2,1)S(1)} %collective-permute-done.14.came_in, ...), custom_call_target="tpu_custom_call" | custom-call | tf_op jit(solution)/shard_map/last/pallas_call | solution.py:356
  43.3 3.4 %collective-permute-done.13.came_in = bf16[16,32,128]{2,1,0:T(8,128)(2,1)S(1)} collective-permute-done((bf16[16,32,128]{2,1,0:T(8,128)(2,1)S(1)}, bf16[16,32,128]{2,1,0:T(8,128)(2,1)S(1)}, u32[]{:S(2)}, u32[]{:S(2)}) %collective-permute-start.13) | collective-permute-done | bytes 131104 | tf_op jit(solution)/shard_map/ppermute | solution.py:32
  46.7 1.4 %last.7 = (bf16[8,2,32,128]{3,2,1,0:T(8,128)(2,1)S(1)}, bf16[8,2,32,128]{3,2,1,0:T(8,128)(2,1)S(1)}, bf16[8,2,32,128]{3,2,1,0:T(8,128)(2,1)S(1)}, bf16[8,2,32,128]{3,2,1,0:T(8,128)(2,1)S(1)}) custom-call(bf16[16,32,128]{2,1,0:T(8,128)(2,1)S(1)} %get-tuple-element.92._.own_in, ...), custom_call_target="tpu_custom_call", output_to_operand_aliasing={{0}: (5, {}), {1}: (6, {}), {2}: (7, {}), {3}: (8, {})} | custom-call | tf_op jit(solution)/shard_map/last/pallas_call | solution.py:356
  48.1 0.1 collective-permute-start.15
  48.2 1.5 %collective-permute-start.16 = (bf16[8,2,32,128]{3,2,1,0:T(8,128)(2,1)S(1)}, bf16[8,2,32,128]{3,2,1,0:T(8,128)(2,1)S(1)}, u32[]{:S(2)}, u32[]{:S(2)}) collective-permute-start(bf16[8,2,32,128]{3,2,1,0:T(8,128)(2,1)S(1)} %get-tuple-element.101), channel_id=1, source_target_pairs={{0,16},{8,24},{16,0},{24,8},{1,17},{9,25},{17,1},{25,9},{2,18},{10... | collective-permute-start | bytes 393224 | tf_op jit(solution)/shard_map/ppermute | solution.py:32
  49.8 0.0 collective-permute-done.9.refs_1_
  49.8 0.3 collective-permute-start.17
  50.1 4.5 %collective-permute-done.16.refs_6_ = bf16[8,2,32,128]{3,2,1,0:T(8,128)(2,1)S(1)} collective-permute-done((bf16[8,2,32,128]{3,2,1,0:T(8,128)(2,1)S(1)}, bf16[8,2,32,128]{3,2,1,0:T(8,128)(2,1)S(1)}, u32[]{:S(2)}, u32[]{:S(2)}) %collective-permute-start.16) | collective-permute-done | bytes 131104 | tf_op jit(solution)/shard_map/ppermute | solution.py:32
  54.6 1.9 %collective-permute-done.17.refs_7_ = bf16[8,2,32,128]{3,2,1,0:T(8,128)(2,1)S(1)} collective-permute-done((bf16[8,2,32,128]{3,2,1,0:T(8,128)(2,1)S(1)}, bf16[8,2,32,128]{3,2,1,0:T(8,128)(2,1)S(1)}, u32[]{:S(2)}, u32[]{:S(2)}) %collective-permute-start.17) | collective-permute-done | bytes 131104 | tf_op jit(solution)/shard_map/ppermute | solution.py:32
  56.5 8.7 %synthesis.1 = bf16[8,128,8192]{2,1,0:T(8,128)(2,1)} custom-call(bf16[8,2,32,128]{3,2,1,0:T(8,128)(2,1)S(1)} %get-tuple-element.87.refs_3_.refs_0_, bf16[8,2,32,128]{3,2,1,0:T(8,128)(2,1)S(1)} %collective-permute-done.9.refs_1_, bf16[8,2,32,128]{3,2,1,0:T(8,128)(2,1)S(1)} %collective-permute-done.10.refs_2_, ...), custom_call_target="tpu_custom_call" | custom-call | tf_op jit(solution)/shard_map/synthesis/pallas_call | solution.py:275
  (16 shorter events, 0.0 us)
Async XLA Ops:
  0.0 9.5 %slice-start = ((s8[6291456]{0:T(1024)(128)(4,1)}), s8[4194304]{0:T(1024)(128)(4,1)S(1)}, s32[]{:S(2)}) async-start(s8[6291456]{0:T(1024)(128)(4,1)} %bitcast.1), calls=%async_computation | async-start | bytes 8388608
  0.0 9.5 %slice-start.1 = ((s8[6291456]{0:T(1024)(128)(4,1)}), s8[2097152]{0:T(1024)(128)(4,1)S(1)}, s32[]{:S(2)}) async-start(s8[6291456]{0:T(1024)(128)(4,1)} %bitcast.1), calls=%async_computation.1 | async-start | bytes 4194304
  2.7 6.8 %collective-permute-start.1 = (bf16[16,32,128]{2,1,0:T(8,128)(2,1)S(1)}, bf16[16,32,128]{2,1,0:T(8,128)(2,1)S(1)}, u32[]{:S(2)}, u32[]{:S(2)}) collective-permute-start(bf16[16,32,128]{2,1,0:T(8,128)(2,1)S(1)} %get-tuple-element.63), channel_id=1, source_target_pairs={{0,1},{1,0},{2,3},{3,2},{4,5},{5,4},{6,7},{7,6},{8,9},{9,8},{10,11... | collective-permute-start | bytes 393224 | tf_op jit(solution)/shard_map/ppermute | solution.py:32
  7.5 7.9 %collective-permute-start = (bf16[16,32,128]{2,1,0:T(8,128)(2,1)S(1)}, bf16[16,32,128]{2,1,0:T(8,128)(2,1)S(1)}, u32[]{:S(2)}, u32[]{:S(2)}) collective-permute-start(bf16[16,32,128]{2,1,0:T(8,128)(2,1)S(1)} %get-tuple-element.59), channel_id=1, source_target_pairs={{0,1},{1,0},{2,3},{3,2},{4,5},{5,4},{6,7},{7,6},{8,9},{9,8},{10,11... | collective-permute-start | bytes 393224 | tf_op jit(solution)/shard_map/ppermute | solution.py:32
  10.9 5.7 %collective-permute-start.4 = (bf16[16,32,128]{2,1,0:T(8,128)(2,1)S(1)}, bf16[16,32,128]{2,1,0:T(8,128)(2,1)S(1)}, u32[]{:S(2)}, u32[]{:S(2)}) collective-permute-start(bf16[16,32,128]{2,1,0:T(8,128)(2,1)S(1)} %get-tuple-element.72), channel_id=1, source_target_pairs={{0,2},{1,3},{2,0},{3,1},{4,6},{5,7},{6,4},{7,5},{8,10},{9,11},{10,... | collective-permute-start | bytes 393224 | tf_op jit(solution)/shard_map/ppermute | solution.py:32
  13.1 10.2 %collective-permute-start.3 = (bf16[16,32,128]{2,1,0:T(8,128)(2,1)S(1)}, bf16[16,32,128]{2,1,0:T(8,128)(2,1)S(1)}, u32[]{:S(2)}, u32[]{:S(2)}) collective-permute-start(bf16[16,32,128]{2,1,0:T(8,128)(2,1)S(1)} %get-tuple-element.68), channel_id=1, source_target_pairs={{0,1},{1,0},{2,3},{3,2},{4,5},{5,4},{6,7},{7,6},{8,9},{9,8},{10,11... | collective-permute-start | bytes 393224 | tf_op jit(solution)/shard_map/ppermute | solution.py:32
  15.8 9.0 %collective-permute-start.2 = (bf16[16,32,128]{2,1,0:T(8,128)(2,1)S(1)}, bf16[16,32,128]{2,1,0:T(8,128)(2,1)S(1)}, u32[]{:S(2)}, u32[]{:S(2)}) collective-permute-start(bf16[16,32,128]{2,1,0:T(8,128)(2,1)S(1)} %get-tuple-element.67), channel_id=1, source_target_pairs={{0,2},{1,3},{2,0},{3,1},{4,6},{5,7},{6,4},{7,5},{8,10},{9,11},{10,... | collective-permute-start | bytes 393224 | tf_op jit(solution)/shard_map/ppermute | solution.py:32
  17.0 8.9 %collective-permute-start.8 = (bf16[16,32,128]{2,1,0:T(8,128)(2,1)S(1)}, bf16[16,32,128]{2,1,0:T(8,128)(2,1)S(1)}, u32[]{:S(2)}, u32[]{:S(2)}) collective-permute-start(bf16[16,32,128]{2,1,0:T(8,128)(2,1)S(1)} %get-tuple-element.80), channel_id=1, source_target_pairs={{0,4},{1,5},{2,6},{3,7},{4,0},{5,1},{6,2},{7,3},{8,12},{9,13},{10,... | collective-permute-start | bytes 393224 | tf_op jit(solution)/shard_map/ppermute | solution.py:32
  20.0 7.4 %collective-permute-start.7 = (bf16[16,32,128]{2,1,0:T(8,128)(2,1)S(1)}, bf16[16,32,128]{2,1,0:T(8,128)(2,1)S(1)}, u32[]{:S(2)}, u32[]{:S(2)}) collective-permute-start(bf16[16,32,128]{2,1,0:T(8,128)(2,1)S(1)} %get-tuple-element.79), channel_id=1, source_target_pairs={{0,1},{1,0},{2,3},{3,2},{4,5},{5,4},{6,7},{7,6},{8,9},{9,8},{10,11... | collective-permute-start | bytes 393224 | tf_op jit(solution)/shard_map/ppermute | solution.py:32
  23.7 2.2 %copy-start = (bf16[64,128,128]{2,1,0:T(8,128)(2,1)S(1)}, bf16[64,128,128]{2,1,0:T(8,128)(2,1)}, u32[]{:S(2)}) copy-start(bf16[64,128,128]{2,1,0:T(8,128)(2,1)} %lats.7) | copy-start | bytes 6291460
  23.7 10.5 %collective-permute-start.6 = (bf16[16,32,128]{2,1,0:T(8,128)(2,1)S(1)}, bf16[16,32,128]{2,1,0:T(8,128)(2,1)S(1)}, u32[]{:S(2)}, u32[]{:S(2)}) collective-permute-start(bf16[16,32,128]{2,1,0:T(8,128)(2,1)S(1)} %get-tuple-element.78), channel_id=1, source_target_pairs={{0,2},{1,3},{2,0},{3,1},{4,6},{5,7},{6,4},{7,5},{8,10},{9,11},{10,... | collective-permute-start | bytes 393224 | tf_op jit(solution)/shard_map/ppermute | solution.py:32
  25.2 12.6 %collective-permute-start.5 = (bf16[16,32,128]{2,1,0:T(8,128)(2,1)S(1)}, bf16[16,32,128]{2,1,0:T(8,128)(2,1)S(1)}, u32[]{:S(2)}, u32[]{:S(2)}) collective-permute-start(bf16[16,32,128]{2,1,0:T(8,128)(2,1)S(1)} %get-tuple-element.77), channel_id=1, source_target_pairs={{0,4},{1,5},{2,6},{3,7},{4,0},{5,1},{6,2},{7,3},{8,12},{9,13},{10,... | collective-permute-start | bytes 393224 | tf_op jit(solution)/shard_map/ppermute | solution.py:32
  27.4 2.5 %copy-start.1 = (s32[256]{0:T(256)S(1)}, s32[256]{0:T(256)}, u32[]{:S(2)}) copy-start(s32[256]{0:T(256)} %map_ref.1) | copy-start | bytes 3076
  27.8 11.5 %collective-permute-start.12 = (bf16[16,32,128]{2,1,0:T(8,128)(2,1)S(1)}, bf16[16,32,128]{2,1,0:T(8,128)(2,1)S(1)}, u32[]{:S(2)}, u32[]{:S(2)}) collective-permute-start(bf16[16,32,128]{2,1,0:T(8,128)(2,1)S(1)} %get-tuple-element.91), channel_id=1, source_target_pairs={{0,2},{1,3},{2,0},{3,1},{4,6},{5,7},{6,4},{7,5},{8,10},{9,11},{10,... | collective-permute-start | bytes 393224 | tf_op jit(solution)/shard_map/ppermute | solution.py:32
  34.6 7.2 %collective-permute-start.14 = (bf16[16,32,128]{2,1,0:T(8,128)(2,1)S(1)}, bf16[16,32,128]{2,1,0:T(8,128)(2,1)S(1)}, u32[]{:S(2)}, u32[]{:S(2)}) collective-permute-start(bf16[16,32,128]{2,1,0:T(8,128)(2,1)S(1)} %get-tuple-element.94), channel_id=1, source_target_pairs={{0,4},{1,5},{2,6},{3,7},{4,0},{5,1},{6,2},{7,3},{8,12},{9,13},{10,... | collective-permute-start | bytes 393224 | tf_op jit(solution)/shard_map/ppermute | solution.py:32
  39.7 7.0 %collective-permute-start.13 = (bf16[16,32,128]{2,1,0:T(8,128)(2,1)S(1)}, bf16[16,32,128]{2,1,0:T(8,128)(2,1)S(1)}, u32[]{:S(2)}, u32[]{:S(2)}) collective-permute-start(bf16[16,32,128]{2,1,0:T(8,128)(2,1)S(1)} %get-tuple-element.93), channel_id=1, source_target_pairs={{0,4},{1,5},{2,6},{3,7},{4,0},{5,1},{6,2},{7,3},{8,12},{9,13},{10,... | collective-permute-start | bytes 393224 | tf_op jit(solution)/shard_map/ppermute | solution.py:32
  39.8 9.9 %collective-permute-start.9 = (bf16[8,2,32,128]{3,2,1,0:T(8,128)(2,1)S(1)}, bf16[8,2,32,128]{3,2,1,0:T(8,128)(2,1)S(1)}, u32[]{:S(2)}, u32[]{:S(2)}) collective-permute-start(bf16[8,2,32,128]{3,2,1,0:T(8,128)(2,1)S(1)} %get-tuple-element.88), channel_id=1, source_target_pairs={{0,8},{8,0},{16,24},{24,16},{1,9},{9,1},{17,25},{25,17},{2,10},{10... | collective-permute-start | bytes 393224 | tf_op jit(solution)/shard_map/ppermute | solution.py:32
  39.9 10.2 %collective-permute-start.10 = (bf16[8,2,32,128]{3,2,1,0:T(8,128)(2,1)S(1)}, bf16[8,2,32,128]{3,2,1,0:T(8,128)(2,1)S(1)}, u32[]{:S(2)}, u32[]{:S(2)}) collective-permute-start(bf16[8,2,32,128]{3,2,1,0:T(8,128)(2,1)S(1)} %get-tuple-element.89), channel_id=1, source_target_pairs={{0,16},{8,24},{16,0},{24,8},{1,17},{9,25},{17,1},{25,9},{2,18},{10... | collective-permute-start | bytes 393224 | tf_op jit(solution)/shard_map/ppermute | solution.py:32
  41.5 8.6 %collective-permute-start.11 = (bf16[8,2,32,128]{3,2,1,0:T(8,128)(2,1)S(1)}, bf16[8,2,32,128]{3,2,1,0:T(8,128)(2,1)S(1)}, u32[]{:S(2)}, u32[]{:S(2)}) collective-permute-start(bf16[8,2,32,128]{3,2,1,0:T(8,128)(2,1)S(1)} %get-tuple-element.90), channel_id=1, source_target_pairs={{0,24},{8,16},{16,8},{24,0},{1,25},{9,17},{17,9},{25,1},{2,26},{10... | collective-permute-start | bytes 393224 | tf_op jit(solution)/shard_map/ppermute | solution.py:32
  48.1 2.0 %collective-permute-start.15 = (bf16[8,2,32,128]{3,2,1,0:T(8,128)(2,1)S(1)}, bf16[8,2,32,128]{3,2,1,0:T(8,128)(2,1)S(1)}, u32[]{:S(2)}, u32[]{:S(2)}) collective-permute-start(bf16[8,2,32,128]{3,2,1,0:T(8,128)(2,1)S(1)} %get-tuple-element.100), channel_id=1, source_target_pairs={{0,8},{8,0},{16,24},{24,16},{1,9},{9,1},{17,25},{25,17},{2,10},{10... | collective-permute-start | bytes 393224 | tf_op jit(solution)/shard_map/ppermute | solution.py:32
  48.2 6.4 %collective-permute-start.16 = (bf16[8,2,32,128]{3,2,1,0:T(8,128)(2,1)S(1)}, bf16[8,2,32,128]{3,2,1,0:T(8,128)(2,1)S(1)}, u32[]{:S(2)}, u32[]{:S(2)}) collective-permute-start(bf16[8,2,32,128]{3,2,1,0:T(8,128)(2,1)S(1)} %get-tuple-element.101), channel_id=1, source_target_pairs={{0,16},{8,24},{16,0},{24,8},{1,17},{9,25},{17,1},{25,9},{2,18},{10... | collective-permute-start | bytes 393224 | tf_op jit(solution)/shard_map/ppermute | solution.py:32
  49.8 6.7 %collective-permute-start.17 = (bf16[8,2,32,128]{3,2,1,0:T(8,128)(2,1)S(1)}, bf16[8,2,32,128]{3,2,1,0:T(8,128)(2,1)S(1)}, u32[]{:S(2)}, u32[]{:S(2)}) collective-permute-start(bf16[8,2,32,128]{3,2,1,0:T(8,128)(2,1)S(1)} %get-tuple-element.102), channel_id=1, source_target_pairs={{0,24},{8,16},{16,8},{24,0},{1,25},{9,17},{17,9},{25,1},{2,26},{10... | collective-permute-start | bytes 393224 | tf_op jit(solution)/shard_map/ppermute | solution.py:32

commit v5 on v4

--- a/solution.py
+++ b/solution.py
@@ -12,8 +12,7 @@
 GROUPS = ((0, 1), (2, 3))
 TURN = -1
 BLOCK = 64
-TABLE_STAGE = 2
-TABLE_CHUNK = 2
+TABLE_AT = ()
 LANES = 128
 PARTS = 4
 TILE = 512
@@ -145,7 +144,9 @@
     size = tile * tile
     out_at = lax.broadcasted_iota(jnp.int32, (size, size), 0)
     in_at = lax.broadcasted_iota(jnp.int32, (size, size), 1)
-    swap = ((out_at // tile == in_at % tile) & (out_at % tile == in_at // tile)).astype(jnp.bfloat16)
+    shift = tile.bit_length() - 1
+    swap = (out_at >> shift) + ((out_at & tile - 1) << shift) == in_at
+    swap = swap.astype(jnp.bfloat16)
     rows = block_ref.shape[2]
     me = lax.axis_index("wave")
     for g in range(0, count, tile):
@@ -162,7 +163,8 @@
                         out_refs[step][:, part, offset + g : offset + g + tile, :] = moved[at : at + share]
 
 
-def table_kernel(lon_count, slots, sizes, map_ref, after_ref, table_ref, q_ref):
+def table_kernel(lon_count, slots, sizes, first, count, map_ref, *refs):
+    table_ref, q_ref = refs[-2:]
     me = lax.axis_index("wave")
     row = 0
     for n, size in enumerate(sizes):
@@ -173,7 +175,8 @@
                 q_ref[pl.ds(row + m, 1), :] = jnp.full((1, LANES), map_ref[start + m], jnp.int32)
                 return carry
 
-            lax.fori_loop(0, size, put, 0, unroll=8)
+            if first <= row < first + count:
+                lax.fori_loop(0, size, put, 0, unroll=8)
             row += size
     scale = 2.0 * jnp.pi / lon_count
     lane = lax.broadcasted_iota(jnp.int32, (BLOCK, LANES), 1)
@@ -192,21 +195,22 @@
             table_ref[1, here, h * LANES : (h + 1) * LANES] = (c * sl - s * cl).astype(jnp.bfloat16)
         return carry
 
-    lax.fori_loop(0, q_ref.shape[0] // BLOCK, rows, 0)
-
-
-def wave_table(wavemap, slots, sizes, lon_count, after):
+    lax.fori_loop(first // BLOCK, (first + count) // BLOCK, rows, 0)
+
+
+def wave_table(wavemap, slots, sizes, lon_count, after, begun, first, count):
     total = wavemap.shape[0]
     return pl.pallas_call(
-        functools.partial(table_kernel, lon_count, slots, sizes),
-        in_specs=[pl.BlockSpec(memory_space=pltpu.SMEM), IN_ANY],
+        functools.partial(table_kernel, lon_count, slots, sizes, first, count),
+        in_specs=[pl.BlockSpec(memory_space=pltpu.SMEM), IN_ANY] + [IN_VMEM] * len(begun),
+        input_output_aliases={2: 0} if begun else {},
         out_specs=IN_VMEM,
         out_shape=jax.ShapeDtypeStruct((2, total, lon_count // 2 + LANES), jnp.bfloat16),
         scratch_shapes=[pltpu.VMEM((total, LANES), jnp.int32)],
         cost_estimate=CHEAP,
         compiler_params=pltpu.CompilerParams(vmem_limit_bytes=16 * 2**20),
         name="table",
-    )(wavemap, after)
+    )(wavemap, after, *begun)
 
 
 def synthesis_kernel(*refs):
@@ -375,12 +379,21 @@
             wanted.append((("leaf", chunk), [(array, ahead) for array in whole]))
     wanted.reverse()
     held = {("leaf", 0): [stay(array) for array in whole]}
-    before, table = stay(skeleton), None
+    before, table, filled = stay(skeleton), None, 0
+    group_sizes = [sum(sizes[n] for n in group) for group in GROUPS]
+    share_rows = slots * peers // (1 + len(TABLE_AT))
+
+    def make_table(after, table):
+        nonlocal filled
+        begun = [] if table is None else [table]
+        filled += share_rows
+        return wave_table(wavemap, slots, group_sizes, NLON, after, begun, filled - share_rows, share_rows)
+
     state, begun, blocks = {}, [], []
     for chunk, stage in order:
         name, fetches = wanted.pop() if wanted else (None, [])
-        if stage == TABLE_STAGE and chunk == TABLE_CHUNK:
-            before = table = wave_table(wavemap, slots, [sum(sizes[n] for n in group) for group in GROUPS], NLON, before)
+        if (chunk, stage) in TABLE_AT:
+            before = table = make_table(before, table)
         if stage == levels:
             group = next(group for group in GROUPS if chunk in group)
             begun = last(chunk, *state[chunk], level_maps, lat_map, before, group, begun)
@@ -395,6 +408,8 @@
             before, send, *more = level(chunk, stage - 1, *state[chunk], level_maps, before, fetches)
         held[name] = more
         state[chunk] = before, exchange(send, "deg", 1 << stage)
+    while filled < slots * peers:
+        before = table = make_table(before, table)
     return synthesis(blocks, table, NLON)
 
 

time: 65.3 us -> 62.6 us (0.959)
  waiting for transfers between devices: 11.7 us -> 9.09 us
  starting transfers between devices: 24.6 us -> 23.9 us
    ppermute x18, waiting for transfers between devices: 11.7 us -> 9.09 us  [exchange(): lax.ppermute(shard, axis, [(i, i ^ step) for i in range(lax.axis_size(axi...]
  transfers between devices with their start and end apart: 18 -> 18, of which waited for: 5 -> 7; matrix products, arithmetic and copies ran while one was open for 0% -> 0% of each run, Pallas kernels for 26% -> 28%
where the time goes in v5:
time: 62.6 us; the launch traced here: 62.2 us
  Pallas kernels  28.8 us (46%)
  starting transfers between devices  23.9 us (38%)
  waiting for transfers between devices  9.09 us (15%)
    ppermute x18, starting transfers between devices, exchange(): lax.ppermute(shard, axis, [(i, i ^ step) for i in range(lax.axis_size(axi...  23.9 us
    ppermute x18, waiting for transfers between devices, exchange(): lax.ppermute(shard, axis, [(i, i ^ step) for i in range(lax.axis_size(axi...  9.09 us
    pallas_call x1, Pallas kernels, synthesis(): pl.pallas_call(synthesis_kernel, in_specs=[IN_VMEM] * (len(blocks) + 1),...  8.69 us
    pallas_call x4, Pallas kernels, last(): pl.pallas_call(functools.partial(last_kernel, firsts[chunk], levels - 1,...  5.95 us
    pallas_call x4, Pallas kernels, leaf(): pl.pallas_call(functools.partial(leaf_kernel, places), in_specs=[IN_VMEM...  5.6 us
    pallas_call x8, Pallas kernels, level(): pl.pallas_call(functools.partial(level_kernel, firsts[chunk], num, places...  4.29 us
    pallas_call x1, Pallas kernels, wave_table(): pl.pallas_call(functools.partial(table_kernel, lon_count, slots, sizes, f...  4.27 us
  transfers between devices with their start and end apart: 18, of which 7 were waited for; matrix products, arithmetic and copies ran while one was open for 0% of the time, Pallas kernels for 28%

profile of v5, /device:TPU:0, one launch (start us, length us, event | category | flops | bytes accessed | tf_op | source)
XLA Modules:
  0.0 62.2 jit_solution(16297923742507070202)
XLA Ops:
  0.0 2.7 %leaf.4 = (bf16[16,32,128]{2,1,0:T(8,128)(2,1)S(1)}, bf16[16,32,128]{2,1,0:T(8,128)(2,1)S(1)}, bf16[16,64,256]{2,1,0:T(8,128)(2,1)S(1)}, bf16[16,256,128]{2,1,0:T(8,128)(2,1)S(1)}, s32[16,128]{1,0:T(8,128)S(1)}) custom-call(bf16[64,64,256]{2,1,0:T(8,128)(2,1)} %bitcast.3, bf16[64,256,128]{2,1,0:T(8,128)(2,1)} %refs_5_.5, s32[64,128]{1,0:T(8,128)} %refs_6_.5, ...), custom_call_target="tpu_custom_call" | custom-call | tf_op jit(solution)/shard_map/leaf/pallas_call | solution.py:332
  2.7 3.0 %collective-permute-start.1 = (bf16[16,32,128]{2,1,0:T(8,128)(2,1)S(1)}, bf16[16,32,128]{2,1,0:T(8,128)(2,1)S(1)}, u32[]{:S(2)}, u32[]{:S(2)}) collective-permute-start(bf16[16,32,128]{2,1,0:T(8,128)(2,1)S(1)} %get-tuple-element.63), channel_id=1, source_target_pairs={{0,1},{1,0},{2,3},{3,2},{4,5},{5,4},{6,7},{7,6},{8,9},{9,8},{10,11... | collective-permute-start | bytes 393224 | tf_op jit(solution)/shard_map/ppermute | solution.py:31
  5.7 1.8 %leaf.5 = (bf16[16,32,128]{2,1,0:T(8,128)(2,1)S(1)}, bf16[16,32,128]{2,1,0:T(8,128)(2,1)S(1)}, bf16[16,64,256]{2,1,0:T(8,128)(2,1)S(1)}, bf16[16,256,128]{2,1,0:T(8,128)(2,1)S(1)}, s32[16,128]{1,0:T(8,128)S(1)}) custom-call(bf16[16,64,256]{2,1,0:T(8,128)(2,1)S(1)} %get-tuple-element.54.refs_0_, bf16[16,256,128]{2,1,0:T(8,128)(2,1)S(1)} %get-tuple-element.55.refs_1_, ...), custom_call_target="tpu_custom_call" | custom-call | tf_op jit(solution)/shard_map/leaf/pallas_call | solution.py:332
  7.5 0.1 collective-permute-start
  7.6 1.9 %collective-permute-done.1.refs_1_ = bf16[16,32,128]{2,1,0:T(8,128)(2,1)S(1)} collective-permute-done((bf16[16,32,128]{2,1,0:T(8,128)(2,1)S(1)}, bf16[16,32,128]{2,1,0:T(8,128)(2,1)S(1)}, u32[]{:S(2)}, u32[]{:S(2)}) %collective-permute-start.1) | collective-permute-done | bytes 131104 | tf_op jit(solution)/shard_map/ppermute | solution.py:31
  9.5 1.4 %level.8 = (bf16[16,32,128]{2,1,0:T(8,128)(2,1)S(1)}, bf16[16,32,128]{2,1,0:T(8,128)(2,1)S(1)}, bf16[16,64,256]{2,1,0:T(8,128)(2,1)S(1)}, bf16[16,256,128]{2,1,0:T(8,128)(2,1)S(1)}, s32[16,128]{1,0:T(8,128)S(1)}) custom-call(bf16[16,32,128]{2,1,0:T(8,128)(2,1)S(1)} %get-tuple-element.57.refs_3_.refs_0_, ...), custom_call_target="tpu_custom_call" | custom-call | tf_op jit(solution)/shard_map/level/pallas_call | solution.py:346
  10.9 1.6 %collective-permute-start.4 = (bf16[16,32,128]{2,1,0:T(8,128)(2,1)S(1)}, bf16[16,32,128]{2,1,0:T(8,128)(2,1)S(1)}, u32[]{:S(2)}, u32[]{:S(2)}) collective-permute-start(bf16[16,32,128]{2,1,0:T(8,128)(2,1)S(1)} %get-tuple-element.72), channel_id=1, source_target_pairs={{0,2},{1,3},{2,0},{3,1},{4,6},{5,7},{6,4},{7,5},{8,10},{9,11},{10,... | collective-permute-start | bytes 393224 | tf_op jit(solution)/shard_map/ppermute | solution.py:31
  12.5 0.6 leaf.6
  13.1 2.3 %collective-permute-start.3 = (bf16[16,32,128]{2,1,0:T(8,128)(2,1)S(1)}, bf16[16,32,128]{2,1,0:T(8,128)(2,1)S(1)}, u32[]{:S(2)}, u32[]{:S(2)}) collective-permute-start(bf16[16,32,128]{2,1,0:T(8,128)(2,1)S(1)} %get-tuple-element.68), channel_id=1, source_target_pairs={{0,1},{1,0},{2,3},{3,2},{4,5},{5,4},{6,7},{7,6},{8,9},{9,8},{10,11... | collective-permute-start | bytes 393224 | tf_op jit(solution)/shard_map/ppermute | solution.py:31
  15.4 0.4 level.9
  15.8 0.8 %collective-permute-start.2 = (bf16[16,32,128]{2,1,0:T(8,128)(2,1)S(1)}, bf16[16,32,128]{2,1,0:T(8,128)(2,1)S(1)}, u32[]{:S(2)}, u32[]{:S(2)}) collective-permute-start(bf16[16,32,128]{2,1,0:T(8,128)(2,1)S(1)} %get-tuple-element.67), channel_id=1, source_target_pairs={{0,2},{1,3},{2,0},{3,1},{4,6},{5,7},{6,4},{7,5},{8,10},{9,11},{10,... | collective-permute-start | bytes 393224 | tf_op jit(solution)/shard_map/ppermute | solution.py:31
  16.6 0.4 level.10
  17.0 2.4 %collective-permute-start.8 = (bf16[16,32,128]{2,1,0:T(8,128)(2,1)S(1)}, bf16[16,32,128]{2,1,0:T(8,128)(2,1)S(1)}, u32[]{:S(2)}, u32[]{:S(2)}) collective-permute-start(bf16[16,32,128]{2,1,0:T(8,128)(2,1)S(1)} %get-tuple-element.80), channel_id=1, source_target_pairs={{0,4},{1,5},{2,6},{3,7},{4,0},{5,1},{6,2},{7,3},{8,12},{9,13},{10,... | collective-permute-start | bytes 393224 | tf_op jit(solution)/shard_map/ppermute | solution.py:31
  19.4 0.6 leaf.7
  20.0 3.3 %collective-permute-start.7 = (bf16[16,32,128]{2,1,0:T(8,128)(2,1)S(1)}, bf16[16,32,128]{2,1,0:T(8,128)(2,1)S(1)}, u32[]{:S(2)}, u32[]{:S(2)}) collective-permute-start(bf16[16,32,128]{2,1,0:T(8,128)(2,1)S(1)} %get-tuple-element.79), channel_id=1, source_target_pairs={{0,1},{1,0},{2,3},{3,2},{4,5},{5,4},{6,7},{7,6},{8,9},{9,8},{10,11... | collective-permute-start | bytes 393224 | tf_op jit(solution)/shard_map/ppermute | solution.py:31
  23.3 0.0 collective-permute-done.3.refs_1_
  23.3 0.4 level.11
  23.7 0.0 copy-start
  23.7 1.1 %collective-permute-start.6 = (bf16[16,32,128]{2,1,0:T(8,128)(2,1)S(1)}, bf16[16,32,128]{2,1,0:T(8,128)(2,1)S(1)}, u32[]{:S(2)}, u32[]{:S(2)}) collective-permute-start(bf16[16,32,128]{2,1,0:T(8,128)(2,1)S(1)} %get-tuple-element.78), channel_id=1, source_target_pairs={{0,2},{1,3},{2,0},{3,1},{4,6},{5,7},{6,4},{7,5},{8,10},{9,11},{10,... | collective-permute-start | bytes 393224 | tf_op jit(solution)/shard_map/ppermute | solution.py:31
  24.8 0.0 collective-permute-done.2.refs_1_
  24.8 0.4 level.12
  25.2 0.7 %collective-permute-start.5 = (bf16[16,32,128]{2,1,0:T(8,128)(2,1)S(1)}, bf16[16,32,128]{2,1,0:T(8,128)(2,1)S(1)}, u32[]{:S(2)}, u32[]{:S(2)}) collective-permute-start(bf16[16,32,128]{2,1,0:T(8,128)(2,1)S(1)} %get-tuple-element.77), channel_id=1, source_target_pairs={{0,4},{1,5},{2,6},{3,7},{4,0},{5,1},{6,2},{7,3},{8,12},{9,13},{10,... | collective-permute-start | bytes 393224 | tf_op jit(solution)/shard_map/ppermute | solution.py:31
  26.0 1.4 %last.4 = (bf16[8,2,32,128]{3,2,1,0:T(8,128)(2,1)S(1)}, bf16[8,2,32,128]{3,2,1,0:T(8,128)(2,1)S(1)}, bf16[8,2,32,128]{3,2,1,0:T(8,128)(2,1)S(1)}, bf16[8,2,32,128]{3,2,1,0:T(8,128)(2,1)S(1)}) custom-call(bf16[16,32,128]{2,1,0:T(8,128)(2,1)S(1)} %get-tuple-element.73.refs_3_.own_in, bf16[16,32,128]{2,1,0:T(8,128)(2,1)S(1)} %collective-permute-done.8.came_in, ...), custom_call_target="tpu_custom_call" | custom-call | tf_op jit(solution)/shard_map/last/pallas_call | solution.py:360
  27.4 0.4 level.13
  27.8 2.1 %collective-permute-start.12 = (bf16[16,32,128]{2,1,0:T(8,128)(2,1)S(1)}, bf16[16,32,128]{2,1,0:T(8,128)(2,1)S(1)}, u32[]{:S(2)}, u32[]{:S(2)}) collective-permute-start(bf16[16,32,128]{2,1,0:T(8,128)(2,1)S(1)} %get-tuple-element.91), channel_id=1, source_target_pairs={{0,2},{1,3},{2,0},{3,1},{4,6},{5,7},{6,4},{7,5},{8,10},{9,11},{10,... | collective-permute-start | bytes 393224 | tf_op jit(solution)/shard_map/ppermute | solution.py:31
  29.9 1.6 %collective-permute-done.6.refs_1_ = bf16[16,32,128]{2,1,0:T(8,128)(2,1)S(1)} collective-permute-done((bf16[16,32,128]{2,1,0:T(8,128)(2,1)S(1)}, bf16[16,32,128]{2,1,0:T(8,128)(2,1)S(1)}, u32[]{:S(2)}, u32[]{:S(2)}) %collective-permute-start.6) | collective-permute-done | bytes 131104 | tf_op jit(solution)/shard_map/ppermute | solution.py:31
  31.5 0.4 level.14
  31.9 1.7 %collective-permute-start.14 = (bf16[16,32,128]{2,1,0:T(8,128)(2,1)S(1)}, bf16[16,32,128]{2,1,0:T(8,128)(2,1)S(1)}, u32[]{:S(2)}, u32[]{:S(2)}) collective-permute-start(bf16[16,32,128]{2,1,0:T(8,128)(2,1)S(1)} %get-tuple-element.94), channel_id=1, source_target_pairs={{0,4},{1,5},{2,6},{3,7},{4,0},{5,1},{6,2},{7,3},{8,12},{9,13},{10,... | collective-permute-start | bytes 393224 | tf_op jit(solution)/shard_map/ppermute | solution.py:31
  33.6 0.6 %collective-permute-done.5.came_in = bf16[16,32,128]{2,1,0:T(8,128)(2,1)S(1)} collective-permute-done((bf16[16,32,128]{2,1,0:T(8,128)(2,1)S(1)}, bf16[16,32,128]{2,1,0:T(8,128)(2,1)S(1)}, u32[]{:S(2)}, u32[]{:S(2)}) %collective-permute-start.5) | collective-permute-done | bytes 131104 | tf_op jit(solution)/shard_map/ppermute | solution.py:31
  34.2 1.4 %last.5 = (bf16[8,2,32,128]{3,2,1,0:T(8,128)(2,1)S(1)}, bf16[8,2,32,128]{3,2,1,0:T(8,128)(2,1)S(1)}, bf16[8,2,32,128]{3,2,1,0:T(8,128)(2,1)S(1)}, bf16[8,2,32,128]{3,2,1,0:T(8,128)(2,1)S(1)}) custom-call(bf16[16,32,128]{2,1,0:T(8,128)(2,1)S(1)} %get-tuple-element.76._.own_in, ...), custom_call_target="tpu_custom_call", output_to_operand_aliasing={{0}: (5, {}), {1}: (6, {}), {2}: (7, {}), {3}: (8, {})} | custom-call | tf_op jit(solution)/shard_map/last/pallas_call | solution.py:360
  35.6 0.0 collective-permute-done.12.refs_1_
  35.6 0.4 level.15
  36.1 1.1 %collective-permute-start.13 = (bf16[16,32,128]{2,1,0:T(8,128)(2,1)S(1)}, bf16[16,32,128]{2,1,0:T(8,128)(2,1)S(1)}, u32[]{:S(2)}, u32[]{:S(2)}) collective-permute-start(bf16[16,32,128]{2,1,0:T(8,128)(2,1)S(1)} %get-tuple-element.93), channel_id=1, source_target_pairs={{0,4},{1,5},{2,6},{3,7},{4,0},{5,1},{6,2},{7,3},{8,12},{9,13},{10,... | collective-permute-start | bytes 393224 | tf_op jit(solution)/shard_map/ppermute | solution.py:31
  37.2 0.0 collective-permute-start.9
  37.2 1.4 %collective-permute-start.10 = (bf16[8,2,32,128]{3,2,1,0:T(8,128)(2,1)S(1)}, bf16[8,2,32,128]{3,2,1,0:T(8,128)(2,1)S(1)}, u32[]{:S(2)}, u32[]{:S(2)}) collective-permute-start(bf16[8,2,32,128]{3,2,1,0:T(8,128)(2,1)S(1)} %get-tuple-element.89), channel_id=1, source_target_pairs={{0,16},{8,24},{16,0},{24,8},{1,17},{9,25},{17,1},{25,9},{2,18},{10... | collective-permute-start | bytes 393224 | tf_op jit(solution)/shard_map/ppermute | solution.py:31
  38.6 0.5 collective-permute-start.11
  39.0 0.6 %collective-permute-done.14.came_in = bf16[16,32,128]{2,1,0:T(8,128)(2,1)S(1)} collective-permute-done((bf16[16,32,128]{2,1,0:T(8,128)(2,1)S(1)}, bf16[16,32,128]{2,1,0:T(8,128)(2,1)S(1)}, u32[]{:S(2)}, u32[]{:S(2)}) %collective-permute-start.14) | collective-permute-done | bytes 131104 | tf_op jit(solution)/shard_map/ppermute | solution.py:31
  39.7 1.4 %last.6 = (bf16[8,2,32,128]{3,2,1,0:T(8,128)(2,1)S(1)}, bf16[8,2,32,128]{3,2,1,0:T(8,128)(2,1)S(1)}, bf16[8,2,32,128]{3,2,1,0:T(8,128)(2,1)S(1)}, bf16[8,2,32,128]{3,2,1,0:T(8,128)(2,1)S(1)}) custom-call(bf16[16,32,128]{2,1,0:T(8,128)(2,1)S(1)} %get-tuple-element.83._.own_in, bf16[16,32,128]{2,1,0:T(8,128)(2,1)S(1)} %collective-permute-done.14.came_in, ...), custom_call_target="tpu_custom_call" | custom-call | tf_op jit(solution)/shard_map/last/pallas_call | solution.py:360
  41.1 2.3 %collective-permute-done.13.came_in = bf16[16,32,128]{2,1,0:T(8,128)(2,1)S(1)} collective-permute-done((bf16[16,32,128]{2,1,0:T(8,128)(2,1)S(1)}, bf16[16,32,128]{2,1,0:T(8,128)(2,1)S(1)}, u32[]{:S(2)}, u32[]{:S(2)}) %collective-permute-start.13) | collective-permute-done | bytes 131104 | tf_op jit(solution)/shard_map/ppermute | solution.py:31
  43.4 1.6 %last.7 = (bf16[8,2,32,128]{3,2,1,0:T(8,128)(2,1)S(1)}, bf16[8,2,32,128]{3,2,1,0:T(8,128)(2,1)S(1)}, bf16[8,2,32,128]{3,2,1,0:T(8,128)(2,1)S(1)}, bf16[8,2,32,128]{3,2,1,0:T(8,128)(2,1)S(1)}) custom-call(bf16[16,32,128]{2,1,0:T(8,128)(2,1)S(1)} %get-tuple-element.92._.own_in, ...), custom_call_target="tpu_custom_call", output_to_operand_aliasing={{0}: (5, {}), {1}: (6, {}), {2}: (7, {}), {3}: (8, {})} | custom-call | tf_op jit(solution)/shard_map/last/pallas_call | solution.py:360
  45.0 0.1 collective-permute-start.15
  45.1 1.3 %collective-permute-start.16 = (bf16[8,2,32,128]{3,2,1,0:T(8,128)(2,1)S(1)}, bf16[8,2,32,128]{3,2,1,0:T(8,128)(2,1)S(1)}, u32[]{:S(2)}, u32[]{:S(2)}) collective-permute-start(bf16[8,2,32,128]{3,2,1,0:T(8,128)(2,1)S(1)} %get-tuple-element.101), channel_id=1, source_target_pairs={{0,16},{8,24},{16,0},{24,8},{1,17},{9,25},{17,1},{25,9},{2,18},{10... | collective-permute-start | bytes 393224 | tf_op jit(solution)/shard_map/ppermute | solution.py:31
  46.4 0.6 collective-permute-start.17
  47.0 4.3 %table.1.refs_8_ = bf16[2,256,4224]{2,1,0:T(8,128)(2,1)S(1)} custom-call(s32[256]{0:T(256)S(1)} %copy-done.1, bf16[8,2,32,128]{3,2,1,0:T(8,128)(2,1)S(1)} %get-tuple-element.99.refs_0_.refs_4_), custom_call_target="tpu_custom_call" | custom-call | tf_op jit(solution)/shard_map/table/pallas_call | solution.py:203
  51.3 0.0 collective-permute-done.10.refs_2_
  51.3 0.2 collective-permute-done.16.refs_6_
  51.5 1.9 %collective-permute-done.17.refs_7_ = bf16[8,2,32,128]{3,2,1,0:T(8,128)(2,1)S(1)} collective-permute-done((bf16[8,2,32,128]{3,2,1,0:T(8,128)(2,1)S(1)}, bf16[8,2,32,128]{3,2,1,0:T(8,128)(2,1)S(1)}, u32[]{:S(2)}, u32[]{:S(2)}) %collective-permute-start.17) | collective-permute-done | bytes 131104 | tf_op jit(solution)/shard_map/ppermute | solution.py:31
  53.4 8.7 %synthesis.1 = bf16[8,128,8192]{2,1,0:T(8,128)(2,1)} custom-call(bf16[8,2,32,128]{3,2,1,0:T(8,128)(2,1)S(1)} %get-tuple-element.87.refs_3_.refs_0_, bf16[8,2,32,128]{3,2,1,0:T(8,128)(2,1)S(1)} %collective-permute-done.9.refs_1_, bf16[8,2,32,128]{3,2,1,0:T(8,128)(2,1)S(1)} %collective-permute-done.10.refs_2_, ...), custom_call_target="tpu_custom_call" | custom-call | tf_op jit(solution)/shard_map/synthesis/pallas_call | solution.py:279
  (16 shorter events, 0.0 us)
Async XLA Ops:
  0.0 9.5 %slice-start = ((s8[6291456]{0:T(1024)(128)(4,1)}), s8[4194304]{0:T(1024)(128)(4,1)S(1)}, s32[]{:S(2)}) async-start(s8[6291456]{0:T(1024)(128)(4,1)} %bitcast.1), calls=%async_computation | async-start | bytes 8388608
  0.0 9.5 %slice-start.1 = ((s8[6291456]{0:T(1024)(128)(4,1)}), s8[2097152]{0:T(1024)(128)(4,1)S(1)}, s32[]{:S(2)}) async-start(s8[6291456]{0:T(1024)(128)(4,1)} %bitcast.1), calls=%async_computation.1 | async-start | bytes 4194304
  2.7 6.8 %collective-permute-start.1 = (bf16[16,32,128]{2,1,0:T(8,128)(2,1)S(1)}, bf16[16,32,128]{2,1,0:T(8,128)(2,1)S(1)}, u32[]{:S(2)}, u32[]{:S(2)}) collective-permute-start(bf16[16,32,128]{2,1,0:T(8,128)(2,1)S(1)} %get-tuple-element.63), channel_id=1, source_target_pairs={{0,1},{1,0},{2,3},{3,2},{4,5},{5,4},{6,7},{7,6},{8,9},{9,8},{10,11... | collective-permute-start | bytes 393224 | tf_op jit(solution)/shard_map/ppermute | solution.py:31
  7.5 7.9 %collective-permute-start = (bf16[16,32,128]{2,1,0:T(8,128)(2,1)S(1)}, bf16[16,32,128]{2,1,0:T(8,128)(2,1)S(1)}, u32[]{:S(2)}, u32[]{:S(2)}) collective-permute-start(bf16[16,32,128]{2,1,0:T(8,128)(2,1)S(1)} %get-tuple-element.59), channel_id=1, source_target_pairs={{0,1},{1,0},{2,3},{3,2},{4,5},{5,4},{6,7},{7,6},{8,9},{9,8},{10,11... | collective-permute-start | bytes 393224 | tf_op jit(solution)/shard_map/ppermute | solution.py:31
  10.9 5.7 %collective-permute-start.4 = (bf16[16,32,128]{2,1,0:T(8,128)(2,1)S(1)}, bf16[16,32,128]{2,1,0:T(8,128)(2,1)S(1)}, u32[]{:S(2)}, u32[]{:S(2)}) collective-permute-start(bf16[16,32,128]{2,1,0:T(8,128)(2,1)S(1)} %get-tuple-element.72), channel_id=1, source_target_pairs={{0,2},{1,3},{2,0},{3,1},{4,6},{5,7},{6,4},{7,5},{8,10},{9,11},{10,... | collective-permute-start | bytes 393224 | tf_op jit(solution)/shard_map/ppermute | solution.py:31
  13.1 10.2 %collective-permute-start.3 = (bf16[16,32,128]{2,1,0:T(8,128)(2,1)S(1)}, bf16[16,32,128]{2,1,0:T(8,128)(2,1)S(1)}, u32[]{:S(2)}, u32[]{:S(2)}) collective-permute-start(bf16[16,32,128]{2,1,0:T(8,128)(2,1)S(1)} %get-tuple-element.68), channel_id=1, source_target_pairs={{0,1},{1,0},{2,3},{3,2},{4,5},{5,4},{6,7},{7,6},{8,9},{9,8},{10,11... | collective-permute-start | bytes 393224 | tf_op jit(solution)/shard_map/ppermute | solution.py:31
  15.8 9.0 %collective-permute-start.2 = (bf16[16,32,128]{2,1,0:T(8,128)(2,1)S(1)}, bf16[16,32,128]{2,1,0:T(8,128)(2,1)S(1)}, u32[]{:S(2)}, u32[]{:S(2)}) collective-permute-start(bf16[16,32,128]{2,1,0:T(8,128)(2,1)S(1)} %get-tuple-element.67), channel_id=1, source_target_pairs={{0,2},{1,3},{2,0},{3,1},{4,6},{5,7},{6,4},{7,5},{8,10},{9,11},{10,... | collective-permute-start | bytes 393224 | tf_op jit(solution)/shard_map/ppermute | solution.py:31
  17.0 8.9 %collective-permute-start.8 = (bf16[16,32,128]{2,1,0:T(8,128)(2,1)S(1)}, bf16[16,32,128]{2,1,0:T(8,128)(2,1)S(1)}, u32[]{:S(2)}, u32[]{:S(2)}) collective-permute-start(bf16[16,32,128]{2,1,0:T(8,128)(2,1)S(1)} %get-tuple-element.80), channel_id=1, source_target_pairs={{0,4},{1,5},{2,6},{3,7},{4,0},{5,1},{6,2},{7,3},{8,12},{9,13},{10,... | collective-permute-start | bytes 393224 | tf_op jit(solution)/shard_map/ppermute | solution.py:31
  20.0 7.4 %collective-permute-start.7 = (bf16[16,32,128]{2,1,0:T(8,128)(2,1)S(1)}, bf16[16,32,128]{2,1,0:T(8,128)(2,1)S(1)}, u32[]{:S(2)}, u32[]{:S(2)}) collective-permute-start(bf16[16,32,128]{2,1,0:T(8,128)(2,1)S(1)} %get-tuple-element.79), channel_id=1, source_target_pairs={{0,1},{1,0},{2,3},{3,2},{4,5},{5,4},{6,7},{7,6},{8,9},{9,8},{10,11... | collective-permute-start | bytes 393224 | tf_op jit(solution)/shard_map/ppermute | solution.py:31
  23.7 2.2 %copy-start = (bf16[64,128,128]{2,1,0:T(8,128)(2,1)S(1)}, bf16[64,128,128]{2,1,0:T(8,128)(2,1)}, u32[]{:S(2)}) copy-start(bf16[64,128,128]{2,1,0:T(8,128)(2,1)} %lats.7) | copy-start | bytes 6291460
  23.7 7.8 %collective-permute-start.6 = (bf16[16,32,128]{2,1,0:T(8,128)(2,1)S(1)}, bf16[16,32,128]{2,1,0:T(8,128)(2,1)S(1)}, u32[]{:S(2)}, u32[]{:S(2)}) collective-permute-start(bf16[16,32,128]{2,1,0:T(8,128)(2,1)S(1)} %get-tuple-element.78), channel_id=1, source_target_pairs={{0,2},{1,3},{2,0},{3,1},{4,6},{5,7},{6,4},{7,5},{8,10},{9,11},{10,... | collective-permute-start | bytes 393224 | tf_op jit(solution)/shard_map/ppermute | solution.py:31
  25.2 8.9 %collective-permute-start.5 = (bf16[16,32,128]{2,1,0:T(8,128)(2,1)S(1)}, bf16[16,32,128]{2,1,0:T(8,128)(2,1)S(1)}, u32[]{:S(2)}, u32[]{:S(2)}) collective-permute-start(bf16[16,32,128]{2,1,0:T(8,128)(2,1)S(1)} %get-tuple-element.77), channel_id=1, source_target_pairs={{0,4},{1,5},{2,6},{3,7},{4,0},{5,1},{6,2},{7,3},{8,12},{9,13},{10,... | collective-permute-start | bytes 393224 | tf_op jit(solution)/shard_map/ppermute | solution.py:31
  27.8 7.8 %collective-permute-start.12 = (bf16[16,32,128]{2,1,0:T(8,128)(2,1)S(1)}, bf16[16,32,128]{2,1,0:T(8,128)(2,1)S(1)}, u32[]{:S(2)}, u32[]{:S(2)}) collective-permute-start(bf16[16,32,128]{2,1,0:T(8,128)(2,1)S(1)} %get-tuple-element.91), channel_id=1, source_target_pairs={{0,2},{1,3},{2,0},{3,1},{4,6},{5,7},{6,4},{7,5},{8,10},{9,11},{10,... | collective-permute-start | bytes 393224 | tf_op jit(solution)/shard_map/ppermute | solution.py:31
  31.9 7.8 %collective-permute-start.14 = (bf16[16,32,128]{2,1,0:T(8,128)(2,1)S(1)}, bf16[16,32,128]{2,1,0:T(8,128)(2,1)S(1)}, u32[]{:S(2)}, u32[]{:S(2)}) collective-permute-start(bf16[16,32,128]{2,1,0:T(8,128)(2,1)S(1)} %get-tuple-element.94), channel_id=1, source_target_pairs={{0,4},{1,5},{2,6},{3,7},{4,0},{5,1},{6,2},{7,3},{8,12},{9,13},{10,... | collective-permute-start | bytes 393224 | tf_op jit(solution)/shard_map/ppermute | solution.py:31
  36.1 7.3 %collective-permute-start.13 = (bf16[16,32,128]{2,1,0:T(8,128)(2,1)S(1)}, bf16[16,32,128]{2,1,0:T(8,128)(2,1)S(1)}, u32[]{:S(2)}, u32[]{:S(2)}) collective-permute-start(bf16[16,32,128]{2,1,0:T(8,128)(2,1)S(1)} %get-tuple-element.93), channel_id=1, source_target_pairs={{0,4},{1,5},{2,6},{3,7},{4,0},{5,1},{6,2},{7,3},{8,12},{9,13},{10,... | collective-permute-start | bytes 393224 | tf_op jit(solution)/shard_map/ppermute | solution.py:31
  37.2 9.2 %collective-permute-start.9 = (bf16[8,2,32,128]{3,2,1,0:T(8,128)(2,1)S(1)}, bf16[8,2,32,128]{3,2,1,0:T(8,128)(2,1)S(1)}, u32[]{:S(2)}, u32[]{:S(2)}) collective-permute-start(bf16[8,2,32,128]{3,2,1,0:T(8,128)(2,1)S(1)} %get-tuple-element.88), channel_id=1, source_target_pairs={{0,8},{8,0},{16,24},{24,16},{1,9},{9,1},{17,25},{25,17},{2,10},{10... | collective-permute-start | bytes 393224 | tf_op jit(solution)/shard_map/ppermute | solution.py:31
  37.2 14.1 %collective-permute-start.10 = (bf16[8,2,32,128]{3,2,1,0:T(8,128)(2,1)S(1)}, bf16[8,2,32,128]{3,2,1,0:T(8,128)(2,1)S(1)}, u32[]{:S(2)}, u32[]{:S(2)}) collective-permute-start(bf16[8,2,32,128]{3,2,1,0:T(8,128)(2,1)S(1)} %get-tuple-element.89), channel_id=1, source_target_pairs={{0,16},{8,24},{16,0},{24,8},{1,17},{9,25},{17,1},{25,9},{2,18},{10... | collective-permute-start | bytes 393224 | tf_op jit(solution)/shard_map/ppermute | solution.py:31
  38.6 12.7 %collective-permute-start.11 = (bf16[8,2,32,128]{3,2,1,0:T(8,128)(2,1)S(1)}, bf16[8,2,32,128]{3,2,1,0:T(8,128)(2,1)S(1)}, u32[]{:S(2)}, u32[]{:S(2)}) collective-permute-start(bf16[8,2,32,128]{3,2,1,0:T(8,128)(2,1)S(1)} %get-tuple-element.90), channel_id=1, source_target_pairs={{0,24},{8,16},{16,8},{24,0},{1,25},{9,17},{17,9},{25,1},{2,26},{10... | collective-permute-start | bytes 393224 | tf_op jit(solution)/shard_map/ppermute | solution.py:31
  43.4 3.6 %copy-start.1 = (s32[256]{0:T(256)S(1)}, s32[256]{0:T(256)}, u32[]{:S(2)}) copy-start(s32[256]{0:T(256)} %map_ref.1) | copy-start | bytes 3076
  45.0 6.2 %collective-permute-start.15 = (bf16[8,2,32,128]{3,2,1,0:T(8,128)(2,1)S(1)}, bf16[8,2,32,128]{3,2,1,0:T(8,128)(2,1)S(1)}, u32[]{:S(2)}, u32[]{:S(2)}) collective-permute-start(bf16[8,2,32,128]{3,2,1,0:T(8,128)(2,1)S(1)} %get-tuple-element.100), channel_id=1, source_target_pairs={{0,8},{8,0},{16,24},{24,16},{1,9},{9,1},{17,25},{25,17},{2,10},{10... | collective-permute-start | bytes 393224 | tf_op jit(solution)/shard_map/ppermute | solution.py:31
  45.1 6.4 %collective-permute-start.16 = (bf16[8,2,32,128]{3,2,1,0:T(8,128)(2,1)S(1)}, bf16[8,2,32,128]{3,2,1,0:T(8,128)(2,1)S(1)}, u32[]{:S(2)}, u32[]{:S(2)}) collective-permute-start(bf16[8,2,32,128]{3,2,1,0:T(8,128)(2,1)S(1)} %get-tuple-element.101), channel_id=1, source_target_pairs={{0,16},{8,24},{16,0},{24,8},{1,17},{9,25},{17,1},{25,9},{2,18},{10... | collective-permute-start | bytes 393224 | tf_op jit(solution)/shard_map/ppermute | solution.py:31
  46.4 7.0 %collective-permute-start.17 = (bf16[8,2,32,128]{3,2,1,0:T(8,128)(2,1)S(1)}, bf16[8,2,32,128]{3,2,1,0:T(8,128)(2,1)S(1)}, u32[]{:S(2)}, u32[]{:S(2)}) collective-permute-start(bf16[8,2,32,128]{3,2,1,0:T(8,128)(2,1)S(1)} %get-tuple-element.102), channel_id=1, source_target_pairs={{0,24},{8,16},{16,8},{24,0},{1,25},{9,17},{17,9},{25,1},{2,26},{10... | collective-permute-start | bytes 393224 | tf_op jit(solution)/shard_map/ppermute | solution.py:31

commit v6 on v5

--- a/solution.py
+++ b/solution.py
@@ -9,15 +9,16 @@
 
 NLON = 8192
 SHARES = (1, 1, 1, 1)
-GROUPS = ((0, 1), (2, 3))
+GROUPS = ((0, 1), (2,), (3,))
 TURN = -1
 BLOCK = 64
-TABLE_AT = ()
+TABLE_AT = ((3, 3),)
 LANES = 128
-PARTS = 4
+PARTS = 2
 TILE = 512
 ROWS = 256
 SLOTS = 3
+UNROLL = 4
 CHEAP = pl.CostEstimate(flops=0, bytes_accessed=0, transcendentals=0)
 IN_ANY = pl.BlockSpec(memory_space=pl.ANY)
 IN_VMEM = pl.BlockSpec(memory_space=pltpu.VMEM)
@@ -133,7 +134,7 @@
 
 def last_kernel(first, num, offset, own_in, came_in, maps, lats, _, *refs):
     peers = lax.axis_size("wave")
-    out_refs, block_ref = refs[-1 - peers : -1], refs[-1]
+    out_refs, (block_ref, moved_ref) = refs[-2 - peers : -2], refs[-2:]
     count, fields = own_in.shape[:2]
     share = fields // peers
     for g in range(count):
@@ -155,12 +156,9 @@
             moved = moved.reshape(tile, tile, rows)
             part, field = c // fields, c % fields
             for at in range(0, tile, share):
-                peer = (field + at) // share
-                for step in range(peers):
-
-                    @pl.when((me ^ peer) == step)
-                    def _():
-                        out_refs[step][:, part, offset + g : offset + g + tile, :] = moved[at : at + share]
+                moved_ref[(field + at) // share, :, part, g : g + tile, :] = moved[at : at + share]
+    for step, out_ref in enumerate(out_refs):
+        out_ref[:, :, offset : offset + count, :] = moved_ref[me ^ step]
 
 
 def table_kernel(lon_count, slots, sizes, first, count, map_ref, *refs):
@@ -267,7 +265,7 @@
             copy.start()
         return carry
 
-    lax.fori_loop(0, steps, step, 0)
+    lax.fori_loop(0, steps, step, 0, unroll=UNROLL)
     for i in range(max(0, steps - slots), steps):
         for copy in copies(i):
             copy.wait()
@@ -363,7 +361,10 @@
             out_specs=[IN_VMEM] * peers,
             out_shape=[piece] * peers,
             input_output_aliases={5 + n: n for n in range(len(begun))},
-            scratch_shapes=[pltpu.VMEM((count, columns, rows), jnp.bfloat16)],
+            scratch_shapes=[
+                pltpu.VMEM((count, columns, rows), jnp.bfloat16),
+                pltpu.VMEM((peers, fields // peers, 2, count, rows), jnp.bfloat16),
+            ],
             cost_estimate=CHEAP,
             compiler_params=params,
             name="last",

time: 62.6 us -> 61.8 us (0.987)
  Pallas kernels: 28.8 us -> 26.7 us
  starting transfers between devices: 23.9 us -> 24.8 us
    pallas_call x4, Pallas kernels: 5.95 us -> 3.44 us  [last(): pl.pallas_call(functools.partial(last_kernel, firsts[chunk], levels - 1,...]
    ppermute x18 -> x21, starting transfers between devices: 23.9 us -> 24.8 us  [exchange(): lax.ppermute(shard, axis, [(i, i ^ step) for i in range(lax.axis_size(axi...]
    pallas_call x1 -> x2, Pallas kernels: 4.27 us -> 5.01 us  [wave_table(): pl.pallas_call(functools.partial(table_kernel, lon_count, slots, sizes, f...]
    ppermute x18 -> x21, waiting for transfers between devices: 9.09 us -> 9.7 us  [exchange(): lax.ppermute(shard, axis, [(i, i ^ step) for i in range(lax.axis_size(axi...]
  transfers between devices with their start and end apart: 18 -> 21, of which waited for: 7 -> 7; matrix products, arithmetic and copies ran while one was open for 0% -> 0% of each run, Pallas kernels for 28% -> 25%
where the time goes in v6:
time: 61.8 us; the launch traced here: 61.6 us
  Pallas kernels  26.7 us (43%)
  starting transfers between devices  24.8 us (40%)
  waiting for transfers between devices  9.7 us (16%)
    ppermute x21, starting transfers between devices, exchange(): lax.ppermute(shard, axis, [(i, i ^ step) for i in range(lax.axis_size(axi...  24.8 us
    ppermute x21, waiting for transfers between devices, exchange(): lax.ppermute(shard, axis, [(i, i ^ step) for i in range(lax.axis_size(axi...  9.7 us
    pallas_call x1, Pallas kernels, synthesis(): pl.pallas_call(synthesis_kernel, in_specs=[IN_VMEM] * (len(blocks) + 1),...  8.62 us
    pallas_call x4, Pallas kernels, leaf(): pl.pallas_call(functools.partial(leaf_kernel, places), in_specs=[IN_VMEM...  5.37 us
    pallas_call x2, Pallas kernels, wave_table(): pl.pallas_call(functools.partial(table_kernel, lon_count, slots, sizes, f...  5.01 us
    pallas_call x8, Pallas kernels, level(): pl.pallas_call(functools.partial(level_kernel, firsts[chunk], num, places...  4.29 us
    pallas_call x4, Pallas kernels, last(): pl.pallas_call(functools.partial(last_kernel, firsts[chunk], levels - 1,...  3.44 us
  transfers between devices with their start and end apart: 21, of which 7 were waited for; matrix products, arithmetic and copies ran while one was open for 0% of the time, Pallas kernels for 25%

profile of v6, /device:TPU:0, one launch (start us, length us, event | category | flops | bytes accessed | tf_op | source)
XLA Modules:
  0.0 61.6 jit_solution(13141736622555030415)
XLA Ops:
  0.0 2.4 %leaf.4 = (bf16[16,32,128]{2,1,0:T(8,128)(2,1)S(1)}, bf16[16,32,128]{2,1,0:T(8,128)(2,1)S(1)}, bf16[16,64,256]{2,1,0:T(8,128)(2,1)S(1)}, bf16[16,256,128]{2,1,0:T(8,128)(2,1)S(1)}, s32[16,128]{1,0:T(8,128)S(1)}) custom-call(bf16[64,64,256]{2,1,0:T(8,128)(2,1)} %bitcast.3, bf16[64,256,128]{2,1,0:T(8,128)(2,1)} %refs_5_.5, s32[64,128]{1,0:T(8,128)} %refs_6_.5, ...), custom_call_target="tpu_custom_call" | custom-call | tf_op jit(solution)/shard_map/leaf/pallas_call | solution.py:330
  2.5 3.0 %collective-permute-start.1 = (bf16[16,32,128]{2,1,0:T(8,128)(2,1)S(1)}, bf16[16,32,128]{2,1,0:T(8,128)(2,1)S(1)}, u32[]{:S(2)}, u32[]{:S(2)}) collective-permute-start(bf16[16,32,128]{2,1,0:T(8,128)(2,1)S(1)} %get-tuple-element.63), channel_id=1, source_target_pairs={{0,1},{1,0},{2,3},{3,2},{4,5},{5,4},{6,7},{7,6},{8,9},{9,8},{10,11... | collective-permute-start | bytes 393224 | tf_op jit(solution)/shard_map/ppermute | solution.py:32
  5.5 1.8 %leaf.5 = (bf16[16,32,128]{2,1,0:T(8,128)(2,1)S(1)}, bf16[16,32,128]{2,1,0:T(8,128)(2,1)S(1)}, bf16[16,64,256]{2,1,0:T(8,128)(2,1)S(1)}, bf16[16,256,128]{2,1,0:T(8,128)(2,1)S(1)}, s32[16,128]{1,0:T(8,128)S(1)}) custom-call(bf16[16,64,256]{2,1,0:T(8,128)(2,1)S(1)} %get-tuple-element.54.refs_0_, bf16[16,256,128]{2,1,0:T(8,128)(2,1)S(1)} %get-tuple-element.55.refs_1_, ...), custom_call_target="tpu_custom_call" | custom-call | tf_op jit(solution)/shard_map/leaf/pallas_call | solution.py:330
  7.3 0.1 collective-permute-start
  7.4 1.9 %collective-permute-done.1.refs_1_ = bf16[16,32,128]{2,1,0:T(8,128)(2,1)S(1)} collective-permute-done((bf16[16,32,128]{2,1,0:T(8,128)(2,1)S(1)}, bf16[16,32,128]{2,1,0:T(8,128)(2,1)S(1)}, u32[]{:S(2)}, u32[]{:S(2)}) %collective-permute-start.1) | collective-permute-done | bytes 131104 | tf_op jit(solution)/shard_map/ppermute | solution.py:32
  9.2 1.4 %level.8 = (bf16[16,32,128]{2,1,0:T(8,128)(2,1)S(1)}, bf16[16,32,128]{2,1,0:T(8,128)(2,1)S(1)}, bf16[16,64,256]{2,1,0:T(8,128)(2,1)S(1)}, bf16[16,256,128]{2,1,0:T(8,128)(2,1)S(1)}, s32[16,128]{1,0:T(8,128)S(1)}) custom-call(bf16[16,32,128]{2,1,0:T(8,128)(2,1)S(1)} %get-tuple-element.57.refs_3_.refs_0_, ...), custom_call_target="tpu_custom_call" | custom-call | tf_op jit(solution)/shard_map/level/pallas_call | solution.py:344
  10.7 1.6 %collective-permute-start.4 = (bf16[16,32,128]{2,1,0:T(8,128)(2,1)S(1)}, bf16[16,32,128]{2,1,0:T(8,128)(2,1)S(1)}, u32[]{:S(2)}, u32[]{:S(2)}) collective-permute-start(bf16[16,32,128]{2,1,0:T(8,128)(2,1)S(1)} %get-tuple-element.72), channel_id=1, source_target_pairs={{0,2},{1,3},{2,0},{3,1},{4,6},{5,7},{6,4},{7,5},{8,10},{9,11},{10,... | collective-permute-start | bytes 393224 | tf_op jit(solution)/shard_map/ppermute | solution.py:32
  12.3 0.6 leaf.6
  12.9 2.3 %collective-permute-start.3 = (bf16[16,32,128]{2,1,0:T(8,128)(2,1)S(1)}, bf16[16,32,128]{2,1,0:T(8,128)(2,1)S(1)}, u32[]{:S(2)}, u32[]{:S(2)}) collective-permute-start(bf16[16,32,128]{2,1,0:T(8,128)(2,1)S(1)} %get-tuple-element.68), channel_id=1, source_target_pairs={{0,1},{1,0},{2,3},{3,2},{4,5},{5,4},{6,7},{7,6},{8,9},{9,8},{10,11... | collective-permute-start | bytes 393224 | tf_op jit(solution)/shard_map/ppermute | solution.py:32
  15.2 0.0 collective-permute-done.refs_1_
  15.2 0.4 level.9
  15.6 0.8 %collective-permute-start.2 = (bf16[16,32,128]{2,1,0:T(8,128)(2,1)S(1)}, bf16[16,32,128]{2,1,0:T(8,128)(2,1)S(1)}, u32[]{:S(2)}, u32[]{:S(2)}) collective-permute-start(bf16[16,32,128]{2,1,0:T(8,128)(2,1)S(1)} %get-tuple-element.67), channel_id=1, source_target_pairs={{0,2},{1,3},{2,0},{3,1},{4,6},{5,7},{6,4},{7,5},{8,10},{9,11},{10,... | collective-permute-start | bytes 393224 | tf_op jit(solution)/shard_map/ppermute | solution.py:32
  16.4 0.4 level.10
  16.8 2.4 %collective-permute-start.8 = (bf16[16,32,128]{2,1,0:T(8,128)(2,1)S(1)}, bf16[16,32,128]{2,1,0:T(8,128)(2,1)S(1)}, u32[]{:S(2)}, u32[]{:S(2)}) collective-permute-start(bf16[16,32,128]{2,1,0:T(8,128)(2,1)S(1)} %get-tuple-element.80), channel_id=1, source_target_pairs={{0,4},{1,5},{2,6},{3,7},{4,0},{5,1},{6,2},{7,3},{8,12},{9,13},{10,... | collective-permute-start | bytes 393224 | tf_op jit(solution)/shard_map/ppermute | solution.py:32
  19.2 0.6 leaf.7
  19.8 3.3 %collective-permute-start.7 = (bf16[16,32,128]{2,1,0:T(8,128)(2,1)S(1)}, bf16[16,32,128]{2,1,0:T(8,128)(2,1)S(1)}, u32[]{:S(2)}, u32[]{:S(2)}) collective-permute-start(bf16[16,32,128]{2,1,0:T(8,128)(2,1)S(1)} %get-tuple-element.79), channel_id=1, source_target_pairs={{0,1},{1,0},{2,3},{3,2},{4,5},{5,4},{6,7},{7,6},{8,9},{9,8},{10,11... | collective-permute-start | bytes 393224 | tf_op jit(solution)/shard_map/ppermute | solution.py:32
  23.1 0.4 level.11
  23.5 0.0 copy-start
  23.5 1.1 %collective-permute-start.6 = (bf16[16,32,128]{2,1,0:T(8,128)(2,1)S(1)}, bf16[16,32,128]{2,1,0:T(8,128)(2,1)S(1)}, u32[]{:S(2)}, u32[]{:S(2)}) collective-permute-start(bf16[16,32,128]{2,1,0:T(8,128)(2,1)S(1)} %get-tuple-element.78), channel_id=1, source_target_pairs={{0,2},{1,3},{2,0},{3,1},{4,6},{5,7},{6,4},{7,5},{8,10},{9,11},{10,... | collective-permute-start | bytes 393224 | tf_op jit(solution)/shard_map/ppermute | solution.py:32
  24.6 0.4 level.12
  25.0 0.7 %collective-permute-start.5 = (bf16[16,32,128]{2,1,0:T(8,128)(2,1)S(1)}, bf16[16,32,128]{2,1,0:T(8,128)(2,1)S(1)}, u32[]{:S(2)}, u32[]{:S(2)}) collective-permute-start(bf16[16,32,128]{2,1,0:T(8,128)(2,1)S(1)} %get-tuple-element.77), channel_id=1, source_target_pairs={{0,4},{1,5},{2,6},{3,7},{4,0},{5,1},{6,2},{7,3},{8,12},{9,13},{10,... | collective-permute-start | bytes 393224 | tf_op jit(solution)/shard_map/ppermute | solution.py:32
  25.7 0.9 %last.4 = (bf16[8,2,32,128]{3,2,1,0:T(8,128)(2,1)S(1)}, bf16[8,2,32,128]{3,2,1,0:T(8,128)(2,1)S(1)}, bf16[8,2,32,128]{3,2,1,0:T(8,128)(2,1)S(1)}, bf16[8,2,32,128]{3,2,1,0:T(8,128)(2,1)S(1)}) custom-call(bf16[16,32,128]{2,1,0:T(8,128)(2,1)S(1)} %get-tuple-element.73.refs_3_.own_in, bf16[16,32,128]{2,1,0:T(8,128)(2,1)S(1)} %collective-permute-done.8.came_in, ...), custom_call_target="tpu_custom_call" | custom-call | tf_op jit(solution)/shard_map/last/pallas_call | solution.py:358
  26.6 0.4 level.13
  27.0 2.1 %collective-permute-start.13 = (bf16[16,32,128]{2,1,0:T(8,128)(2,1)S(1)}, bf16[16,32,128]{2,1,0:T(8,128)(2,1)S(1)}, u32[]{:S(2)}, u32[]{:S(2)}) collective-permute-start(bf16[16,32,128]{2,1,0:T(8,128)(2,1)S(1)} %get-tuple-element.92), channel_id=1, source_target_pairs={{0,2},{1,3},{2,0},{3,1},{4,6},{5,7},{6,4},{7,5},{8,10},{9,11},{10,... | collective-permute-start | bytes 393224 | tf_op jit(solution)/shard_map/ppermute | solution.py:32
  29.1 1.9 %collective-permute-done.6.refs_1_ = bf16[16,32,128]{2,1,0:T(8,128)(2,1)S(1)} collective-permute-done((bf16[16,32,128]{2,1,0:T(8,128)(2,1)S(1)}, bf16[16,32,128]{2,1,0:T(8,128)(2,1)S(1)}, u32[]{:S(2)}, u32[]{:S(2)}) %collective-permute-start.6) | collective-permute-done | bytes 131104 | tf_op jit(solution)/shard_map/ppermute | solution.py:32
  31.0 0.4 level.14
  31.4 1.4 %collective-permute-start.12 = (bf16[16,32,128]{2,1,0:T(8,128)(2,1)S(1)}, bf16[16,32,128]{2,1,0:T(8,128)(2,1)S(1)}, u32[]{:S(2)}, u32[]{:S(2)}) collective-permute-start(bf16[16,32,128]{2,1,0:T(8,128)(2,1)S(1)} %get-tuple-element.91), channel_id=1, source_target_pairs={{0,4},{1,5},{2,6},{3,7},{4,0},{5,1},{6,2},{7,3},{8,12},{9,13},{10,... | collective-permute-start | bytes 393224 | tf_op jit(solution)/shard_map/ppermute | solution.py:32
  32.7 3.2 %collective-permute-done.5.came_in = bf16[16,32,128]{2,1,0:T(8,128)(2,1)S(1)} collective-permute-done((bf16[16,32,128]{2,1,0:T(8,128)(2,1)S(1)}, bf16[16,32,128]{2,1,0:T(8,128)(2,1)S(1)}, u32[]{:S(2)}, u32[]{:S(2)}) %collective-permute-start.5) | collective-permute-done | bytes 131104 | tf_op jit(solution)/shard_map/ppermute | solution.py:32
  35.9 0.9 %last.5 = (bf16[8,2,32,128]{3,2,1,0:T(8,128)(2,1)S(1)}, bf16[8,2,32,128]{3,2,1,0:T(8,128)(2,1)S(1)}, bf16[8,2,32,128]{3,2,1,0:T(8,128)(2,1)S(1)}, bf16[8,2,32,128]{3,2,1,0:T(8,128)(2,1)S(1)}) custom-call(bf16[16,32,128]{2,1,0:T(8,128)(2,1)S(1)} %get-tuple-element.76._.own_in, ...), custom_call_target="tpu_custom_call", output_to_operand_aliasing={{0}: (5, {}), {1}: (6, {}), {2}: (7, {}), {3}: (8, {})} | custom-call | tf_op jit(solution)/shard_map/last/pallas_call | solution.py:358
  36.8 0.4 level.15
  37.2 0.1 collective-permute-start.17
  37.3 0.1 collective-permute-start.9
  37.4 1.4 %collective-permute-start.10 = (bf16[8,2,32,128]{3,2,1,0:T(8,128)(2,1)S(1)}, bf16[8,2,32,128]{3,2,1,0:T(8,128)(2,1)S(1)}, u32[]{:S(2)}, u32[]{:S(2)}) collective-permute-start(bf16[8,2,32,128]{3,2,1,0:T(8,128)(2,1)S(1)} %get-tuple-element.89), channel_id=1, source_target_pairs={{0,16},{8,24},{16,0},{24,8},{1,17},{9,25},{17,1},{25,9},{2,18},{10... | collective-permute-start | bytes 393224 | tf_op jit(solution)/shard_map/ppermute | solution.py:32
  38.8 0.5 collective-permute-start.11
  39.2 0.1 collective-permute-done.12.came_in
  39.3 0.9 %last.6 = (bf16[8,2,16,128]{3,2,1,0:T(8,128)(2,1)S(1)}, bf16[8,2,16,128]{3,2,1,0:T(8,128)(2,1)S(1)}, bf16[8,2,16,128]{3,2,1,0:T(8,128)(2,1)S(1)}, bf16[8,2,16,128]{3,2,1,0:T(8,128)(2,1)S(1)}) custom-call(bf16[16,32,128]{2,1,0:T(8,128)(2,1)S(1)} %get-tuple-element.83._.own_in, bf16[16,32,128]{2,1,0:T(8,128)(2,1)S(1)} %collective-permute-done.12.came_in, ...), custom_call_target="tpu_custom_call" | custom-call | tf_op jit(solution)/shard_map/last/pallas_call | solution.py:358
  40.2 0.3 collective-permute-start.14
  40.5 2.6 %table.2._.refs_1_ = bf16[2,256,4224]{2,1,0:T(8,128)(2,1)S(1)} custom-call(s32[256]{0:T(256)S(1)} %copy-done.1, bf16[8,2,16,128]{3,2,1,0:T(8,128)(2,1)S(1)} %get-tuple-element.94.refs_0_.refs_4_), custom_call_target="tpu_custom_call" | custom-call | tf_op jit(solution)/shard_map/table/pallas_call | solution.py:201
  43.1 0.7 %collective-permute-done.17.came_in = bf16[16,32,128]{2,1,0:T(8,128)(2,1)S(1)} collective-permute-done((bf16[16,32,128]{2,1,0:T(8,128)(2,1)S(1)}, bf16[16,32,128]{2,1,0:T(8,128)(2,1)S(1)}, u32[]{:S(2)}, u32[]{:S(2)}) %collective-permute-start.17) | collective-permute-done | bytes 131104 | tf_op jit(solution)/shard_map/ppermute | solution.py:32
  43.9 1.5 %collective-permute-start.15 = (bf16[8,2,16,128]{3,2,1,0:T(8,128)(2,1)S(1)}, bf16[8,2,16,128]{3,2,1,0:T(8,128)(2,1)S(1)}, u32[]{:S(2)}, u32[]{:S(2)}) collective-permute-start(bf16[8,2,16,128]{3,2,1,0:T(8,128)(2,1)S(1)} %get-tuple-element.96), channel_id=1, source_target_pairs={{0,16},{8,24},{16,0},{24,8},{1,17},{9,25},{17,1},{25,9},{2,18},{10... | collective-permute-start | bytes 196616 | tf_op jit(solution)/shard_map/ppermute | solution.py:32
  45.3 0.9 %last.7 = (bf16[8,2,16,128]{3,2,1,0:T(8,128)(2,1)S(1)}, bf16[8,2,16,128]{3,2,1,0:T(8,128)(2,1)S(1)}, bf16[8,2,16,128]{3,2,1,0:T(8,128)(2,1)S(1)}, bf16[8,2,16,128]{3,2,1,0:T(8,128)(2,1)S(1)}) custom-call(bf16[16,32,128]{2,1,0:T(8,128)(2,1)S(1)} %get-tuple-element.93._.own_in, bf16[16,32,128]{2,1,0:T(8,128)(2,1)S(1)} %collective-permute-done.17.came_in, ...), custom_call_target="tpu_custom_call" | custom-call | tf_op jit(solution)/shard_map/last/pallas_call | solution.py:358
  46.2 0.1 collective-permute-start.16
  46.3 0.6 %collective-permute-start.18 = (bf16[8,2,16,128]{3,2,1,0:T(8,128)(2,1)S(1)}, bf16[8,2,16,128]{3,2,1,0:T(8,128)(2,1)S(1)}, u32[]{:S(2)}, u32[]{:S(2)}) collective-permute-start(bf16[8,2,16,128]{3,2,1,0:T(8,128)(2,1)S(1)} %get-tuple-element.100), channel_id=1, source_target_pairs={{0,8},{8,0},{16,24},{24,16},{1,9},{9,1},{17,25},{25,17},{2,10},{10... | collective-permute-start | bytes 196616 | tf_op jit(solution)/shard_map/ppermute | solution.py:32
  46.9 1.5 %collective-permute-start.19 = (bf16[8,2,16,128]{3,2,1,0:T(8,128)(2,1)S(1)}, bf16[8,2,16,128]{3,2,1,0:T(8,128)(2,1)S(1)}, u32[]{:S(2)}, u32[]{:S(2)}) collective-permute-start(bf16[8,2,16,128]{3,2,1,0:T(8,128)(2,1)S(1)} %get-tuple-element.101), channel_id=1, source_target_pairs={{0,16},{8,24},{16,0},{24,8},{1,17},{9,25},{17,1},{25,9},{2,18},{10... | collective-permute-start | bytes 196616 | tf_op jit(solution)/shard_map/ppermute | solution.py:32
  48.4 2.4 %table.3.refs_12_ = bf16[2,256,4224]{2,1,0:T(8,128)(2,1)S(1)} custom-call(s32[256]{0:T(256)S(1)} %copy-done.1, bf16[8,2,16,128]{3,2,1,0:T(8,128)(2,1)S(1)} %get-tuple-element.99.refs_0_.refs_8_, bf16[2,256,4224]{2,1,0:T(8,128)(2,1)S(1)} %table.2._.refs_1_), custom_call_target="tpu_custom_call", output_to_operand_aliasing={{}: (2, {})} | custom-call | tf_op jit(solution)/shard_map/table/pallas_call | solution.py:201
  50.9 0.9 %collective-permute-done.19.refs_10_ = bf16[8,2,16,128]{3,2,1,0:T(8,128)(2,1)S(1)} collective-permute-done((bf16[8,2,16,128]{3,2,1,0:T(8,128)(2,1)S(1)}, bf16[8,2,16,128]{3,2,1,0:T(8,128)(2,1)S(1)}, u32[]{:S(2)}, u32[]{:S(2)}) %collective-permute-start.19) | collective-permute-done | bytes 65568 | tf_op jit(solution)/shard_map/ppermute | solution.py:32
  51.8 1.0 %collective-permute-done.20.refs_11_ = bf16[8,2,16,128]{3,2,1,0:T(8,128)(2,1)S(1)} collective-permute-done((bf16[8,2,16,128]{3,2,1,0:T(8,128)(2,1)S(1)}, bf16[8,2,16,128]{3,2,1,0:T(8,128)(2,1)S(1)}, u32[]{:S(2)}, u32[]{:S(2)}) %collective-permute-start.20) | collective-permute-done | bytes 65568 | tf_op jit(solution)/shard_map/ppermute | solution.py:32
  52.8 8.6 %synthesis.1 = bf16[8,128,8192]{2,1,0:T(8,128)(2,1)} custom-call(bf16[8,2,32,128]{3,2,1,0:T(8,128)(2,1)S(1)} %get-tuple-element.87.refs_3_.refs_0_, bf16[8,2,32,128]{3,2,1,0:T(8,128)(2,1)S(1)} %collective-permute-done.9.refs_1_, bf16[8,2,32,128]{3,2,1,0:T(8,128)(2,1)S(1)} %collective-permute-done.10.refs_2_, ...), custom_call_target="tpu_custom_call" | custom-call | tf_op jit(solution)/shard_map/synthesis/pallas_call | solution.py:277
  (22 shorter events, 0.1 us)
Async XLA Ops:
  0.0 9.2 %slice-start = ((s8[6291456]{0:T(1024)(128)(4,1)}), s8[4194304]{0:T(1024)(128)(4,1)S(1)}, s32[]{:S(2)}) async-start(s8[6291456]{0:T(1024)(128)(4,1)} %bitcast.1), calls=%async_computation | async-start | bytes 8388608
  0.0 9.2 %slice-start.1 = ((s8[6291456]{0:T(1024)(128)(4,1)}), s8[2097152]{0:T(1024)(128)(4,1)S(1)}, s32[]{:S(2)}) async-start(s8[6291456]{0:T(1024)(128)(4,1)} %bitcast.1), calls=%async_computation.1 | async-start | bytes 4194304
  2.5 6.8 %collective-permute-start.1 = (bf16[16,32,128]{2,1,0:T(8,128)(2,1)S(1)}, bf16[16,32,128]{2,1,0:T(8,128)(2,1)S(1)}, u32[]{:S(2)}, u32[]{:S(2)}) collective-permute-start(bf16[16,32,128]{2,1,0:T(8,128)(2,1)S(1)} %get-tuple-element.63), channel_id=1, source_target_pairs={{0,1},{1,0},{2,3},{3,2},{4,5},{5,4},{6,7},{7,6},{8,9},{9,8},{10,11... | collective-permute-start | bytes 393224 | tf_op jit(solution)/shard_map/ppermute | solution.py:32
  7.3 7.9 %collective-permute-start = (bf16[16,32,128]{2,1,0:T(8,128)(2,1)S(1)}, bf16[16,32,128]{2,1,0:T(8,128)(2,1)S(1)}, u32[]{:S(2)}, u32[]{:S(2)}) collective-permute-start(bf16[16,32,128]{2,1,0:T(8,128)(2,1)S(1)} %get-tuple-element.59), channel_id=1, source_target_pairs={{0,1},{1,0},{2,3},{3,2},{4,5},{5,4},{6,7},{7,6},{8,9},{9,8},{10,11... | collective-permute-start | bytes 393224 | tf_op jit(solution)/shard_map/ppermute | solution.py:32
  10.7 5.7 %collective-permute-start.4 = (bf16[16,32,128]{2,1,0:T(8,128)(2,1)S(1)}, bf16[16,32,128]{2,1,0:T(8,128)(2,1)S(1)}, u32[]{:S(2)}, u32[]{:S(2)}) collective-permute-start(bf16[16,32,128]{2,1,0:T(8,128)(2,1)S(1)} %get-tuple-element.72), channel_id=1, source_target_pairs={{0,2},{1,3},{2,0},{3,1},{4,6},{5,7},{6,4},{7,5},{8,10},{9,11},{10,... | collective-permute-start | bytes 393224 | tf_op jit(solution)/shard_map/ppermute | solution.py:32
  12.9 10.2 %collective-permute-start.3 = (bf16[16,32,128]{2,1,0:T(8,128)(2,1)S(1)}, bf16[16,32,128]{2,1,0:T(8,128)(2,1)S(1)}, u32[]{:S(2)}, u32[]{:S(2)}) collective-permute-start(bf16[16,32,128]{2,1,0:T(8,128)(2,1)S(1)} %get-tuple-element.68), channel_id=1, source_target_pairs={{0,1},{1,0},{2,3},{3,2},{4,5},{5,4},{6,7},{7,6},{8,9},{9,8},{10,11... | collective-permute-start | bytes 393224 | tf_op jit(solution)/shard_map/ppermute | solution.py:32
  15.6 9.0 %collective-permute-start.2 = (bf16[16,32,128]{2,1,0:T(8,128)(2,1)S(1)}, bf16[16,32,128]{2,1,0:T(8,128)(2,1)S(1)}, u32[]{:S(2)}, u32[]{:S(2)}) collective-permute-start(bf16[16,32,128]{2,1,0:T(8,128)(2,1)S(1)} %get-tuple-element.67), channel_id=1, source_target_pairs={{0,2},{1,3},{2,0},{3,1},{4,6},{5,7},{6,4},{7,5},{8,10},{9,11},{10,... | collective-permute-start | bytes 393224 | tf_op jit(solution)/shard_map/ppermute | solution.py:32
  16.8 8.9 %collective-permute-start.8 = (bf16[16,32,128]{2,1,0:T(8,128)(2,1)S(1)}, bf16[16,32,128]{2,1,0:T(8,128)(2,1)S(1)}, u32[]{:S(2)}, u32[]{:S(2)}) collective-permute-start(bf16[16,32,128]{2,1,0:T(8,128)(2,1)S(1)} %get-tuple-element.80), channel_id=1, source_target_pairs={{0,4},{1,5},{2,6},{3,7},{4,0},{5,1},{6,2},{7,3},{8,12},{9,13},{10,... | collective-permute-start | bytes 393224 | tf_op jit(solution)/shard_map/ppermute | solution.py:32
  19.8 6.8 %collective-permute-start.7 = (bf16[16,32,128]{2,1,0:T(8,128)(2,1)S(1)}, bf16[16,32,128]{2,1,0:T(8,128)(2,1)S(1)}, u32[]{:S(2)}, u32[]{:S(2)}) collective-permute-start(bf16[16,32,128]{2,1,0:T(8,128)(2,1)S(1)} %get-tuple-element.79), channel_id=1, source_target_pairs={{0,1},{1,0},{2,3},{3,2},{4,5},{5,4},{6,7},{7,6},{8,9},{9,8},{10,11... | collective-permute-start | bytes 393224 | tf_op jit(solution)/shard_map/ppermute | solution.py:32
  23.5 2.2 %copy-start = (bf16[64,128,128]{2,1,0:T(8,128)(2,1)S(1)}, bf16[64,128,128]{2,1,0:T(8,128)(2,1)}, u32[]{:S(2)}) copy-start(bf16[64,128,128]{2,1,0:T(8,128)(2,1)} %lats.7) | copy-start | bytes 6291460
  23.5 7.5 %collective-permute-start.6 = (bf16[16,32,128]{2,1,0:T(8,128)(2,1)S(1)}, bf16[16,32,128]{2,1,0:T(8,128)(2,1)S(1)}, u32[]{:S(2)}, u32[]{:S(2)}) collective-permute-start(bf16[16,32,128]{2,1,0:T(8,128)(2,1)S(1)} %get-tuple-element.78), channel_id=1, source_target_pairs={{0,2},{1,3},{2,0},{3,1},{4,6},{5,7},{6,4},{7,5},{8,10},{9,11},{10,... | collective-permute-start | bytes 393224 | tf_op jit(solution)/shard_map/ppermute | solution.py:32
  25.0 10.9 %collective-permute-start.5 = (bf16[16,32,128]{2,1,0:T(8,128)(2,1)S(1)}, bf16[16,32,128]{2,1,0:T(8,128)(2,1)S(1)}, u32[]{:S(2)}, u32[]{:S(2)}) collective-permute-start(bf16[16,32,128]{2,1,0:T(8,128)(2,1)S(1)} %get-tuple-element.77), channel_id=1, source_target_pairs={{0,4},{1,5},{2,6},{3,7},{4,0},{5,1},{6,2},{7,3},{8,12},{9,13},{10,... | collective-permute-start | bytes 393224 | tf_op jit(solution)/shard_map/ppermute | solution.py:32
  27.0 9.8 %collective-permute-start.13 = (bf16[16,32,128]{2,1,0:T(8,128)(2,1)S(1)}, bf16[16,32,128]{2,1,0:T(8,128)(2,1)S(1)}, u32[]{:S(2)}, u32[]{:S(2)}) collective-permute-start(bf16[16,32,128]{2,1,0:T(8,128)(2,1)S(1)} %get-tuple-element.92), channel_id=1, source_target_pairs={{0,2},{1,3},{2,0},{3,1},{4,6},{5,7},{6,4},{7,5},{8,10},{9,11},{10,... | collective-permute-start | bytes 393224 | tf_op jit(solution)/shard_map/ppermute | solution.py:32
  31.4 8.0 %collective-permute-start.12 = (bf16[16,32,128]{2,1,0:T(8,128)(2,1)S(1)}, bf16[16,32,128]{2,1,0:T(8,128)(2,1)S(1)}, u32[]{:S(2)}, u32[]{:S(2)}) collective-permute-start(bf16[16,32,128]{2,1,0:T(8,128)(2,1)S(1)} %get-tuple-element.91), channel_id=1, source_target_pairs={{0,4},{1,5},{2,6},{3,7},{4,0},{5,1},{6,2},{7,3},{8,12},{9,13},{10,... | collective-permute-start | bytes 393224 | tf_op jit(solution)/shard_map/ppermute | solution.py:32
  37.2 6.6 %collective-permute-start.17 = (bf16[16,32,128]{2,1,0:T(8,128)(2,1)S(1)}, bf16[16,32,128]{2,1,0:T(8,128)(2,1)S(1)}, u32[]{:S(2)}, u32[]{:S(2)}) collective-permute-start(bf16[16,32,128]{2,1,0:T(8,128)(2,1)S(1)} %get-tuple-element.98), channel_id=1, source_target_pairs={{0,4},{1,5},{2,6},{3,7},{4,0},{5,1},{6,2},{7,3},{8,12},{9,13},{10,... | collective-permute-start | bytes 393224 | tf_op jit(solution)/shard_map/ppermute | solution.py:32
  37.3 8.9 %collective-permute-start.9 = (bf16[8,2,32,128]{3,2,1,0:T(8,128)(2,1)S(1)}, bf16[8,2,32,128]{3,2,1,0:T(8,128)(2,1)S(1)}, u32[]{:S(2)}, u32[]{:S(2)}) collective-permute-start(bf16[8,2,32,128]{3,2,1,0:T(8,128)(2,1)S(1)} %get-tuple-element.88), channel_id=1, source_target_pairs={{0,8},{8,0},{16,24},{24,16},{1,9},{9,1},{17,25},{25,17},{2,10},{10... | collective-permute-start | bytes 393224 | tf_op jit(solution)/shard_map/ppermute | solution.py:32
  37.4 8.9 %collective-permute-start.10 = (bf16[8,2,32,128]{3,2,1,0:T(8,128)(2,1)S(1)}, bf16[8,2,32,128]{3,2,1,0:T(8,128)(2,1)S(1)}, u32[]{:S(2)}, u32[]{:S(2)}) collective-permute-start(bf16[8,2,32,128]{3,2,1,0:T(8,128)(2,1)S(1)} %get-tuple-element.89), channel_id=1, source_target_pairs={{0,16},{8,24},{16,0},{24,8},{1,17},{9,25},{17,1},{25,9},{2,18},{10... | collective-permute-start | bytes 393224 | tf_op jit(solution)/shard_map/ppermute | solution.py:32
  38.8 8.2 %collective-permute-start.11 = (bf16[8,2,32,128]{3,2,1,0:T(8,128)(2,1)S(1)}, bf16[8,2,32,128]{3,2,1,0:T(8,128)(2,1)S(1)}, u32[]{:S(2)}, u32[]{:S(2)}) collective-permute-start(bf16[8,2,32,128]{3,2,1,0:T(8,128)(2,1)S(1)} %get-tuple-element.90), channel_id=1, source_target_pairs={{0,24},{8,16},{16,8},{24,0},{1,25},{9,17},{17,9},{25,1},{2,26},{10... | collective-permute-start | bytes 393224 | tf_op jit(solution)/shard_map/ppermute | solution.py:32
  39.3 1.2 %copy-start.1 = (s32[256]{0:T(256)S(1)}, s32[256]{0:T(256)}, u32[]{:S(2)}) copy-start(s32[256]{0:T(256)} %map_ref.3) | copy-start | bytes 3076
  40.2 8.2 %collective-permute-start.14 = (bf16[8,2,16,128]{3,2,1,0:T(8,128)(2,1)S(1)}, bf16[8,2,16,128]{3,2,1,0:T(8,128)(2,1)S(1)}, u32[]{:S(2)}, u32[]{:S(2)}) collective-permute-start(bf16[8,2,16,128]{3,2,1,0:T(8,128)(2,1)S(1)} %get-tuple-element.95), channel_id=1, source_target_pairs={{0,8},{8,0},{16,24},{24,16},{1,9},{9,1},{17,25},{25,17},{2,10},{10... | collective-permute-start | bytes 196616 | tf_op jit(solution)/shard_map/ppermute | solution.py:32
  43.9 7.0 %collective-permute-start.15 = (bf16[8,2,16,128]{3,2,1,0:T(8,128)(2,1)S(1)}, bf16[8,2,16,128]{3,2,1,0:T(8,128)(2,1)S(1)}, u32[]{:S(2)}, u32[]{:S(2)}) collective-permute-start(bf16[8,2,16,128]{3,2,1,0:T(8,128)(2,1)S(1)} %get-tuple-element.96), channel_id=1, source_target_pairs={{0,16},{8,24},{16,0},{24,8},{1,17},{9,25},{17,1},{25,9},{2,18},{10... | collective-permute-start | bytes 196616 | tf_op jit(solution)/shard_map/ppermute | solution.py:32
  46.2 4.7 %collective-permute-start.16 = (bf16[8,2,16,128]{3,2,1,0:T(8,128)(2,1)S(1)}, bf16[8,2,16,128]{3,2,1,0:T(8,128)(2,1)S(1)}, u32[]{:S(2)}, u32[]{:S(2)}) collective-permute-start(bf16[8,2,16,128]{3,2,1,0:T(8,128)(2,1)S(1)} %get-tuple-element.97), channel_id=1, source_target_pairs={{0,24},{8,16},{16,8},{24,0},{1,25},{9,17},{17,9},{25,1},{2,26},{10... | collective-permute-start | bytes 196616 | tf_op jit(solution)/shard_map/ppermute | solution.py:32
  46.3 4.6 %collective-permute-start.18 = (bf16[8,2,16,128]{3,2,1,0:T(8,128)(2,1)S(1)}, bf16[8,2,16,128]{3,2,1,0:T(8,128)(2,1)S(1)}, u32[]{:S(2)}, u32[]{:S(2)}) collective-permute-start(bf16[8,2,16,128]{3,2,1,0:T(8,128)(2,1)S(1)} %get-tuple-element.100), channel_id=1, source_target_pairs={{0,8},{8,0},{16,24},{24,16},{1,9},{9,1},{17,25},{25,17},{2,10},{10... | collective-permute-start | bytes 196616 | tf_op jit(solution)/shard_map/ppermute | solution.py:32
  46.9 4.9 %collective-permute-start.19 = (bf16[8,2,16,128]{3,2,1,0:T(8,128)(2,1)S(1)}, bf16[8,2,16,128]{3,2,1,0:T(8,128)(2,1)S(1)}, u32[]{:S(2)}, u32[]{:S(2)}) collective-permute-start(bf16[8,2,16,128]{3,2,1,0:T(8,128)(2,1)S(1)} %get-tuple-element.101), channel_id=1, source_target_pairs={{0,16},{8,24},{16,0},{24,8},{1,17},{9,25},{17,1},{25,9},{2,18},{10... | collective-permute-start | bytes 196616 | tf_op jit(solution)/shard_map/ppermute | solution.py:32
  48.4 4.4 %collective-permute-start.20 = (bf16[8,2,16,128]{3,2,1,0:T(8,128)(2,1)S(1)}, bf16[8,2,16,128]{3,2,1,0:T(8,128)(2,1)S(1)}, u32[]{:S(2)}, u32[]{:S(2)}) collective-permute-start(bf16[8,2,16,128]{3,2,1,0:T(8,128)(2,1)S(1)} %get-tuple-element.102), channel_id=1, source_target_pairs={{0,24},{8,16},{16,8},{24,0},{1,25},{9,17},{17,9},{25,1},{2,26},{10... | collective-permute-start | bytes 196616 | tf_op jit(solution)/shard_map/ppermute | solution.py:32

commit v7 on v6

--- a/solution.py
+++ b/solution.py
@@ -392,7 +392,7 @@
 
     state, begun, blocks = {}, [], []
     for chunk, stage in order:
-        name, fetches = wanted.pop() if wanted else (None, [])
+        name, fetches = wanted.pop() if wanted and stage == 0 else (None, [])
         if (chunk, stage) in TABLE_AT:
             before = table = make_table(before, table)
         if stage == levels:

time: 61.8 us -> 63.1 us (1.021)
  starting transfers between devices: 24.8 us -> 26.1 us
    ppermute x21, starting transfers between devices: 24.8 us -> 26.1 us  [exchange(): lax.ppermute(shard, axis, [(i, i ^ step) for i in range(lax.axis_size(axi...]
    pallas_call x4, Pallas kernels: 5.37 us -> 6.57 us  [leaf(): pl.pallas_call(functools.partial(leaf_kernel, places), in_specs=[IN_VMEM...]
    pallas_call x8, Pallas kernels: 4.29 us -> 3.27 us  [level(): pl.pallas_call(functools.partial(level_kernel, firsts[chunk], num, places...]
  transfers between devices with their start and end apart: 21 -> 21, of which waited for: 7 -> 5; matrix products, arithmetic and copies ran while one was open for 0% -> 0% of each run, Pallas kernels for 25% -> 25%
where the time goes in v7:
time: 63.1 us; the launch traced here: 63 us
  Pallas kernels  26.9 us (43%)
  starting transfers between devices  26.1 us (41%)
  waiting for transfers between devices  9.56 us (15%)
    ppermute x21, starting transfers between devices, exchange(): lax.ppermute(shard, axis, [(i, i ^ step) for i in range(lax.axis_size(axi...  26.1 us
    ppermute x21, waiting for transfers between devices, exchange(): lax.ppermute(shard, axis, [(i, i ^ step) for i in range(lax.axis_size(axi...  9.56 us
    pallas_call x1, Pallas kernels, synthesis(): pl.pallas_call(synthesis_kernel, in_specs=[IN_VMEM] * (len(blocks) + 1),...  8.62 us
    pallas_call x4, Pallas kernels, leaf(): pl.pallas_call(functools.partial(leaf_kernel, places), in_specs=[IN_VMEM...  6.57 us
    pallas_call x2, Pallas kernels, wave_table(): pl.pallas_call(functools.partial(table_kernel, lon_count, slots, sizes, f...  5.01 us
    pallas_call x4, Pallas kernels, last(): pl.pallas_call(functools.partial(last_kernel, firsts[chunk], levels - 1,...  3.44 us
    pallas_call x8, Pallas kernels, level(): pl.pallas_call(functools.partial(level_kernel, firsts[chunk], num, places...  3.27 us
  transfers between devices with their start and end apart: 21, of which 5 were waited for; matrix products, arithmetic and copies ran while one was open for 0% of the time, Pallas kernels for 25%

profile of v7, /device:TPU:0, one launch (start us, length us, event | category | flops | bytes accessed | tf_op | source)
XLA Modules:
  0.0 63.0 jit_solution(15259090292109477965)
XLA Ops:
  0.0 2.4 %leaf.4 = (bf16[16,32,128]{2,1,0:T(8,128)(2,1)S(1)}, bf16[16,32,128]{2,1,0:T(8,128)(2,1)S(1)}, bf16[16,64,256]{2,1,0:T(8,128)(2,1)S(1)}, bf16[16,256,128]{2,1,0:T(8,128)(2,1)S(1)}, s32[16,128]{1,0:T(8,128)S(1)}) custom-call(bf16[64,64,256]{2,1,0:T(8,128)(2,1)} %bitcast.3, bf16[64,256,128]{2,1,0:T(8,128)(2,1)} %refs_5_.5, s32[64,128]{1,0:T(8,128)} %refs_6_.5, ...), custom_call_target="tpu_custom_call" | custom-call | tf_op jit(solution)/shard_map/leaf/pallas_call | solution.py:330
  2.5 3.0 %collective-permute-start.1 = (bf16[16,32,128]{2,1,0:T(8,128)(2,1)S(1)}, bf16[16,32,128]{2,1,0:T(8,128)(2,1)S(1)}, u32[]{:S(2)}, u32[]{:S(2)}) collective-permute-start(bf16[16,32,128]{2,1,0:T(8,128)(2,1)S(1)} %get-tuple-element.63), channel_id=1, source_target_pairs={{0,1},{1,0},{2,3},{3,2},{4,5},{5,4},{6,7},{7,6},{8,9},{9,8},{10,11... | collective-permute-start | bytes 393224 | tf_op jit(solution)/shard_map/ppermute | solution.py:32
  5.5 1.8 %leaf.5 = (bf16[16,32,128]{2,1,0:T(8,128)(2,1)S(1)}, bf16[16,32,128]{2,1,0:T(8,128)(2,1)S(1)}, bf16[16,64,256]{2,1,0:T(8,128)(2,1)S(1)}, bf16[16,256,128]{2,1,0:T(8,128)(2,1)S(1)}, s32[16,128]{1,0:T(8,128)S(1)}) custom-call(bf16[16,64,256]{2,1,0:T(8,128)(2,1)S(1)} %get-tuple-element.54.refs_0_, bf16[16,256,128]{2,1,0:T(8,128)(2,1)S(1)} %get-tuple-element.55.refs_1_, ...), custom_call_target="tpu_custom_call" | custom-call | tf_op jit(solution)/shard_map/leaf/pallas_call | solution.py:330
  7.3 0.1 collective-permute-start
  7.4 1.8 %collective-permute-done.1.refs_1_ = bf16[16,32,128]{2,1,0:T(8,128)(2,1)S(1)} collective-permute-done((bf16[16,32,128]{2,1,0:T(8,128)(2,1)S(1)}, bf16[16,32,128]{2,1,0:T(8,128)(2,1)S(1)}, u32[]{:S(2)}, u32[]{:S(2)}) %collective-permute-start.1) | collective-permute-done | bytes 131104 | tf_op jit(solution)/shard_map/ppermute | solution.py:32
  9.2 0.4 level.8
  9.6 1.6 %collective-permute-start.4 = (bf16[16,32,128]{2,1,0:T(8,128)(2,1)S(1)}, bf16[16,32,128]{2,1,0:T(8,128)(2,1)S(1)}, u32[]{:S(2)}, u32[]{:S(2)}) collective-permute-start(bf16[16,32,128]{2,1,0:T(8,128)(2,1)S(1)} %get-tuple-element.72), channel_id=1, source_target_pairs={{0,2},{1,3},{2,0},{3,1},{4,6},{5,7},{6,4},{7,5},{8,10},{9,11},{10,... | collective-permute-start | bytes 393224 | tf_op jit(solution)/shard_map/ppermute | solution.py:32
  11.3 1.8 %leaf.6 = (bf16[16,32,128]{2,1,0:T(8,128)(2,1)S(1)}, bf16[16,32,128]{2,1,0:T(8,128)(2,1)S(1)}, bf16[16,64,256]{2,1,0:T(8,128)(2,1)S(1)}, bf16[16,256,128]{2,1,0:T(8,128)(2,1)S(1)}, s32[16,128]{1,0:T(8,128)S(1)}) custom-call(bf16[16,64,256]{2,1,0:T(8,128)(2,1)S(1)} %get-tuple-element.60.refs_0_, bf16[16,256,128]{2,1,0:T(8,128)(2,1)S(1)} %get-tuple-element.61.refs_1_, ...), custom_call_target="tpu_custom_call" | custom-call | tf_op jit(solution)/shard_map/leaf/pallas_call | solution.py:330
  13.1 2.3 %collective-permute-start.3 = (bf16[16,32,128]{2,1,0:T(8,128)(2,1)S(1)}, bf16[16,32,128]{2,1,0:T(8,128)(2,1)S(1)}, u32[]{:S(2)}, u32[]{:S(2)}) collective-permute-start(bf16[16,32,128]{2,1,0:T(8,128)(2,1)S(1)} %get-tuple-element.68), channel_id=1, source_target_pairs={{0,1},{1,0},{2,3},{3,2},{4,5},{5,4},{6,7},{7,6},{8,9},{9,8},{10,11... | collective-permute-start | bytes 393224 | tf_op jit(solution)/shard_map/ppermute | solution.py:32
  15.4 0.4 level.9
  15.8 0.8 %collective-permute-start.2 = (bf16[16,32,128]{2,1,0:T(8,128)(2,1)S(1)}, bf16[16,32,128]{2,1,0:T(8,128)(2,1)S(1)}, u32[]{:S(2)}, u32[]{:S(2)}) collective-permute-start(bf16[16,32,128]{2,1,0:T(8,128)(2,1)S(1)} %get-tuple-element.67), channel_id=1, source_target_pairs={{0,2},{1,3},{2,0},{3,1},{4,6},{5,7},{6,4},{7,5},{8,10},{9,11},{10,... | collective-permute-start | bytes 393224 | tf_op jit(solution)/shard_map/ppermute | solution.py:32
  16.5 0.0 collective-permute-done.4.refs_1_
  16.5 0.4 level.10
  17.0 2.4 %collective-permute-start.8 = (bf16[16,32,128]{2,1,0:T(8,128)(2,1)S(1)}, bf16[16,32,128]{2,1,0:T(8,128)(2,1)S(1)}, u32[]{:S(2)}, u32[]{:S(2)}) collective-permute-start(bf16[16,32,128]{2,1,0:T(8,128)(2,1)S(1)} %get-tuple-element.80), channel_id=1, source_target_pairs={{0,4},{1,5},{2,6},{3,7},{4,0},{5,1},{6,2},{7,3},{8,12},{9,13},{10,... | collective-permute-start | bytes 393224 | tf_op jit(solution)/shard_map/ppermute | solution.py:32
  19.4 0.6 leaf.7
  20.0 0.9 %collective-permute-start.7 = (bf16[16,32,128]{2,1,0:T(8,128)(2,1)S(1)}, bf16[16,32,128]{2,1,0:T(8,128)(2,1)S(1)}, u32[]{:S(2)}, u32[]{:S(2)}) collective-permute-start(bf16[16,32,128]{2,1,0:T(8,128)(2,1)S(1)} %get-tuple-element.79), channel_id=1, source_target_pairs={{0,1},{1,0},{2,3},{3,2},{4,5},{5,4},{6,7},{7,6},{8,9},{9,8},{10,11... | collective-permute-start | bytes 393224 | tf_op jit(solution)/shard_map/ppermute | solution.py:32
  20.9 0.0 collective-permute-done.3.refs_1_
  20.9 0.4 level.11
  21.3 0.0 copy-start
  21.3 2.4 %collective-permute-start.6 = (bf16[16,32,128]{2,1,0:T(8,128)(2,1)S(1)}, bf16[16,32,128]{2,1,0:T(8,128)(2,1)S(1)}, u32[]{:S(2)}, u32[]{:S(2)}) collective-permute-start(bf16[16,32,128]{2,1,0:T(8,128)(2,1)S(1)} %get-tuple-element.78), channel_id=1, source_target_pairs={{0,2},{1,3},{2,0},{3,1},{4,6},{5,7},{6,4},{7,5},{8,10},{9,11},{10,... | collective-permute-start | bytes 393224 | tf_op jit(solution)/shard_map/ppermute | solution.py:32
  23.7 0.4 level.12
  24.1 1.7 %collective-permute-start.5 = (bf16[16,32,128]{2,1,0:T(8,128)(2,1)S(1)}, bf16[16,32,128]{2,1,0:T(8,128)(2,1)S(1)}, u32[]{:S(2)}, u32[]{:S(2)}) collective-permute-start(bf16[16,32,128]{2,1,0:T(8,128)(2,1)S(1)} %get-tuple-element.77), channel_id=1, source_target_pairs={{0,4},{1,5},{2,6},{3,7},{4,0},{5,1},{6,2},{7,3},{8,12},{9,13},{10,... | collective-permute-start | bytes 393224 | tf_op jit(solution)/shard_map/ppermute | solution.py:32
  25.8 0.0 collective-permute-done.8.came_in
  25.8 0.9 %last.4 = (bf16[8,2,32,128]{3,2,1,0:T(8,128)(2,1)S(1)}, bf16[8,2,32,128]{3,2,1,0:T(8,128)(2,1)S(1)}, bf16[8,2,32,128]{3,2,1,0:T(8,128)(2,1)S(1)}, bf16[8,2,32,128]{3,2,1,0:T(8,128)(2,1)S(1)}) custom-call(bf16[16,32,128]{2,1,0:T(8,128)(2,1)S(1)} %get-tuple-element.73.refs_3_.own_in, bf16[16,32,128]{2,1,0:T(8,128)(2,1)S(1)} %collective-permute-done.8.came_in, ...), custom_call_target="tpu_custom_call" | custom-call | tf_op jit(solution)/shard_map/last/pallas_call | solution.py:358
  26.7 0.4 level.13
  27.1 2.5 %collective-permute-start.13 = (bf16[16,32,128]{2,1,0:T(8,128)(2,1)S(1)}, bf16[16,32,128]{2,1,0:T(8,128)(2,1)S(1)}, u32[]{:S(2)}, u32[]{:S(2)}) collective-permute-start(bf16[16,32,128]{2,1,0:T(8,128)(2,1)S(1)} %get-tuple-element.92), channel_id=1, source_target_pairs={{0,2},{1,3},{2,0},{3,1},{4,6},{5,7},{6,4},{7,5},{8,10},{9,11},{10,... | collective-permute-start | bytes 393224 | tf_op jit(solution)/shard_map/ppermute | solution.py:32
  29.7 0.4 level.14
  30.1 2.1 %collective-permute-start.12 = (bf16[16,32,128]{2,1,0:T(8,128)(2,1)S(1)}, bf16[16,32,128]{2,1,0:T(8,128)(2,1)S(1)}, u32[]{:S(2)}, u32[]{:S(2)}) collective-permute-start(bf16[16,32,128]{2,1,0:T(8,128)(2,1)S(1)} %get-tuple-element.91), channel_id=1, source_target_pairs={{0,4},{1,5},{2,6},{3,7},{4,0},{5,1},{6,2},{7,3},{8,12},{9,13},{10,... | collective-permute-start | bytes 393224 | tf_op jit(solution)/shard_map/ppermute | solution.py:32
  32.2 4.9 %collective-permute-done.5.came_in = bf16[16,32,128]{2,1,0:T(8,128)(2,1)S(1)} collective-permute-done((bf16[16,32,128]{2,1,0:T(8,128)(2,1)S(1)}, bf16[16,32,128]{2,1,0:T(8,128)(2,1)S(1)}, u32[]{:S(2)}, u32[]{:S(2)}) %collective-permute-start.5) | collective-permute-done | bytes 131104 | tf_op jit(solution)/shard_map/ppermute | solution.py:32
  37.1 0.9 %last.5 = (bf16[8,2,32,128]{3,2,1,0:T(8,128)(2,1)S(1)}, bf16[8,2,32,128]{3,2,1,0:T(8,128)(2,1)S(1)}, bf16[8,2,32,128]{3,2,1,0:T(8,128)(2,1)S(1)}, bf16[8,2,32,128]{3,2,1,0:T(8,128)(2,1)S(1)}) custom-call(bf16[16,32,128]{2,1,0:T(8,128)(2,1)S(1)} %get-tuple-element.76._.own_in, ...), custom_call_target="tpu_custom_call", output_to_operand_aliasing={{0}: (5, {}), {1}: (6, {}), {2}: (7, {}), {3}: (8, {})} | custom-call | tf_op jit(solution)/shard_map/last/pallas_call | solution.py:358
  38.0 0.4 level.15
  38.4 0.1 collective-permute-start.17
  38.5 0.1 collective-permute-start.9
  38.5 1.5 %collective-permute-start.10 = (bf16[8,2,32,128]{3,2,1,0:T(8,128)(2,1)S(1)}, bf16[8,2,32,128]{3,2,1,0:T(8,128)(2,1)S(1)}, u32[]{:S(2)}, u32[]{:S(2)}) collective-permute-start(bf16[8,2,32,128]{3,2,1,0:T(8,128)(2,1)S(1)} %get-tuple-element.89), channel_id=1, source_target_pairs={{0,16},{8,24},{16,0},{24,8},{1,17},{9,25},{17,1},{25,9},{2,18},{10... | collective-permute-start | bytes 393224 | tf_op jit(solution)/shard_map/ppermute | solution.py:32
  40.1 0.3 collective-permute-start.11
  40.4 0.9 %last.6 = (bf16[8,2,16,128]{3,2,1,0:T(8,128)(2,1)S(1)}, bf16[8,2,16,128]{3,2,1,0:T(8,128)(2,1)S(1)}, bf16[8,2,16,128]{3,2,1,0:T(8,128)(2,1)S(1)}, bf16[8,2,16,128]{3,2,1,0:T(8,128)(2,1)S(1)}) custom-call(bf16[16,32,128]{2,1,0:T(8,128)(2,1)S(1)} %get-tuple-element.83._.own_in, bf16[16,32,128]{2,1,0:T(8,128)(2,1)S(1)} %collective-permute-done.12.came_in, ...), custom_call_target="tpu_custom_call" | custom-call | tf_op jit(solution)/shard_map/last/pallas_call | solution.py:358
  41.3 0.4 collective-permute-start.14
  41.7 2.6 %table.2._.refs_1_ = bf16[2,256,4224]{2,1,0:T(8,128)(2,1)S(1)} custom-call(s32[256]{0:T(256)S(1)} %copy-done.1, bf16[8,2,16,128]{3,2,1,0:T(8,128)(2,1)S(1)} %get-tuple-element.94.refs_0_.refs_4_), custom_call_target="tpu_custom_call" | custom-call | tf_op jit(solution)/shard_map/table/pallas_call | solution.py:201
  44.3 0.9 %collective-permute-done.17.came_in = bf16[16,32,128]{2,1,0:T(8,128)(2,1)S(1)} collective-permute-done((bf16[16,32,128]{2,1,0:T(8,128)(2,1)S(1)}, bf16[16,32,128]{2,1,0:T(8,128)(2,1)S(1)}, u32[]{:S(2)}, u32[]{:S(2)}) %collective-permute-start.17) | collective-permute-done | bytes 131104 | tf_op jit(solution)/shard_map/ppermute | solution.py:32
  45.2 1.5 %collective-permute-start.15 = (bf16[8,2,16,128]{3,2,1,0:T(8,128)(2,1)S(1)}, bf16[8,2,16,128]{3,2,1,0:T(8,128)(2,1)S(1)}, u32[]{:S(2)}, u32[]{:S(2)}) collective-permute-start(bf16[8,2,16,128]{3,2,1,0:T(8,128)(2,1)S(1)} %get-tuple-element.96), channel_id=1, source_target_pairs={{0,16},{8,24},{16,0},{24,8},{1,17},{9,25},{17,1},{25,9},{2,18},{10... | collective-permute-start | bytes 196616 | tf_op jit(solution)/shard_map/ppermute | solution.py:32
  46.7 0.9 %last.7 = (bf16[8,2,16,128]{3,2,1,0:T(8,128)(2,1)S(1)}, bf16[8,2,16,128]{3,2,1,0:T(8,128)(2,1)S(1)}, bf16[8,2,16,128]{3,2,1,0:T(8,128)(2,1)S(1)}, bf16[8,2,16,128]{3,2,1,0:T(8,128)(2,1)S(1)}) custom-call(bf16[16,32,128]{2,1,0:T(8,128)(2,1)S(1)} %get-tuple-element.93._.own_in, bf16[16,32,128]{2,1,0:T(8,128)(2,1)S(1)} %collective-permute-done.17.came_in, ...), custom_call_target="tpu_custom_call" | custom-call | tf_op jit(solution)/shard_map/last/pallas_call | solution.py:358
  47.6 0.1 collective-permute-start.16
  47.7 0.6 collective-permute-start.18
  48.3 1.5 %collective-permute-start.19 = (bf16[8,2,16,128]{3,2,1,0:T(8,128)(2,1)S(1)}, bf16[8,2,16,128]{3,2,1,0:T(8,128)(2,1)S(1)}, u32[]{:S(2)}, u32[]{:S(2)}) collective-permute-start(bf16[8,2,16,128]{3,2,1,0:T(8,128)(2,1)S(1)} %get-tuple-element.101), channel_id=1, source_target_pairs={{0,16},{8,24},{16,0},{24,8},{1,17},{9,25},{17,1},{25,9},{2,18},{10... | collective-permute-start | bytes 196616 | tf_op jit(solution)/shard_map/ppermute | solution.py:32
  49.8 2.4 %table.3.refs_12_ = bf16[2,256,4224]{2,1,0:T(8,128)(2,1)S(1)} custom-call(s32[256]{0:T(256)S(1)} %copy-done.1, bf16[8,2,16,128]{3,2,1,0:T(8,128)(2,1)S(1)} %get-tuple-element.99.refs_0_.refs_8_, bf16[2,256,4224]{2,1,0:T(8,128)(2,1)S(1)} %table.2._.refs_1_), custom_call_target="tpu_custom_call", output_to_operand_aliasing={{}: (2, {})} | custom-call | tf_op jit(solution)/shard_map/table/pallas_call | solution.py:201
  52.3 0.5 collective-permute-done.19.refs_10_
  52.8 1.4 %collective-permute-done.20.refs_11_ = bf16[8,2,16,128]{3,2,1,0:T(8,128)(2,1)S(1)} collective-permute-done((bf16[8,2,16,128]{3,2,1,0:T(8,128)(2,1)S(1)}, bf16[8,2,16,128]{3,2,1,0:T(8,128)(2,1)S(1)}, u32[]{:S(2)}, u32[]{:S(2)}) %collective-permute-start.20) | collective-permute-done | bytes 65568 | tf_op jit(solution)/shard_map/ppermute | solution.py:32
  54.2 8.6 %synthesis.1 = bf16[8,128,8192]{2,1,0:T(8,128)(2,1)} custom-call(bf16[8,2,32,128]{3,2,1,0:T(8,128)(2,1)S(1)} %get-tuple-element.87.refs_3_.refs_0_, bf16[8,2,32,128]{3,2,1,0:T(8,128)(2,1)S(1)} %collective-permute-done.9.refs_1_, bf16[8,2,32,128]{3,2,1,0:T(8,128)(2,1)S(1)} %collective-permute-done.10.refs_2_, ...), custom_call_target="tpu_custom_call" | custom-call | tf_op jit(solution)/shard_map/synthesis/pallas_call | solution.py:277
  (22 shorter events, 0.1 us)
Async XLA Ops:
  0.0 9.2 %slice-start = ((s8[6291456]{0:T(1024)(128)(4,1)}), s8[4194304]{0:T(1024)(128)(4,1)S(1)}, s32[]{:S(2)}) async-start(s8[6291456]{0:T(1024)(128)(4,1)} %bitcast.1), calls=%async_computation | async-start | bytes 8388608
  0.0 9.2 %slice-start.1 = ((s8[6291456]{0:T(1024)(128)(4,1)}), s8[2097152]{0:T(1024)(128)(4,1)S(1)}, s32[]{:S(2)}) async-start(s8[6291456]{0:T(1024)(128)(4,1)} %bitcast.1), calls=%async_computation.1 | async-start | bytes 4194304
  2.5 6.8 %collective-permute-start.1 = (bf16[16,32,128]{2,1,0:T(8,128)(2,1)S(1)}, bf16[16,32,128]{2,1,0:T(8,128)(2,1)S(1)}, u32[]{:S(2)}, u32[]{:S(2)}) collective-permute-start(bf16[16,32,128]{2,1,0:T(8,128)(2,1)S(1)} %get-tuple-element.63), channel_id=1, source_target_pairs={{0,1},{1,0},{2,3},{3,2},{4,5},{5,4},{6,7},{7,6},{8,9},{9,8},{10,11... | collective-permute-start | bytes 393224 | tf_op jit(solution)/shard_map/ppermute | solution.py:32
  7.3 8.1 %collective-permute-start = (bf16[16,32,128]{2,1,0:T(8,128)(2,1)S(1)}, bf16[16,32,128]{2,1,0:T(8,128)(2,1)S(1)}, u32[]{:S(2)}, u32[]{:S(2)}) collective-permute-start(bf16[16,32,128]{2,1,0:T(8,128)(2,1)S(1)} %get-tuple-element.59), channel_id=1, source_target_pairs={{0,1},{1,0},{2,3},{3,2},{4,5},{5,4},{6,7},{7,6},{8,9},{9,8},{10,11... | collective-permute-start | bytes 393224 | tf_op jit(solution)/shard_map/ppermute | solution.py:32
  9.6 6.9 %collective-permute-start.4 = (bf16[16,32,128]{2,1,0:T(8,128)(2,1)S(1)}, bf16[16,32,128]{2,1,0:T(8,128)(2,1)S(1)}, u32[]{:S(2)}, u32[]{:S(2)}) collective-permute-start(bf16[16,32,128]{2,1,0:T(8,128)(2,1)S(1)} %get-tuple-element.72), channel_id=1, source_target_pairs={{0,2},{1,3},{2,0},{3,1},{4,6},{5,7},{6,4},{7,5},{8,10},{9,11},{10,... | collective-permute-start | bytes 393224 | tf_op jit(solution)/shard_map/ppermute | solution.py:32
  13.1 7.8 %collective-permute-start.3 = (bf16[16,32,128]{2,1,0:T(8,128)(2,1)S(1)}, bf16[16,32,128]{2,1,0:T(8,128)(2,1)S(1)}, u32[]{:S(2)}, u32[]{:S(2)}) collective-permute-start(bf16[16,32,128]{2,1,0:T(8,128)(2,1)S(1)} %get-tuple-element.68), channel_id=1, source_target_pairs={{0,1},{1,0},{2,3},{3,2},{4,5},{5,4},{6,7},{7,6},{8,9},{9,8},{10,11... | collective-permute-start | bytes 393224 | tf_op jit(solution)/shard_map/ppermute | solution.py:32
  15.8 7.9 %collective-permute-start.2 = (bf16[16,32,128]{2,1,0:T(8,128)(2,1)S(1)}, bf16[16,32,128]{2,1,0:T(8,128)(2,1)S(1)}, u32[]{:S(2)}, u32[]{:S(2)}) collective-permute-start(bf16[16,32,128]{2,1,0:T(8,128)(2,1)S(1)} %get-tuple-element.67), channel_id=1, source_target_pairs={{0,2},{1,3},{2,0},{3,1},{4,6},{5,7},{6,4},{7,5},{8,10},{9,11},{10,... | collective-permute-start | bytes 393224 | tf_op jit(solution)/shard_map/ppermute | solution.py:32
  17.0 8.9 %collective-permute-start.8 = (bf16[16,32,128]{2,1,0:T(8,128)(2,1)S(1)}, bf16[16,32,128]{2,1,0:T(8,128)(2,1)S(1)}, u32[]{:S(2)}, u32[]{:S(2)}) collective-permute-start(bf16[16,32,128]{2,1,0:T(8,128)(2,1)S(1)} %get-tuple-element.80), channel_id=1, source_target_pairs={{0,4},{1,5},{2,6},{3,7},{4,0},{5,1},{6,2},{7,3},{8,12},{9,13},{10,... | collective-permute-start | bytes 393224 | tf_op jit(solution)/shard_map/ppermute | solution.py:32
  20.0 6.7 %collective-permute-start.7 = (bf16[16,32,128]{2,1,0:T(8,128)(2,1)S(1)}, bf16[16,32,128]{2,1,0:T(8,128)(2,1)S(1)}, u32[]{:S(2)}, u32[]{:S(2)}) collective-permute-start(bf16[16,32,128]{2,1,0:T(8,128)(2,1)S(1)} %get-tuple-element.79), channel_id=1, source_target_pairs={{0,1},{1,0},{2,3},{3,2},{4,5},{5,4},{6,7},{7,6},{8,9},{9,8},{10,11... | collective-permute-start | bytes 393224 | tf_op jit(solution)/shard_map/ppermute | solution.py:32
  21.3 4.5 %copy-start = (bf16[64,128,128]{2,1,0:T(8,128)(2,1)S(1)}, bf16[64,128,128]{2,1,0:T(8,128)(2,1)}, u32[]{:S(2)}) copy-start(bf16[64,128,128]{2,1,0:T(8,128)(2,1)} %lats.7) | copy-start | bytes 6291460
  21.3 8.3 %collective-permute-start.6 = (bf16[16,32,128]{2,1,0:T(8,128)(2,1)S(1)}, bf16[16,32,128]{2,1,0:T(8,128)(2,1)S(1)}, u32[]{:S(2)}, u32[]{:S(2)}) collective-permute-start(bf16[16,32,128]{2,1,0:T(8,128)(2,1)S(1)} %get-tuple-element.78), channel_id=1, source_target_pairs={{0,2},{1,3},{2,0},{3,1},{4,6},{5,7},{6,4},{7,5},{8,10},{9,11},{10,... | collective-permute-start | bytes 393224 | tf_op jit(solution)/shard_map/ppermute | solution.py:32
  24.1 13.0 %collective-permute-start.5 = (bf16[16,32,128]{2,1,0:T(8,128)(2,1)S(1)}, bf16[16,32,128]{2,1,0:T(8,128)(2,1)S(1)}, u32[]{:S(2)}, u32[]{:S(2)}) collective-permute-start(bf16[16,32,128]{2,1,0:T(8,128)(2,1)S(1)} %get-tuple-element.77), channel_id=1, source_target_pairs={{0,4},{1,5},{2,6},{3,7},{4,0},{5,1},{6,2},{7,3},{8,12},{9,13},{10,... | collective-permute-start | bytes 393224 | tf_op jit(solution)/shard_map/ppermute | solution.py:32
  27.1 10.8 %collective-permute-start.13 = (bf16[16,32,128]{2,1,0:T(8,128)(2,1)S(1)}, bf16[16,32,128]{2,1,0:T(8,128)(2,1)S(1)}, u32[]{:S(2)}, u32[]{:S(2)}) collective-permute-start(bf16[16,32,128]{2,1,0:T(8,128)(2,1)S(1)} %get-tuple-element.92), channel_id=1, source_target_pairs={{0,2},{1,3},{2,0},{3,1},{4,6},{5,7},{6,4},{7,5},{8,10},{9,11},{10,... | collective-permute-start | bytes 393224 | tf_op jit(solution)/shard_map/ppermute | solution.py:32
  30.1 10.3 %collective-permute-start.12 = (bf16[16,32,128]{2,1,0:T(8,128)(2,1)S(1)}, bf16[16,32,128]{2,1,0:T(8,128)(2,1)S(1)}, u32[]{:S(2)}, u32[]{:S(2)}) collective-permute-start(bf16[16,32,128]{2,1,0:T(8,128)(2,1)S(1)} %get-tuple-element.91), channel_id=1, source_target_pairs={{0,4},{1,5},{2,6},{3,7},{4,0},{5,1},{6,2},{7,3},{8,12},{9,13},{10,... | collective-permute-start | bytes 393224 | tf_op jit(solution)/shard_map/ppermute | solution.py:32
  38.4 6.8 %collective-permute-start.17 = (bf16[16,32,128]{2,1,0:T(8,128)(2,1)S(1)}, bf16[16,32,128]{2,1,0:T(8,128)(2,1)S(1)}, u32[]{:S(2)}, u32[]{:S(2)}) collective-permute-start(bf16[16,32,128]{2,1,0:T(8,128)(2,1)S(1)} %get-tuple-element.98), channel_id=1, source_target_pairs={{0,4},{1,5},{2,6},{3,7},{4,0},{5,1},{6,2},{7,3},{8,12},{9,13},{10,... | collective-permute-start | bytes 393224 | tf_op jit(solution)/shard_map/ppermute | solution.py:32
  38.5 9.1 %collective-permute-start.9 = (bf16[8,2,32,128]{3,2,1,0:T(8,128)(2,1)S(1)}, bf16[8,2,32,128]{3,2,1,0:T(8,128)(2,1)S(1)}, u32[]{:S(2)}, u32[]{:S(2)}) collective-permute-start(bf16[8,2,32,128]{3,2,1,0:T(8,128)(2,1)S(1)} %get-tuple-element.88), channel_id=1, source_target_pairs={{0,8},{8,0},{16,24},{24,16},{1,9},{9,1},{17,25},{25,17},{2,10},{10... | collective-permute-start | bytes 393224 | tf_op jit(solution)/shard_map/ppermute | solution.py:32
  38.5 9.1 %collective-permute-start.10 = (bf16[8,2,32,128]{3,2,1,0:T(8,128)(2,1)S(1)}, bf16[8,2,32,128]{3,2,1,0:T(8,128)(2,1)S(1)}, u32[]{:S(2)}, u32[]{:S(2)}) collective-permute-start(bf16[8,2,32,128]{3,2,1,0:T(8,128)(2,1)S(1)} %get-tuple-element.89), channel_id=1, source_target_pairs={{0,16},{8,24},{16,0},{24,8},{1,17},{9,25},{17,1},{25,9},{2,18},{10... | collective-permute-start | bytes 393224 | tf_op jit(solution)/shard_map/ppermute | solution.py:32
  40.1 8.2 %collective-permute-start.11 = (bf16[8,2,32,128]{3,2,1,0:T(8,128)(2,1)S(1)}, bf16[8,2,32,128]{3,2,1,0:T(8,128)(2,1)S(1)}, u32[]{:S(2)}, u32[]{:S(2)}) collective-permute-start(bf16[8,2,32,128]{3,2,1,0:T(8,128)(2,1)S(1)} %get-tuple-element.90), channel_id=1, source_target_pairs={{0,24},{8,16},{16,8},{24,0},{1,25},{9,17},{17,9},{25,1},{2,26},{10... | collective-permute-start | bytes 393224 | tf_op jit(solution)/shard_map/ppermute | solution.py:32
  40.4 1.3 %copy-start.1 = (s32[256]{0:T(256)S(1)}, s32[256]{0:T(256)}, u32[]{:S(2)}) copy-start(s32[256]{0:T(256)} %map_ref.3) | copy-start | bytes 3076
  41.3 8.5 %collective-permute-start.14 = (bf16[8,2,16,128]{3,2,1,0:T(8,128)(2,1)S(1)}, bf16[8,2,16,128]{3,2,1,0:T(8,128)(2,1)S(1)}, u32[]{:S(2)}, u32[]{:S(2)}) collective-permute-start(bf16[8,2,16,128]{3,2,1,0:T(8,128)(2,1)S(1)} %get-tuple-element.95), channel_id=1, source_target_pairs={{0,8},{8,0},{16,24},{24,16},{1,9},{9,1},{17,25},{25,17},{2,10},{10... | collective-permute-start | bytes 196616 | tf_op jit(solution)/shard_map/ppermute | solution.py:32
  45.2 7.0 %collective-permute-start.15 = (bf16[8,2,16,128]{3,2,1,0:T(8,128)(2,1)S(1)}, bf16[8,2,16,128]{3,2,1,0:T(8,128)(2,1)S(1)}, u32[]{:S(2)}, u32[]{:S(2)}) collective-permute-start(bf16[8,2,16,128]{3,2,1,0:T(8,128)(2,1)S(1)} %get-tuple-element.96), channel_id=1, source_target_pairs={{0,16},{8,24},{16,0},{24,8},{1,17},{9,25},{17,1},{25,9},{2,18},{10... | collective-permute-start | bytes 196616 | tf_op jit(solution)/shard_map/ppermute | solution.py:32
  47.6 4.7 %collective-permute-start.16 = (bf16[8,2,16,128]{3,2,1,0:T(8,128)(2,1)S(1)}, bf16[8,2,16,128]{3,2,1,0:T(8,128)(2,1)S(1)}, u32[]{:S(2)}, u32[]{:S(2)}) collective-permute-start(bf16[8,2,16,128]{3,2,1,0:T(8,128)(2,1)S(1)} %get-tuple-element.97), channel_id=1, source_target_pairs={{0,24},{8,16},{16,8},{24,0},{1,25},{9,17},{17,9},{25,1},{2,26},{10... | collective-permute-start | bytes 196616 | tf_op jit(solution)/shard_map/ppermute | solution.py:32
  47.7 4.6 %collective-permute-start.18 = (bf16[8,2,16,128]{3,2,1,0:T(8,128)(2,1)S(1)}, bf16[8,2,16,128]{3,2,1,0:T(8,128)(2,1)S(1)}, u32[]{:S(2)}, u32[]{:S(2)}) collective-permute-start(bf16[8,2,16,128]{3,2,1,0:T(8,128)(2,1)S(1)} %get-tuple-element.100), channel_id=1, source_target_pairs={{0,8},{8,0},{16,24},{24,16},{1,9},{9,1},{17,25},{25,17},{2,10},{10... | collective-permute-start | bytes 196616 | tf_op jit(solution)/shard_map/ppermute | solution.py:32
  48.3 4.4 %collective-permute-start.19 = (bf16[8,2,16,128]{3,2,1,0:T(8,128)(2,1)S(1)}, bf16[8,2,16,128]{3,2,1,0:T(8,128)(2,1)S(1)}, u32[]{:S(2)}, u32[]{:S(2)}) collective-permute-start(bf16[8,2,16,128]{3,2,1,0:T(8,128)(2,1)S(1)} %get-tuple-element.101), channel_id=1, source_target_pairs={{0,16},{8,24},{16,0},{24,8},{1,17},{9,25},{17,1},{25,9},{2,18},{10... | collective-permute-start | bytes 196616 | tf_op jit(solution)/shard_map/ppermute | solution.py:32
  49.8 4.4 %collective-permute-start.20 = (bf16[8,2,16,128]{3,2,1,0:T(8,128)(2,1)S(1)}, bf16[8,2,16,128]{3,2,1,0:T(8,128)(2,1)S(1)}, u32[]{:S(2)}, u32[]{:S(2)}) collective-permute-start(bf16[8,2,16,128]{3,2,1,0:T(8,128)(2,1)S(1)} %get-tuple-element.102), channel_id=1, source_target_pairs={{0,24},{8,16},{16,8},{24,0},{1,25},{9,17},{17,9},{25,1},{2,26},{10... | collective-permute-start | bytes 196616 | tf_op jit(solution)/shard_map/ppermute | solution.py:32
